TPU v7x, 32 devices: a whole 2x2x4 slice. The times are simulated.
32 devices in a mesh: rep: 16 (over z, y, x), mp: 2 (over core).
Axes of the slice: x: 2, y: 2, z: 4, core: 2. Of those that a mesh axis runs over, the one named last changes fastest.
Arguments:
- tokens_in: bfloat16 [4096, 8192], P('rep', 'mp'), may hold values from -2100 to 2100
- norm_gain: bfloat16 [8192], P('mp'), may hold values from 0.5 to 1.5
- key_grad: bfloat16 [4096, 512], P('rep'), may hold values from -1 to 1
- error_in: float32 [16, 8192, 512], P('rep', 'mp'), may hold values from -6 to 6
- basis_init: float32 [512, 128], P('mp'), may hold values from -6 to 6
- weights_in: float32 [2, 4096, 512], P('mp', 'rep'), may hold values from -0.75 to 0.75
- momentum_in: float32 [2, 4096, 512], P('mp', 'rep'), may hold values from -1.5 to 1.5
Outputs:
- error_out: float32 [16, 8192, 512], P('rep', 'mp')
- weights_out: float32 [2, 4096, 512], P('mp', 'rep')
- momentum_out: float32 [2, 4096, 512], P('mp', 'rep')
All inputs are finite; a program needn't handle non-finite values.
Results may differ from a plain program's by a relative error of at most 0.0025.
Values sent between devices are 32-bit elements; how exact they have to be, the bound alone decides.
No kernel may reach another device: no remote copies, remote signals or barrier semaphores. Data moves between devices by JAX's collectives and lax.ppermute only.
A program may use at most 64 MiB of HBM per device.

v0:
```python
import jax
import jax.numpy as jnp
from jax import lax
from jax.sharding import PartitionSpec as P

D = 8192
ITERS = 2


precise = lax.Precision.HIGHEST
epsilon = 1e-05
momentum_rate = 0.9
outer_rate = 0.7


def product(first, second):
    return jnp.dot(first, second, precision=precise, preferred_element_type=jnp.float32)


def inner_product(first, second):
    return lax.dot_general(
        first,
        second,
        (((0,), (0,)), ((), ())),
        precision=precise,
        preferred_element_type=jnp.float32,
    )


def outer_product(first, second):
    return lax.dot_general(
        first,
        second,
        (((1,), (1,)), ((), ())),
        precision=precise,
        preferred_element_type=jnp.float32,
    )


def right_solve(lower_factor, row_block):
    return jax.scipy.linalg.solve_triangular(lower_factor, row_block.T, lower=True).T


def on_device(tokens_in, norm_gain, key_grad, error_in, basis_init, weights_in, momentum_in):
    replicas = lax.axis_size("rep")
    widened = tokens_in.astype(jnp.float32)
    square_sums = lax.psum(jnp.sum(widened * widened, axis=1), "mp")
    mean_square = square_sums / D
    right_factor = lax.all_gather(basis_init, "mp", axis=0, tiled=True)
    normed = (
        widened * lax.rsqrt(mean_square + epsilon)[:, None] * norm_gain.astype(jnp.float32)[None, :]
    ).astype(jnp.bfloat16)
    weight_change = lax.dot_general(
        normed, key_grad, (((0,), (0,)), ((), ())), preferred_element_type=jnp.float32
    )
    merged = weight_change + error_in[0]
    orthonormal = jnp.zeros((merged.shape[0], basis_init.shape[1]), jnp.float32)
    combined = lax.psum(merged, "rep") / replicas
    for iteration in range(ITERS):
        left_factor = product(combined, right_factor)
        gram_matrix = lax.psum(inner_product(left_factor, left_factor), "mp")
        lower_factor = jnp.linalg.cholesky(gram_matrix)
        orthonormal = right_solve(lower_factor, left_factor)
        right_factor = lax.psum(inner_product(combined, orthonormal), "mp")
    approximant = outer_product(orthonormal, right_factor)
    error_out = (merged - approximant)[None]
    rows_each = weights_in.shape[1]
    start_row = lax.axis_index("rep") * rows_each
    own_rows = lax.dynamic_slice_in_dim(approximant, start_row, rows_each, 0)[None]
    momentum_out = momentum_rate * momentum_in + own_rows
    weights_out = weights_in - outer_rate * (own_rows + momentum_rate * momentum_out)
    return (error_out, weights_out, momentum_out)


def solution(mesh):
    in_specs = (
        P("rep", "mp"),
        P("mp"),
        P("rep", None),
        P("rep", "mp", None),
        P("mp", None),
        P("mp", "rep", None),
        P("mp", "rep", None),
    )
    out_specs = (P("rep", "mp", None), P("mp", "rep", None), P("mp", "rep", None))
    return jax.shard_map(
        on_device, mesh=mesh, in_specs=in_specs, out_specs=out_specs, check_vma=False
    )
```

profile of v0, /device:TPU:0, one launch (start us, length us, event | category | flops | bytes accessed | tf_op | source)
XLA Modules:
  0.0 500.7 jit_solution(406407873820874006)
XLA Ops:
  8.1 2.1 fusion.8
  10.2 2.6 psum.42
  12.8 8.4 %bitcast_add_fusion = f32[4096,512]{1,0:T(8,128)} fusion(f32[1,4096,512]{2,1,0:T(8,128)} %param.13, bf16[256,512]{1,0:T(8,128)(2,1)S(1)} %copy-done, bf16[256,4096]{1,0:T(8,128)(2,1)S(1)} %copy-done.2, f32[4096]{0:T(1024)S(1)} %convert_element_type.10, f32[256]{0:T(256)S(1)} %add_rsqrt_fusion), kind=kOutput, calls=%fused_computation | convolution fusion | flops 1080033280 | bytes 19153920 | tf_op jit(solution)/shard_map/dot_general | solution.py:53
  22.0 2.0 all_gather.3
  24.0 256.2 %all-reduce.6.cloned.1.call-done = f32[4096,512]{1,0:T(8,128)} async-done(((f32[4096,512]{1,0:T(8,128)}), f32[4096,512]{1,0:T(8,128)}) %all-reduce.6.cloned.1.call-update) | async-done | bytes 8388624 | tf_op jit(solution)/shard_map/psum | solution.py:58
  280.2 9.1 %fusion.6 = f32[4096,128]{1,0:T(8,128)S(1)} fusion(f32[512,128]{1,0:T(8,128)S(1)} %all_gather.3, f32[4096,512]{1,0:T(8,128)} %all-reduce.6.cloned.1.call-done), kind=kOutput, calls=%fused_computation.8 | convolution fusion | flops 3223322624 | bytes 10747904 | tf_op jit(solution)/shard_map/dot_general | solution.py:17
  289.3 4.1 fusion.36
  294.0 16.2 %all-reduce.8.cloned.1.call-done = f32[128,128]{0,1:T(8,128)} async-done(((f32[128,128]{0,1:T(8,128)}), f32[128,128]{0,1:T(8,128)}) %all-reduce.8.cloned.1.call-update) | async-done | bytes 65552 | tf_op jit(solution)/shard_map/psum | solution.py:61
  312.0 11.7 %cholesky.44 = f32[128,128]{1,0:T(8,128)S(1)} custom-call(f32[128,128]{1,0:T(8,128)S(1)} %fusion.29), custom_call_target="Cholesky" | custom-call | tf_op jit(solution)/shard_map/jit(cholesky)/cholesky | solution.py:62
  325.1 9.8 %custom-call.6 = f32[1,128,128]{1,2,0:T(8,128)S(1)} custom-call(f32[1,128,128]{2,1,0:T(8,128)S(1)} %fusion.24), custom_call_target="InvertDiagBlocksLowerTriangular" | custom-call | tf_op jit(solution)/shard_map/jit(_solve_triangular)/triangular_solve | solution.py:41
  334.9 1.9 fusion.18
  336.9 16.4 %fusion.4 = f32[512,128]{1,0:T(8,128)} fusion(f32[128,4096]{1,0:T(8,128)S(1)} %fusion.18, f32[4096,512]{1,0:T(8,128)} %all-reduce.6.cloned.1.call-done), kind=kOutput, calls=%fused_computation.6 | convolution fusion | flops 3223322624 | bytes 10747904 | tf_op jit(solution)/shard_map/dot_general | solution.py:21
  353.4 19.5 %all-reduce.10.cloned.1.call-done = f32[512,128]{1,0:T(8,128)} async-done(((f32[512,128]{1,0:T(8,128)}), f32[512,128]{1,0:T(8,128)}) %all-reduce.10.cloned.1.call-update) | async-done | bytes 262160 | tf_op jit(solution)/shard_map/psum | solution.py:64
  372.9 9.3 %fusion.2 = f32[4096,128]{1,0:T(8,128)S(1)} fusion(f32[512,128]{1,0:T(8,128)} %all-reduce.10.cloned.1.call-done, f32[4096,512]{1,0:T(8,128)} %all-reduce.6.cloned.1.call-done), kind=kOutput, calls=%fused_computation.4 | convolution fusion | flops 3223322624 | bytes 10747904 | tf_op jit(solution)/shard_map/dot_general | solution.py:17
  382.2 4.1 fusion.37
  386.6 18.7 %all-reduce.12.cloned.1.call-done = f32[128,128]{0,1:T(8,128)} async-done(((f32[128,128]{0,1:T(8,128)}), f32[128,128]{0,1:T(8,128)}) %all-reduce.12.cloned.1.call-update) | async-done | bytes 65552 | tf_op jit(solution)/shard_map/psum | solution.py:61
  407.1 11.7 %cholesky.55 = f32[128,128]{1,0:T(8,128)S(1)} custom-call(f32[128,128]{1,0:T(8,128)S(1)} %fusion.27), custom_call_target="Cholesky" | custom-call | tf_op jit(solution)/shard_map/jit(cholesky)/cholesky | solution.py:62
  420.2 9.8 %custom-call.7 = f32[1,128,128]{1,2,0:T(8,128)S(1)} custom-call(f32[1,128,128]{2,1,0:T(8,128)S(1)} %fusion.25), custom_call_target="InvertDiagBlocksLowerTriangular" | custom-call | tf_op jit(solution)/shard_map/jit(_solve_triangular)/triangular_solve | solution.py:41
  430.0 1.9 fusion.16
  433.4 16.5 %fusion = f32[512,128]{1,0:T(8,128)} fusion(f32[128,4096]{1,0:T(8,128)S(1)} %fusion.16, f32[4096,512]{1,0:T(8,128)} %all-reduce.6.cloned.1.call-done), kind=kOutput, calls=%fused_computation.2 | convolution fusion | flops 3223322624 | bytes 10747904 | tf_op jit(solution)/shard_map/dot_general | solution.py:21
  449.9 19.6 %all-reduce.14.cloned.1.call-done = f32[512,128]{1,0:T(8,128)} async-done(((f32[512,128]{1,0:T(8,128)}), f32[512,128]{1,0:T(8,128)}) %all-reduce.14.cloned.1.call-update) | async-done | bytes 262160 | tf_op jit(solution)/shard_map/psum | solution.py:64
  469.5 10.5 %fusion.38 = f32[4096,512]{1,0:T(8,128)} fusion(f32[128,4096]{1,0:T(8,128)} %copy-done.1, f32[512,128]{1,0:T(8,128)} %all-reduce.14.cloned.1.call-done), kind=kOutput, calls=%fused_computation.53 | convolution fusion | flops 3221225472 | bytes 10747904 | tf_op jit(solution)/shard_map/dot_general | solution.py:31
  480.0 11.3 %subtract_bitcast_fusion = f32[1,4096,512]{2,1,0:T(8,128)} fusion(f32[4096,512]{1,0:T(8,128)} %bitcast_add_fusion, f32[4096,512]{1,0:T(8,128)} %fusion.38), kind=kLoop, calls=%fused_computation.1 | loop fusion | flops 2097152 | bytes 25165824 | tf_op jit(solution)/shard_map/broadcast_in_dim | solution.py:66
  491.4 2.2 fusion.23
  (34 shorter events, 10.4 us)
Async XLA Ops:
  7.2 5.6 %copy-start = (bf16[256,512]{1,0:T(8,128)(2,1)S(1)}, bf16[256,512]{1,0:T(8,128)(2,1)}, u32[]{:S(2)}) copy-start(bf16[256,512]{1,0:T(8,128)(2,1)} %param.12) | copy-start | bytes 786436
  7.2 5.6 %copy-start.2 = (bf16[256,4096]{1,0:T(8,128)(2,1)S(1)}, bf16[256,4096]{1,0:T(8,128)(2,1)}, u32[]{:S(2)}) copy-start(bf16[256,4096]{1,0:T(8,128)(2,1)} %param.10) | copy-start | bytes 6291460
  7.2 273.0 %all-reduce.6.cloned.1.call-start = ((), (), s32[]{:S(2)}) async-start(), calls=%async_computation | async-start | bytes 16777216 | tf_op jit(solution)/shard_map/psum | solution.py:58
  21.1 0.9 copy-start.5
  21.2 289.1 %all-reduce.8.cloned.1.call-start = ((), (), s32[]{:S(2)}) async-start(), calls=%async_computation.1 | async-start | bytes 131072 | tf_op jit(solution)/shard_map/psum | solution.py:61
  293.4 79.5 %all-reduce.10.cloned.1.call-start = ((), (), s32[]{:S(2)}) async-start(), calls=%async_computation.2 | async-start | bytes 524288 | tf_op jit(solution)/shard_map/psum | solution.py:64
  353.3 52.1 %all-reduce.12.cloned.1.call-start = ((), (), s32[]{:S(2)}) async-start(), calls=%async_computation.3 | async-start | bytes 131072 | tf_op jit(solution)/shard_map/psum | solution.py:61
  386.3 83.2 %all-reduce.14.cloned.1.call-start = ((), (), s32[]{:S(2)}) async-start(), calls=%async_computation.4 | async-start | bytes 524288 | tf_op jit(solution)/shard_map/psum | solution.py:64
  432.0 1.4 copy-start.1
  480.0 11.4 %copy-start.3 = (f32[1,256,512]{2,1,0:T(8,128)S(1)}, f32[1,256,512]{2,1,0:T(8,128)}, u32[]{:S(2)}) copy-start(f32[1,256,512]{2,1,0:T(8,128)} %param.15) | copy-start | bytes 1572868
  480.0 11.4 %copy-start.4 = (f32[1,256,512]{2,1,0:T(8,128)S(1)}, f32[1,256,512]{2,1,0:T(8,128)}, u32[]{:S(2)}) copy-start(f32[1,256,512]{2,1,0:T(8,128)} %param.16) | copy-start | bytes 1572868
Sparse Core Ops, SparseCore 0:
  21.3 258.8 all-reduce.5
  293.6 16.6 all-reduce.7
  353.4 19.4 all-reduce.9
  386.5 18.8 all-reduce.11
  450.0 19.4 all-reduce.13
where the time goes:
time: 508 us; the launch traced here: 501 us
  waiting for transfers between devices  330 us (65%)
  matrix products  82.3 us (16%)
  other arithmetic  63.9 us (13%)
  between operations  14.5 us (3%)
    psum x1, waiting for transfers between devices, on_device(): combined = lax.psum(merged, 'rep') / replicas  256 us
    dot_general x4, matrix products, inner_product(): lax.dot_general(first, second, (((0,), (0,)), ((), ())), precision=precis...  41.1 us
    psum x2, waiting for transfers between devices, on_device(): right_factor = lax.psum(inner_product(combined, orthonormal), 'mp')  39.1 us
    psum x2, waiting for transfers between devices, on_device(): gram_matrix = lax.psum(inner_product(left_factor, left_factor), 'mp')  35 us
    another operation x6, other arithmetic, on_device(): lower_factor = jnp.linalg.cholesky(gram_matrix)  24.8 us
    another operation x4, other arithmetic, right_solve(): jax.scipy.linalg.solve_triangular(lower_factor, row_block.T, lower=True)  20.9 us
    dot_general x2, matrix products, product(): jnp.dot(first, second, precision=precise, preferred_element_type=jnp.floa...  18.4 us
    broadcast_in_dim x1, other arithmetic, on_device(): error_out = (merged - approximant)[None]  11.3 us
  transfers between devices with their start and end apart: 5, of which 5 were waited for; matrix products, arithmetic and copies ran while one was open for 0% of the time, Pallas kernels for 0%

commit v1 on v0

v1 whole, which is shorter than its diff:
```python
import functools

import jax
import jax.numpy as jnp
from jax import lax
from jax.experimental import pallas as pl
from jax.experimental.pallas import tpu as pltpu
from jax.sharding import PartitionSpec as P

BLOCK = 128

precise = lax.Precision.HIGHEST
epsilon = 1e-05
momentum_rate = 0.9
outer_rate = 0.7


def contract(first, second, dims, precision=precise):
    return lax.dot_general(
        first,
        second,
        ((dims[:1], dims[1:]), ((), ())),
        precision=precision,
        preferred_element_type=jnp.float32,
    )


def flip(value, axis, mask):
    size = lax.axis_size(axis)
    return lax.ppermute(value, axis, [(i, i ^ mask) for i in range(size)])


def bit_of(axis, bit):
    return (lax.axis_index(axis) >> bit) & 1


def rows_of(value, start, count):
    return lax.dynamic_slice_in_dim(value, start, count, 0)


def halve(value, axis, bit):
    half = value.shape[0] // 2
    side = bit_of(axis, bit)
    sent = rows_of(value, (1 - side) * half, half)
    return rows_of(value, side * half, half) + flip(sent, axis, 1 << bit)


def double(value, axis, bit):
    other = flip(value, axis, 1 << bit)
    side = bit_of(axis, bit)
    both = jnp.concatenate([value, value], 0)
    return lax.dynamic_update_slice_in_dim(both, other, (1 - side) * value.shape[0], 0)


def bit_count(size):
    return size.bit_length() - 1


def sum_over(value, axis):
    for bit in range(bit_count(lax.axis_size(axis))):
        value = value + flip(value, axis, 1 << bit)
    return value


def sum_everywhere(value):
    rep_bits = bit_count(lax.axis_size("rep"))
    mp_bits = bit_count(lax.axis_size("mp"))
    for bit in range(mp_bits):
        value = halve(value, "mp", bit)
    place = lax.axis_index("rep") & 3
    part = value.shape[0] // 4
    pieces = [rows_of(value, (place ^ m) * part, part) for m in range(4)]
    got = [flip(pieces[m], "rep", m) for m in (1, 2, 3)]
    value = (pieces[0] + got[0]) + (got[1] + got[2])
    bit = 2
    while bit < rep_bits:
        if bit + 1 < rep_bits:
            got = [flip(value, "rep", m << bit) for m in (1, 2, 3)]
            value = (value + got[0]) + (got[1] + got[2])
            bit += 2
        else:
            value = value + flip(value, "rep", 1 << bit)
            bit += 1
    got = [value] + [flip(value, "rep", m) for m in (1, 2, 3)]
    whole = jnp.zeros((4 * part,) + value.shape[1:], value.dtype)
    for m in range(4):
        whole = lax.dynamic_update_slice_in_dim(whole, got[m], (place ^ m) * part, 0)
    for bit in reversed(range(mp_bits)):
        whole = double(whole, "mp", bit)
    return whole


LIGHT = pl.CostEstimate(flops=1, bytes_accessed=1, transcendentals=0)


def kernel_call(*args, **options):
    return pl.pallas_call(
        *args, compiler_params=pltpu.CompilerParams(vmem_limit_bytes=16 * 2**20), **options
    )


def near(*arrays):
    return [pltpu.with_memory_space_constraint(array, pltpu.VMEM) for array in arrays]


def distant(array):
    return pltpu.with_memory_space_constraint(array, pltpu.HBM)


def near_shape(shape, dtype=jnp.float32):
    return pltpu.VMEM(shape, dtype)


def specs(*places):
    return [pl.BlockSpec(memory_space=place) for place in places]


def pieces_of(count, most):
    cuts, place = [], 0
    while place < count:
        size = min(most, count - place)
        cuts.append((place, size))
        place += size
    return cuts


def split(value):
    high = value.astype(jnp.bfloat16)
    return high, (value - high.astype(jnp.float32)).astype(jnp.bfloat16)


def squares_kernel(cuts, tokens_ref, out_ref, held_ref, sems):
    copies = []
    for index, (start, size) in enumerate(cuts):
        at = pl.ds(start, size)
        copies.append(
            pltpu.make_async_copy(tokens_ref.at[:, at], held_ref.at[:, at], sems.at[index])
        )
        copies[-1].start()
    total = None
    for copy, (start, size) in zip(copies, cuts):
        copy.wait()
        for place in range(start, start + size, BLOCK):
            wide = held_ref[:, place : place + BLOCK].astype(jnp.float32)
            total = wide * wide if total is None else total + wide * wide
    out_ref[...] = jnp.broadcast_to(jnp.sum(total, axis=1, keepdims=True), out_ref.shape)


def squares(tokens):
    cuts = pieces_of(tokens.shape[1], max(BLOCK, tokens.shape[1] // 4))
    return kernel_call(
        functools.partial(squares_kernel, cuts),
        out_shape=near_shape((tokens.shape[0], BLOCK)),
        in_specs=specs(pltpu.HBM),
        out_specs=specs(pltpu.VMEM)[0],
        scratch_shapes=[
            pltpu.VMEM(tokens.shape, tokens.dtype),
            pltpu.SemaphoreType.DMA((len(cuts),)),
        ],
    )(distant(tokens))


def merge_kernel(
    cuts, depth, start_ref, tokens_ref, squares_ref, gain_ref, grad_ref, error_ref, out_ref, held_ref, sems
):
    copies = []
    for index, (place, size) in enumerate(cuts):
        there = pl.ds(pl.multiple_of(start_ref[0] + place, BLOCK), size)
        here = pl.ds(place, size)
        pair = [
            pltpu.make_async_copy(tokens_ref.at[:, there], held_ref.at[:, here], sems.at[index, 0]),
            pltpu.make_async_copy(error_ref.at[there, :], out_ref.at[here, :], sems.at[index, 1]),
        ]
        for copy in pair:
            copy.start()
        copies.append(pair)
    scale = lax.rsqrt(squares_ref[...] / depth + epsilon)[:, :1]
    for pair, (place, size) in zip(copies, cuts):
        here = pl.ds(place, size)
        there = pl.ds(pl.multiple_of(start_ref[0] + place, BLOCK), size)
        gain = gain_ref[:, there].astype(jnp.float32)
        pair[0].wait()
        normed = (held_ref[:, here].astype(jnp.float32) * scale * gain).astype(jnp.bfloat16)
        change = lax.dot_general(
            normed, grad_ref[...], (((0,), (0,)), ((), ())), preferred_element_type=jnp.float32
        )
        pair[1].wait()
        out_ref[here, :] = change + out_ref[here, :]


def merge(start, count, depth, tokens, square_sums, gain, grad, error):
    cuts = pieces_of(count, 3 * BLOCK)
    return kernel_call(
        functools.partial(merge_kernel, cuts, depth),
        out_shape=near_shape((count, grad.shape[1])),
        in_specs=specs(pltpu.SMEM, pltpu.HBM, pltpu.VMEM, pltpu.VMEM, pltpu.VMEM, pltpu.HBM),
        out_specs=specs(pltpu.VMEM)[0],
        scratch_shapes=[
            pltpu.VMEM((tokens.shape[0], count), tokens.dtype),
            pltpu.SemaphoreType.DMA((len(cuts), 2)),
        ],
        cost_estimate=pl.CostEstimate(
            flops=2 * count * grad.shape[1] * tokens.shape[0],
            bytes_accessed=8 * count * grad.shape[1] + 2 * tokens.shape[0] * count,
            transcendentals=0,
        ),
    )(
        jnp.reshape(start, (1,)).astype(jnp.int32),
        distant(tokens),
        *near(square_sums, gain, grad),
        distant(error),
    )


def sides_of(side, half):
    return pl.ds(pl.multiple_of(side * half, 8), half), pl.ds(pl.multiple_of((1 - side) * half, 8), half)


def join_kernel(count, side_ref, own_ref, got_ref, *refs):
    keep_ref, send_ref = refs[-2:]
    stays, goes = sides_of(side_ref[0], count // 2)
    send_ref[...] = own_ref[goes, :] + got_ref[goes, :]
    keep_ref[...] = own_ref[stays, :] + got_ref[stays, :]


def last_kernel(own_ref, got_ref, *refs):
    refs[-1][...] = own_ref[...] + got_ref[...]


def join(own, got, side, after):
    count, width = own.shape
    arrays, places = near(own, got), [pltpu.VMEM] * 2
    if side is None:
        kernel, shapes = last_kernel, (near_shape((count, width)),)
    else:
        kernel = functools.partial(join_kernel, count)
        shapes = (near_shape((count // 2, width)),) * 2
        arrays.insert(0, jnp.reshape(side, (1,)).astype(jnp.int32))
        places.insert(0, pltpu.SMEM)
    return kernel_call(
        kernel,
        out_shape=shapes,
        in_specs=specs(*places, *[pl.ANY] * len(after)),
        out_specs=tuple(specs(*[pltpu.VMEM] * len(shapes))),
        cost_estimate=LIGHT,
    )(*arrays, *after)


def stack_kernel(count, side_ref, own_ref, got_ref, out_ref):
    stays, goes = sides_of(side_ref[0], count)
    out_ref[stays, :] = own_ref[...]
    out_ref[goes, :] = got_ref[...]


def stack(own, got, side):
    count, width = own.shape
    return kernel_call(
        functools.partial(stack_kernel, count),
        out_shape=near_shape((2 * count, width)),
        in_specs=specs(pltpu.SMEM, pltpu.VMEM, pltpu.VMEM),
        out_specs=specs(pltpu.VMEM)[0],
        cost_estimate=LIGHT,
    )(jnp.reshape(side, (1,)).astype(jnp.int32), *near(own, got))


def gram_kernel(replicas, *refs):
    out_ref = refs[-1]
    rows = jnp.concatenate([ref[...] for ref in refs[:-1]], 0) / replicas
    blocks = rows.shape[1] // BLOCK
    place = 0
    for a in range(blocks):
        left = rows[:, a * BLOCK : (a + 1) * BLOCK]
        band = contract(left, rows[:, a * BLOCK :], (0, 0))
        for b in range(blocks - a):
            out_ref[place * BLOCK : (place + 1) * BLOCK, :] = band[:, b * BLOCK : (b + 1) * BLOCK]
            place += 1


def gram(parts, replicas):
    blocks = parts[0].shape[1] // BLOCK
    return kernel_call(
        functools.partial(gram_kernel, replicas),
        out_shape=near_shape((blocks * (blocks + 1) // 2 * BLOCK, BLOCK)),
        in_specs=specs(*[pltpu.VMEM] * len(parts)),
        out_specs=specs(pltpu.VMEM)[0],
    )(*near(*parts))


def factor(matrix):
    size = matrix.shape[0]
    group = 8
    lane = lax.broadcasted_iota(jnp.int32, (size, size), 1)
    row = lax.broadcasted_iota(jnp.int32, (size, size), 0)
    done = []
    live = matrix
    for start in range(0, size, group):
        if start:
            done.append(live[:group])
            live = live[group:]
        count = size - start
        lanes, rows = lane[start:], row[start:]
        columns = [
            jnp.broadcast_to(live[:, start + t : start + t + 1], (count, size)) for t in range(group)
        ]
        for t in range(group):
            pivot = start + t
            inverse = 1.0 / columns[t][t : t + 1, :]
            below = rows > pivot
            scale = jnp.where(below, columns[t] * inverse, 0.0)
            own = jnp.where(lanes[t : t + 1] == pivot, 1.0, live[t : t + 1, :])
            live = jnp.where(below & (lanes == pivot), 0.0, live) - scale * own
            for s in range(t + 1, group):
                columns[s] = columns[s] - scale * columns[s][t : t + 1, :]
    done.append(live)
    result = jnp.concatenate(done, 0)
    diagonal = jnp.sum(jnp.where(lane == row, result, 0.0), axis=1, keepdims=True)
    unit = jnp.where(lane < row, result, jnp.where(lane == row, 1.0, 0.0))
    return unit, diagonal


def first_kernel(replicas, packed_ref, basis_ref, *refs):
    whole_ref, right_ref, left_ref = refs[-3:]
    blocks = basis_ref.shape[0] // BLOCK
    place = 0
    for a in range(blocks):
        for b in range(a, blocks):
            tile = packed_ref[place * BLOCK : (place + 1) * BLOCK, :]
            whole_ref[a * BLOCK : (a + 1) * BLOCK, b * BLOCK : (b + 1) * BLOCK] = tile
            if b > a:
                whole_ref[b * BLOCK : (b + 1) * BLOCK, a * BLOCK : (a + 1) * BLOCK] = tile.T
            place += 1
    basis = basis_ref[...]
    plain = contract(whole_ref[...], basis, (1, 0))
    unit, diagonal = factor(contract(basis, plain, (0, 0)))
    right = contract(plain, unit * lax.rsqrt(diagonal), (1, 1))
    right_ref[...] = right
    rows = jnp.concatenate([ref[...] for ref in refs[:-3]], 0) / replicas
    left_ref[...] = contract(rows, right, (1, 0))


def first_pass(packed, basis, parts, replicas):
    width, rank = basis.shape
    return kernel_call(
        functools.partial(first_kernel, replicas),
        out_shape=(
            near_shape((width, width)),
            near_shape((width, rank)),
            near_shape((sum(part.shape[0] for part in parts), rank)),
        ),
        in_specs=specs(*[pltpu.VMEM] * (2 + len(parts))),
        out_specs=tuple(specs(*[pltpu.VMEM] * 3)),
    )(*near(packed, basis, *parts))


def product_kernel(whole_ref, right_ref, plain_ref, gram_ref):
    right = right_ref[...]
    plain = contract(whole_ref[...], right, (1, 0))
    plain_ref[...] = plain
    gram_ref[...] = contract(right, plain, (0, 0))


def weight_kernel(plain_ref, gram_ref, high_ref, low_ref):
    unit, diagonal = factor(gram_ref[...])
    inverse = unit * lax.rsqrt(diagonal)
    turned = contract(inverse, plain_ref[...], (1, 1))
    high_ref[...], low_ref[...] = split(contract(inverse, turned, (0, 0)))


def second_pass(whole, right):
    width, rank = right.shape
    pair = functools.partial(
        kernel_call,
        in_specs=specs(pltpu.VMEM, pltpu.VMEM),
        out_specs=tuple(specs(pltpu.VMEM, pltpu.VMEM)),
    )
    plain, gram_matrix = pair(
        product_kernel, out_shape=(near_shape((width, rank)), near_shape((rank, rank)))
    )(*near(whole, right))
    half = near_shape((rank, width), jnp.bfloat16)
    return pair(weight_kernel, out_shape=(half, half))(*near(plain, gram_matrix))


def low_rank(left, high, low):
    left_high, left_low = split(left)
    dot = functools.partial(jnp.dot, preferred_element_type=jnp.float32)
    return dot(left_high, high) + (dot(left_high, low) + dot(left_low, high))


def error_pieces(counts):
    pieces, base = [], 0
    for index, count in enumerate(counts):
        pieces += [(index, place, base + place, size) for place, size in pieces_of(count, 3 * BLOCK)]
        base += count
    return pieces


def fetch_merged(counts, refs, held_ref, sems):
    copies = []
    for number, (index, place, spot, size) in enumerate(error_pieces(counts)):
        copies.append(
            pltpu.make_async_copy(
                refs[index].at[pl.ds(place, size), :], held_ref.at[pl.ds(spot, size), :], sems.at[0, number]
            )
        )
        copies[-1].start()
    return copies


def write_errors(counts, fetched, starts_ref, high, low, lefts, out_ref, held_ref, sems):
    copies = []
    for number, (index, place, spot, size) in enumerate(error_pieces(counts)):
        there = pl.ds(pl.multiple_of(starts_ref[index] + place, BLOCK), size)
        here = pl.ds(spot, size)
        change = low_rank(lefts[index][pl.ds(place, size), :], high, low)
        fetched[number].wait()
        held_ref[here, :] = held_ref[here, :] - change
        copies.append(
            pltpu.make_async_copy(held_ref.at[here, :], out_ref.at[there, :], sems.at[1, number])
        )
        copies[-1].start()
    for copy in copies:
        copy.wait()


def error_kernel(counts, starts_ref, high_ref, low_ref, *refs):
    n = len(counts)
    out_ref, held_ref, sems = refs[-3:]
    fetched = fetch_merged(counts, refs[:n], held_ref, sems)
    high, low = high_ref[...], low_ref[...]
    write_errors(counts, fetched, starts_ref, high, low, refs[n : 2 * n], out_ref, held_ref, sems)


def last_error_kernel(counts, all_counts, starts_ref, high_ref, low_ref, *refs):
    n, total = len(counts), len(all_counts)
    lefts = refs[n : n + total]
    weights_ref, momentum_ref = refs[n + total : n + total + 2]
    out_ref, weights_out, momentum_out, held_ref, left_ref, sems = refs[-6:]
    fetched = fetch_merged(counts, refs[:n], held_ref, sems)
    high, low = high_ref[...], low_ref[...]
    rows = left_ref.shape[0]
    size = min(BLOCK, rows)
    for place in range(0, rows, size):
        want = starts_ref[len(all_counts)] + place
        for index, count in enumerate(all_counts):
            skip = want - starts_ref[index]

            @pl.when((skip >= 0) & (skip < count))
            def _(index=index, skip=skip, place=place):
                left_ref[place : place + size, :] = lefts[index][pl.ds(pl.multiple_of(skip, 8), size), :]

    own_rows = low_rank(left_ref[...], high, low)
    momentum = momentum_rate * momentum_ref[...] + own_rows
    momentum_out[...] = momentum
    weights_out[...] = weights_ref[...] - outer_rate * (own_rows + momentum_rate * momentum)
    write_errors(counts, fetched, starts_ref, high, low, lefts, out_ref, held_ref, sems)


def error_scratch(counts, width):
    cuts = len(error_pieces(counts))
    return pltpu.VMEM((sum(counts), width), jnp.float32), pltpu.SemaphoreType.DMA((2, cuts))


def error_cost(counts, width, rank):
    return pl.CostEstimate(
        flops=6 * sum(counts) * width * rank, bytes_accessed=8 * sum(counts) * width, transcendentals=0
    )


def error_rows(starts, merged, lefts, high, low, shape):
    counts = [left.shape[0] for left in lefts]
    n = len(counts)
    return kernel_call(
        functools.partial(error_kernel, counts),
        out_shape=jax.ShapeDtypeStruct(shape, jnp.float32),
        in_specs=specs(pltpu.SMEM, pltpu.VMEM, pltpu.VMEM, *[pltpu.HBM] * n, *[pltpu.VMEM] * n),
        out_specs=specs(pltpu.HBM)[0],
        scratch_shapes=error_scratch(counts, shape[1]),
        cost_estimate=error_cost(counts, shape[1], high.shape[0]),
    )(jnp.stack(starts).astype(jnp.int32), *near(high, low), *map(distant, merged), *near(*lefts))


def last_rows(kept, starts, merged, lefts, other_starts, other_lefts, high, low, weights, momentum):
    rows, width = weights.shape
    counts = [left.shape[0] for left in lefts]
    all_counts = counts + [left.shape[0] for left in other_lefts]
    own = lax.axis_index("rep") * rows
    arrays = [
        jnp.stack([*starts, *other_starts, own]).astype(jnp.int32),
        *near(high, low),
        *map(distant, merged),
        *near(*lefts, *other_lefts),
        weights,
        momentum,
        kept,
    ]
    result = jax.ShapeDtypeStruct(weights.shape, jnp.float32)
    held, sems = error_scratch(counts, width)
    return kernel_call(
        functools.partial(last_error_kernel, counts, all_counts),
        out_shape=(jax.ShapeDtypeStruct(kept.shape, jnp.float32), result, result),
        in_specs=specs(
            pltpu.SMEM,
            pltpu.VMEM,
            pltpu.VMEM,
            *[pltpu.HBM] * len(counts),
            *[pltpu.VMEM] * (len(all_counts) + 2),
            pltpu.HBM,
        ),
        out_specs=tuple(specs(pltpu.HBM, pltpu.VMEM, pltpu.VMEM)),
        scratch_shapes=[held, pltpu.VMEM((rows, high.shape[0]), jnp.float32), sems],
        input_output_aliases={len(arrays) - 1: 0},
        cost_estimate=error_cost(counts, width, high.shape[0]),
    )(*arrays)


def stream_plan(replicas, rows_each):
    bits = bit_count(replicas)
    grain = max(8, 2 * BLOCK // replicas)
    units = rows_each // grain
    streams = max(1, min(3, units, bits - 1))
    widths = [units // streams + (1 if streams - 1 - s < units % streams else 0) for s in range(streams)]
    lead = list(range(min(3, bits)))
    rest = list(range(len(lead), bits))
    return [
        (w * grain, lead[s % len(lead) :] + lead[: s % len(lead)] + rest) for s, w in enumerate(widths)
    ]


def on_device(tokens_in, norm_gain, key_grad, error_in, basis_init, weights_in, momentum_in):
    replicas = lax.axis_size("rep")
    steps = bit_count(replicas)
    depth = tokens_in.shape[1]
    error = error_in[0]
    square_sums = sum_over(squares(tokens_in), "mp")
    basis = lax.all_gather(basis_init, "mp", axis=0, tiled=True)
    sources = (
        depth * lax.axis_size("mp"), tokens_in, square_sums, norm_gain[None, :], key_grad, error
    )

    plan = stream_plan(replicas, depth // replicas)
    halves, places, place = [], [], 0
    for width, order in plan:
        half = width * replicas // 2
        side = bit_of("rep", order[0])
        halves.append(half)
        places.append((place + side * half, place + (1 - side) * half))
        place += 2 * half
    streams = range(len(plan))
    order = [order for _, order in plan]
    far, got = [None] * len(plan), [None] * len(plan)
    turns = [len(plan) - 1, *range(len(plan) - 1)]
    for s in turns:
        far[s] = merge(places[s][1], halves[s], *sources)
        got[s] = flip(far[s], "rep", 1 << order[s][0])
    own = [merge(places[s][0], halves[s], *sources) for s in streams]
    parts, after = list(own), [*own, basis]
    for step in range(steps):
        for s in streams:
            if step + 1 < steps:
                side = bit_of("rep", order[s][step + 1])
                parts[s], send = join(parts[s], got[s], side, after)
                got[s] = flip(send, "rep", 1 << order[s][step + 1])
            else:
                (parts[s],) = join(parts[s], got[s], None, after)
            after = [parts[s]]

    packed = sum_everywhere(gram(parts, replicas))
    whole, right, left = first_pass(packed, basis, parts, replicas)
    high, low = second_pass(whole, right)

    lefts, place = [], 0
    for width, _ in plan:
        lefts.append(left[place : place + width])
        place += width
    for step in reversed(range(steps)):
        others = [None] * len(plan)
        for bit in range(steps):
            alike = [s for s in streams if order[s][step] == bit]
            if alike:
                came = flip(jnp.concatenate([lefts[s] for s in alike], 0), "rep", 1 << bit)
                place = 0
                for s in alike:
                    others[s] = came[place : place + lefts[s].shape[0]]
                    place += lefts[s].shape[0]
        if step:
            lefts = [stack(lefts[s], others[s], bit_of("rep", order[s][step])) for s in streams]

    here, there = [p[0] for p in places], [p[1] for p in places]
    error_out = error_rows(here, own, lefts, high, low, error.shape)
    error_out, weights_out, momentum_out = last_rows(
        error_out, there, far, others, here, lefts, high, low, weights_in[0], momentum_in[0]
    )
    return (error_out[None], weights_out[None], momentum_out[None])


def solution(mesh):
    in_specs = (
        P("rep", "mp"),
        P("mp"),
        P("rep", None),
        P("rep", "mp", None),
        P("mp", None),
        P("mp", "rep", None),
        P("mp", "rep", None),
    )
    out_specs = (P("rep", "mp", None), P("mp", "rep", None), P("mp", "rep", None))
    return jax.shard_map(
        on_device, mesh=mesh, in_specs=in_specs, out_specs=out_specs, check_vma=False
    )
```

time: 508 us -> 188 us (0.37); the launches traced: 501 us -> 187 us
  waiting for transfers between devices: 330 us -> 93.5 us
  matrix products: 82.3 us -> 0 us
  other arithmetic: 63.9 us -> 0.21 us
  Pallas kernels: 0 us -> 49.3 us
  starting transfers between devices: 0.98 us -> 39.7 us
  between operations: 14.5 us -> 1.29 us
    psum x5 -> x0, waiting for transfers between devices: 330 us -> none  [the longest x1 256 us: on_device(): combined = lax.psum(merged, 'rep') / replicas]
    ppermute x0 -> x34, waiting for transfers between devices: none -> 93.5 us  [flip(): return lax.ppermute(value, axis, [(i, i ^ mask) for i in range(size)])]
    dot_general x8 -> x0, matrix products: 78.4 us -> none  [the longest x4 41.1 us: inner_product(): lax.dot_general(first, second, (((0,), (0,)), ((), ())), precision=precis...]
    pallas_call x0 -> x34, Pallas kernels: none -> 49.3 us  [the longest x6 15.7 us: merge(): kernel_call(functools.partial(merge_kernel, cuts, depth), out_shape=near_...]
    another operation x10 -> x1, other arithmetic: 45.7 us -> 0.08 us  [error_rows(): jnp.stack(starts).astype(jnp.int32)]
    ppermute x0 -> x34, starting transfers between devices: none -> 39.7 us  [flip(): return lax.ppermute(value, axis, [(i, i ^ mask) for i in range(size)])]
    broadcast_in_dim x1 -> x0, other arithmetic: 11.3 us -> none  [on_device(): error_out = (merged - approximant)[None]]
  transfers between devices with their start and end apart: 5 -> 34, of which waited for: 5 -> 26; matrix products, arithmetic and copies ran while one was open for 0% -> 0% of each run, Pallas kernels for 0% -> 15%
where the time goes in v1:
time: 188 us; the launch traced here: 187 us
  waiting for transfers between devices  93.5 us (50%)
  Pallas kernels  49.3 us (26%)
  starting transfers between devices  39.7 us (21%)
  blocking collectives  2.16 us (1%)
    ppermute x34, waiting for transfers between devices, flip(): return lax.ppermute(value, axis, [(i, i ^ mask) for i in range(size)])  93.5 us
    ppermute x34, starting transfers between devices, flip(): return lax.ppermute(value, axis, [(i, i ^ mask) for i in range(size)])  39.7 us
    pallas_call x6, Pallas kernels, merge(): kernel_call(functools.partial(merge_kernel, cuts, depth), out_shape=near_...  15.7 us
    pallas_call x1, Pallas kernels, first_pass(): kernel_call(functools.partial(first_kernel, replicas), out_shape=(near_sh...  7.78 us
    pallas_call x1, Pallas kernels, last_rows(): kernel_call(functools.partial(last_error_kernel, counts, all_counts), out...  6 us
    pallas_call x12, Pallas kernels, join(): kernel_call(kernel, out_shape=shapes, in_specs=specs(*places, *[pl.ANY] *...  5.59 us
    pallas_call x1, Pallas kernels, error_rows(): kernel_call(functools.partial(error_kernel, counts), out_shape=jax.ShapeD...  5.03 us
    pallas_call x1, Pallas kernels, second_pass(): pair(weight_kernel, out_shape=(half, half))(*near(plain, gram_matrix))  4.8 us
  transfers between devices with their start and end apart: 34, of which 26 were waited for; matrix products, arithmetic and copies ran while one was open for 0% of the time, Pallas kernels for 15%

profile of v1, /device:TPU:0, one launch (start us, length us, event | category | flops | bytes accessed | tf_op | source)
XLA Modules:
  0.0 187.5 jit_solution(13102857975722006950)
XLA Ops:
  4.0 3.1 %shard_map.100.refs_2_ = f32[768,512]{1,0:T(8,128)} custom-call(s32[1]{0:T(128)} %bitcast.2.start_ref, bf16[256,4096]{1,0:T(8,128)(2,1)} %tokens_ref.13, f32[256,128]{1,0:T(8,128)S(1)} %add.63.squares_ref, bf16[1,4096]{1,0:T(2,128)(2,1)S(1)} %broadcast_in_dim.16.gain_ref, bf16[256,512]{1,0:T(8,128)(2,1)S(1)} %copy-done.3, f32[4096,512]{1,0:T(8,128)} %bitcast.19), custom_call_target="tpu_custom_call" | custom-call | flops 201326592 | bytes 3538944 | tf_op jit(solution)/shard_map/pallas_call | solution.py:193
  7.1 3.0 %collective-permute-start.3 = (f32[768,512]{1,0:T(8,128)}, f32[768,512]{1,0:T(8,128)}, u32[]{:S(2)}, u32[]{:S(2)}) collective-permute-start(f32[768,512]{1,0:T(8,128)} %shard_map.100.refs_2_), channel_id=1, source_target_pairs={{0,8},{2,10},{4,12},{6,14},{8,0},{10,2},{12,4},{14,6},{16,24},{18,... | collective-permute-start | bytes 4718600 | tf_op jit(solution)/shard_map/ppermute | solution.py:30
  10.1 3.0 %shard_map.96.refs_0_ = f32[640,512]{1,0:T(8,128)} custom-call(s32[1]{0:T(128)} %bitcast.start_ref, bf16[256,4096]{1,0:T(8,128)(2,1)} %tokens_ref.13, f32[256,128]{1,0:T(8,128)S(1)} %add.63.squares_ref, bf16[1,4096]{1,0:T(2,128)(2,1)S(1)} %broadcast_in_dim.16.gain_ref, bf16[256,512]{1,0:T(8,128)(2,1)S(1)} %copy-done.3, f32[4096,512]{1,0:T(8,128)} %bitcast.20), custom_call_target="tpu_custom_call" | custom-call | flops 167772160 | bytes 2949120 | tf_op jit(solution)/shard_map/pallas_call | solution.py:193
  14.6 3.0 %shard_map.101.refs_1_ = f32[640,512]{1,0:T(8,128)} custom-call(s32[1]{0:T(128)} %bitcast.1.start_ref, bf16[256,4096]{1,0:T(8,128)(2,1)} %tokens_ref.13, f32[256,128]{1,0:T(8,128)S(1)} %add.63.squares_ref, bf16[1,4096]{1,0:T(2,128)(2,1)S(1)} %broadcast_in_dim.16.gain_ref, bf16[256,512]{1,0:T(8,128)(2,1)S(1)} %copy-done.3, f32[4096,512]{1,0:T(8,128)} %bitcast.21), custom_call_target="tpu_custom_call" | custom-call | flops 167772160 | bytes 2949120 | tf_op jit(solution)/shard_map/pallas_call | solution.py:193
  23.2 2.3 %shard_map.95.own_ref.refs_0_ = f32[640,512]{1,0:T(8,128)S(1)} custom-call(s32[1]{0:T(128)} %bitcast.3.start_ref, bf16[256,4096]{1,0:T(8,128)(2,1)} %tokens_ref.13, f32[256,128]{1,0:T(8,128)S(1)} %add.63.squares_ref, bf16[1,4096]{1,0:T(2,128)(2,1)S(1)} %broadcast_in_dim.16.gain_ref, bf16[256,512]{1,0:T(8,128)(2,1)S(1)} %copy-done.3, f32[4096,512]{1,0:T(8,128)} %bitcast.23), custom_call_target="tpu_custom_call" | custom-call | flops 167772160 | bytes 2949120 | tf_op jit(solution)/shard_map/pallas_call | solution.py:193
  25.6 2.4 %shard_map.98.refs_2_.own_ref = f32[768,512]{1,0:T(8,128)S(1)} custom-call(s32[1]{0:T(128)} %bitcast.5.start_ref, bf16[256,4096]{1,0:T(8,128)(2,1)} %tokens_ref.13, f32[256,128]{1,0:T(8,128)S(1)} %add.63.squares_ref, bf16[1,4096]{1,0:T(2,128)(2,1)S(1)} %broadcast_in_dim.16.gain_ref, bf16[256,512]{1,0:T(8,128)(2,1)S(1)} %copy-done.3, f32[4096,512]{1,0:T(8,128)} %bitcast.24), custom_call_target="tpu_custom_call" | custom-call | flops 201326592 | bytes 3538944 | tf_op jit(solution)/shard_map/pallas_call | solution.py:193
  28.0 16.0 %collective-permute-done.1.got_ref = f32[640,512]{1,0:T(8,128)} collective-permute-done((f32[640,512]{1,0:T(8,128)}, f32[640,512]{1,0:T(8,128)}, u32[]{:S(2)}, u32[]{:S(2)}) %collective-permute-start.1) | collective-permute-done | bytes 1310752 | tf_op jit(solution)/shard_map/ppermute | solution.py:30
  45.5 2.8 %collective-permute-done.4.got_ref = f32[640,512]{1,0:T(8,128)} collective-permute-done((f32[640,512]{1,0:T(8,128)}, f32[640,512]{1,0:T(8,128)}, u32[]{:S(2)}, u32[]{:S(2)}) %collective-permute-start.4) | collective-permute-done | bytes 1310752 | tf_op jit(solution)/shard_map/ppermute | solution.py:30
  53.9 13.1 %collective-permute-done.2.got_ref = f32[320,512]{1,0:T(8,128)S(1)} collective-permute-done((f32[320,512]{1,0:T(8,128)S(1)}, f32[320,512]{1,0:T(8,128)S(1)}, u32[]{:S(2)}, u32[]{:S(2)}) %collective-permute-start.2) | collective-permute-done | bytes 655392 | tf_op jit(solution)/shard_map/ppermute | solution.py:30
  72.2 6.3 %collective-permute-done.5.got_ref = f32[160,512]{1,0:T(8,128)S(1)} collective-permute-done((f32[160,512]{1,0:T(8,128)}, f32[160,512]{1,0:T(8,128)S(1)}, u32[]{:S(2)}, u32[]{:S(2)}) %collective-permute-start.5) | collective-permute-done | bytes 327712 | tf_op jit(solution)/shard_map/ppermute | solution.py:30
  78.8 3.2 %collective-permute-start.12 = (f32[96,512]{1,0:T(8,128)S(1)}, f32[96,512]{1,0:T(8,128)S(1)}, u32[]{:S(2)}, u32[]{:S(2)}) collective-permute-start(f32[96,512]{1,0:T(8,128)S(1)} %get-tuple-element.48), channel_id=1, source_target_pairs={{0,16},{2,18},{4,20},{6,22},{8,24},{10,26},{12,28},{14,30},{16,0},... | collective-permute-start | bytes 589832 | tf_op jit(solution)/shard_map/ppermute | solution.py:30
  82.1 2.8 %collective-permute-start.11 = (f32[80,512]{1,0:T(8,128)S(1)}, f32[80,512]{1,0:T(8,128)S(1)}, u32[]{:S(2)}, u32[]{:S(2)}) collective-permute-start(f32[80,512]{1,0:T(8,128)S(1)} %get-tuple-element.47), channel_id=1, source_target_pairs={{0,16},{2,18},{4,20},{6,22},{8,24},{10,26},{12,28},{14,30},{16,0},... | collective-permute-start | bytes 491528 | tf_op jit(solution)/shard_map/ppermute | solution.py:30
  84.9 14.7 %collective-permute-done.8.got_ref = f32[80,512]{1,0:T(8,128)S(1)} collective-permute-done((f32[80,512]{1,0:T(8,128)S(1)}, f32[80,512]{1,0:T(8,128)S(1)}, u32[]{:S(2)}, u32[]{:S(2)}) %collective-permute-start.8) | collective-permute-done | bytes 163872 | tf_op jit(solution)/shard_map/ppermute | solution.py:30
  104.7 2.4 %collective-permute-start.16 = (f32[160,128]{1,0:T(8,128)S(1)}, f32[160,128]{1,0:T(8,128)S(1)}, u32[]{:S(2)}, u32[]{:S(2)}) collective-permute-start(f32[160,128]{1,0:T(8,128)S(1)} %get-tuple-element.62), channel_id=1, source_target_pairs={{0,6},{2,4},{4,2},{6,0},{8,14},{10,12},{12,10},{14,8},{16,22},{18,... | collective-permute-start | bytes 245768 | tf_op jit(solution)/shard_map/ppermute | solution.py:30
  109.3 2.2 %collective-permute-done.16 = f32[160,128]{1,0:T(8,128)S(1)} collective-permute-done((f32[160,128]{1,0:T(8,128)S(1)}, f32[160,128]{1,0:T(8,128)S(1)}, u32[]{:S(2)}, u32[]{:S(2)}) %collective-permute-start.16) | collective-permute-done | bytes 81952 | tf_op jit(solution)/shard_map/ppermute | solution.py:30
  112.6 2.7 %collective-permute-start.19 = (f32[160,128]{1,0:T(8,128)S(1)}, f32[160,128]{1,0:T(8,128)S(1)}, u32[]{:S(2)}, u32[]{:S(2)}) collective-permute-start(f32[160,128]{1,0:T(8,128)S(1)} %add_add_fusion.1), channel_id=1, source_target_pairs={{0,24},{2,26},{4,28},{6,30},{8,16},{10,18},{12,20},{14,22},{16,8},... | collective-permute-start | bytes 245768 | tf_op jit(solution)/shard_map/ppermute | solution.py:30
  119.3 2.5 %collective-permute-done.18 = f32[160,128]{1,0:T(8,128)S(1)} collective-permute-done((f32[160,128]{1,0:T(8,128)S(1)}, f32[160,128]{1,0:T(8,128)S(1)}, u32[]{:S(2)}, u32[]{:S(2)}) %collective-permute-start.18) | collective-permute-done | bytes 81952 | tf_op jit(solution)/shard_map/ppermute | solution.py:30
  130.8 7.8 %shard_map.114 = (f32[512,512]{1,0:T(8,128)S(1)}, f32[512,128]{1,0:T(8,128)S(1)}, f32[256,128]{1,0:T(8,128)S(1)}) custom-call(f32[1280,128]{1,0:T(8,128)S(1)} %constant_dynamic-update-slice_fusion.packed_ref, f32[512,128]{1,0:T(8,128)S(1)} %all_gather.3.refs_3_.basis_ref, f32[80,512]{1,0:T(8,128)S(1)} %shard_map.110.refs_0_, ...), custom_call_target="tpu_custom_call" | custom-call | tf_op jit(solution)/shard_map/pallas_call | solution.py:343
  139.8 8.1 %collective-permute-done.24 = f32[256,128]{1,0:T(8,128)S(1)} collective-permute-done((f32[256,128]{1,0:T(8,128)S(1)}, f32[256,128]{1,0:T(8,128)S(1)}, u32[]{:S(2)}, u32[]{:S(2)}) %collective-permute-start.24) | collective-permute-done | bytes 131104 | tf_op jit(solution)/shard_map/ppermute | solution.py:30
  149.0 3.7 %collective-permute-done.31.got_ref = f32[192,128]{1,0:T(8,128)S(1)} collective-permute-done((f32[192,128]{1,0:T(8,128)S(1)}, f32[192,128]{1,0:T(8,128)S(1)}, u32[]{:S(2)}, u32[]{:S(2)}) %collective-permute-start.31) | collective-permute-done | bytes 98336 | tf_op jit(solution)/shard_map/ppermute | solution.py:30
  154.9 3.7 %collective-permute-done.25.got_ref = f32[160,128]{1,0:T(8,128)S(1)} collective-permute-done((f32[160,128]{1,0:T(8,128)S(1)}, f32[160,128]{1,0:T(8,128)S(1)}, u32[]{:S(2)}, u32[]{:S(2)}) %collective-permute-start.25) | collective-permute-done | bytes 81952 | tf_op jit(solution)/shard_map/ppermute | solution.py:30
  171.4 4.8 %shard_map.116 = (bf16[128,512]{1,0:T(8,128)(2,1)S(1)}, bf16[128,512]{1,0:T(8,128)(2,1)S(1)}) custom-call(f32[512,128]{1,0:T(8,128)S(1)} %get-tuple-element.51.plain_ref, f32[128,128]{1,0:T(8,128)S(1)} %get-tuple-element.52.gram_ref), custom_call_target="tpu_custom_call" | custom-call | tf_op jit(solution)/shard_map/pallas_call | solution.py:380
  176.2 5.0 %shard_map.126.refs_11_ = f32[4096,512]{1,0:T(8,128)} custom-call(s32[3]{0:T(128)S(1)} %pad_add_fusion.starts_ref, bf16[128,512]{1,0:T(8,128)(2,1)S(1)} %get-tuple-element.53.high_ref, bf16[128,512]{1,0:T(8,128)(2,1)S(1)} %get-tuple-element.54.low_ref, f32[640,512]{1,0:T(8,128)} %copy-done.2, f32[640,512]{1,0:T(8,128)} %copy-done.1, f32[768,512]{1,0:T(8,128)} %copy-done, ...), custom_call_target="tpu_custom_call" | custom-call | flops 805306368 | bytes 8388608 | tf_op jit(solution)/shard_map/pallas_call | solution.py:472
  181.3 6.0 %shard_map.127 = (f32[4096,512]{1,0:T(8,128)}, f32[256,512]{1,0:T(8,128)}, f32[256,512]{1,0:T(8,128)}) custom-call(s32[7]{0:T(128)S(1)} %stack.37.starts_ref, bf16[128,512]{1,0:T(8,128)(2,1)S(1)} %get-tuple-element.53.high_ref, bf16[128,512]{1,0:T(8,128)(2,1)S(1)} %get-tuple-element.54.low_ref, ...), custom_call_target="tpu_custom_call", output_to_operand_aliasing={{0}: (14, {})} | custom-call | flops 805306368 | bytes 8388608 | tf_op jit(solution)/shard_map/pallas_call | solution.py:498
  (118 shorter events, 61.6 us)
Async XLA Ops:
  7.1 42.6 %collective-permute-start.3 = (f32[768,512]{1,0:T(8,128)}, f32[768,512]{1,0:T(8,128)}, u32[]{:S(2)}, u32[]{:S(2)}) collective-permute-start(f32[768,512]{1,0:T(8,128)} %shard_map.100.refs_2_), channel_id=1, source_target_pairs={{0,8},{2,10},{4,12},{6,14},{8,0},{10,2},{12,4},{14,6},{16,24},{18,... | collective-permute-start | bytes 4718600 | tf_op jit(solution)/shard_map/ppermute | solution.py:30
  13.1 30.9 %collective-permute-start.1 = (f32[640,512]{1,0:T(8,128)}, f32[640,512]{1,0:T(8,128)}, u32[]{:S(2)}, u32[]{:S(2)}) collective-permute-start(f32[640,512]{1,0:T(8,128)} %shard_map.96.refs_0_), channel_id=1, source_target_pairs={{0,2},{2,0},{4,6},{6,4},{8,10},{10,8},{12,14},{14,12},{16,18},{18,... | collective-permute-start | bytes 3932168 | tf_op jit(solution)/shard_map/ppermute | solution.py:30
  17.6 30.7 %collective-permute-start.4 = (f32[640,512]{1,0:T(8,128)}, f32[640,512]{1,0:T(8,128)}, u32[]{:S(2)}, u32[]{:S(2)}) collective-permute-start(f32[640,512]{1,0:T(8,128)} %shard_map.101.refs_1_), channel_id=1, source_target_pairs={{0,4},{2,6},{4,0},{6,2},{8,12},{10,14},{12,8},{14,10},{16,20},{18,... | collective-permute-start | bytes 3932168 | tf_op jit(solution)/shard_map/ppermute | solution.py:30
  51.3 18.2 %collective-permute-start.6 = (f32[384,512]{1,0:T(8,128)S(1)}, f32[384,512]{1,0:T(8,128)S(1)}, u32[]{:S(2)}, u32[]{:S(2)}) collective-permute-start(f32[384,512]{1,0:T(8,128)S(1)} %get-tuple-element.37), channel_id=1, source_target_pairs={{0,2},{2,0},{4,6},{6,4},{8,10},{10,8},{12,14},{14,12},{16,18},{18,... | collective-permute-start | bytes 2359304 | tf_op jit(solution)/shard_map/ppermute | solution.py:30
  51.9 15.0 %collective-permute-start.2 = (f32[320,512]{1,0:T(8,128)S(1)}, f32[320,512]{1,0:T(8,128)S(1)}, u32[]{:S(2)}, u32[]{:S(2)}) collective-permute-start(f32[320,512]{1,0:T(8,128)S(1)} %get-tuple-element.32), channel_id=1, source_target_pairs={{0,4},{2,6},{4,0},{6,2},{8,12},{10,14},{12,8},{14,10},{16,20},{18,... | collective-permute-start | bytes 1966088 | tf_op jit(solution)/shard_map/ppermute | solution.py:30
  53.4 14.8 %collective-permute-start.7 = (f32[320,512]{1,0:T(8,128)S(1)}, f32[320,512]{1,0:T(8,128)S(1)}, u32[]{:S(2)}, u32[]{:S(2)}) collective-permute-start(f32[320,512]{1,0:T(8,128)S(1)} %get-tuple-element.38), channel_id=1, source_target_pairs={{0,8},{2,10},{4,12},{6,14},{8,0},{10,2},{12,4},{14,6},{16,24},{18,... | collective-permute-start | bytes 1966088 | tf_op jit(solution)/shard_map/ppermute | solution.py:30
  69.6 9.2 %collective-permute-start.9 = (f32[192,512]{1,0:T(8,128)S(1)}, f32[192,512]{1,0:T(8,128)S(1)}, u32[]{:S(2)}, u32[]{:S(2)}) collective-permute-start(f32[192,512]{1,0:T(8,128)S(1)} %get-tuple-element.43), channel_id=1, source_target_pairs={{0,4},{2,6},{4,0},{6,2},{8,12},{10,14},{12,8},{14,10},{16,20},{18,... | collective-permute-start | bytes 1179656 | tf_op jit(solution)/shard_map/ppermute | solution.py:30
  71.2 7.3 %collective-permute-start.5 = (f32[160,512]{1,0:T(8,128)}, f32[160,512]{1,0:T(8,128)S(1)}, u32[]{:S(2)}, u32[]{:S(2)}) collective-permute-start(f32[160,512]{1,0:T(8,128)} %get-tuple-element.36), channel_id=1, source_target_pairs={{0,8},{2,10},{4,12},{6,14},{8,0},{10,2},{12,4},{14,6},{16,24},{18,... | collective-permute-start | bytes 983048 | tf_op jit(solution)/shard_map/ppermute | solution.py:30
  71.6 7.1 %collective-permute-start.10 = (f32[160,512]{1,0:T(8,128)S(1)}, f32[160,512]{1,0:T(8,128)S(1)}, u32[]{:S(2)}, u32[]{:S(2)}) collective-permute-start(f32[160,512]{1,0:T(8,128)S(1)} %get-tuple-element.44), channel_id=1, source_target_pairs={{0,2},{2,0},{4,6},{6,4},{8,10},{10,8},{12,14},{14,12},{16,18},{18,... | collective-permute-start | bytes 983048 | tf_op jit(solution)/shard_map/ppermute | solution.py:30
  78.8 22.6 %collective-permute-start.12 = (f32[96,512]{1,0:T(8,128)S(1)}, f32[96,512]{1,0:T(8,128)S(1)}, u32[]{:S(2)}, u32[]{:S(2)}) collective-permute-start(f32[96,512]{1,0:T(8,128)S(1)} %get-tuple-element.48), channel_id=1, source_target_pairs={{0,16},{2,18},{4,20},{6,22},{8,24},{10,26},{12,28},{14,30},{16,0},... | collective-permute-start | bytes 589832 | tf_op jit(solution)/shard_map/ppermute | solution.py:30
  82.0 17.6 %collective-permute-start.8 = (f32[80,512]{1,0:T(8,128)S(1)}, f32[80,512]{1,0:T(8,128)S(1)}, u32[]{:S(2)}, u32[]{:S(2)}) collective-permute-start(f32[80,512]{1,0:T(8,128)S(1)} %get-tuple-element.42), channel_id=1, source_target_pairs={{0,16},{2,18},{4,20},{6,22},{8,24},{10,26},{12,28},{14,30},{16,0},... | collective-permute-start | bytes 491528 | tf_op jit(solution)/shard_map/ppermute | solution.py:30
  82.1 19.3 %collective-permute-start.11 = (f32[80,512]{1,0:T(8,128)S(1)}, f32[80,512]{1,0:T(8,128)S(1)}, u32[]{:S(2)}, u32[]{:S(2)}) collective-permute-start(f32[80,512]{1,0:T(8,128)S(1)} %get-tuple-element.47), channel_id=1, source_target_pairs={{0,16},{2,18},{4,20},{6,22},{8,24},{10,26},{12,28},{14,30},{16,0},... | collective-permute-start | bytes 491528 | tf_op jit(solution)/shard_map/ppermute | solution.py:30
  104.7 6.8 %collective-permute-start.16 = (f32[160,128]{1,0:T(8,128)S(1)}, f32[160,128]{1,0:T(8,128)S(1)}, u32[]{:S(2)}, u32[]{:S(2)}) collective-permute-start(f32[160,128]{1,0:T(8,128)S(1)} %get-tuple-element.62), channel_id=1, source_target_pairs={{0,6},{2,4},{4,2},{6,0},{8,14},{10,12},{12,10},{14,8},{16,22},{18,... | collective-permute-start | bytes 245768 | tf_op jit(solution)/shard_map/ppermute | solution.py:30
  107.2 5.4 %collective-permute-start.15 = (f32[160,128]{1,0:T(8,128)S(1)}, f32[160,128]{1,0:T(8,128)S(1)}, u32[]{:S(2)}, u32[]{:S(2)}) collective-permute-start(f32[160,128]{1,0:T(8,128)S(1)} %get-tuple-element.63), channel_id=1, source_target_pairs={{0,4},{2,6},{4,0},{6,2},{8,12},{10,14},{12,8},{14,10},{16,20},{18,... | collective-permute-start | bytes 245768 | tf_op jit(solution)/shard_map/ppermute | solution.py:30
  112.6 6.6 %collective-permute-start.19 = (f32[160,128]{1,0:T(8,128)S(1)}, f32[160,128]{1,0:T(8,128)S(1)}, u32[]{:S(2)}, u32[]{:S(2)}) collective-permute-start(f32[160,128]{1,0:T(8,128)S(1)} %add_add_fusion.1), channel_id=1, source_target_pairs={{0,24},{2,26},{4,28},{6,30},{8,16},{10,18},{12,20},{14,22},{16,8},... | collective-permute-start | bytes 245768 | tf_op jit(solution)/shard_map/ppermute | solution.py:30
  115.3 6.5 %collective-permute-start.18 = (f32[160,128]{1,0:T(8,128)S(1)}, f32[160,128]{1,0:T(8,128)S(1)}, u32[]{:S(2)}, u32[]{:S(2)}) collective-permute-start(f32[160,128]{1,0:T(8,128)S(1)} %add_add_fusion.1), channel_id=1, source_target_pairs={{0,16},{2,18},{4,20},{6,22},{8,24},{10,26},{12,28},{14,30},{16,0},... | collective-permute-start | bytes 245768 | tf_op jit(solution)/shard_map/ppermute | solution.py:30
  115.3 6.5 %collective-permute-start.17 = (f32[160,128]{1,0:T(8,128)S(1)}, f32[160,128]{1,0:T(8,128)S(1)}, u32[]{:S(2)}, u32[]{:S(2)}) collective-permute-start(f32[160,128]{1,0:T(8,128)S(1)} %add_add_fusion.1), channel_id=1, source_target_pairs={{0,8},{2,10},{4,12},{6,14},{8,0},{10,2},{12,4},{14,6},{16,24},{18,... | collective-permute-start | bytes 245768 | tf_op jit(solution)/shard_map/ppermute | solution.py:30
  138.6 9.3 %collective-permute-start.24 = (f32[256,128]{1,0:T(8,128)S(1)}, f32[256,128]{1,0:T(8,128)S(1)}, u32[]{:S(2)}, u32[]{:S(2)}) collective-permute-start(f32[256,128]{1,0:T(8,128)S(1)} %get-tuple-element.55), channel_id=1, source_target_pairs={{0,16},{2,18},{4,20},{6,22},{8,24},{10,26},{12,28},{14,30},{16,0},... | collective-permute-start | bytes 393224 | tf_op jit(solution)/shard_map/ppermute | solution.py:30
  152.7 8.1 %collective-permute-start.32 = (f32[384,128]{1,0:T(8,128)S(1)}, f32[384,128]{1,0:T(8,128)S(1)}, u32[]{:S(2)}, u32[]{:S(2)}) collective-permute-start(f32[384,128]{1,0:T(8,128)S(1)} %shard_map.124.own_ref), channel_id=1, source_target_pairs={{0,2},{2,0},{4,6},{6,4},{8,10},{10,8},{12,14},{14,12},{16,18},{18,... | collective-permute-start | bytes 589832 | tf_op jit(solution)/shard_map/ppermute | solution.py:30
  154.2 5.5 %collective-permute-start.28 = (f32[160,128]{1,0:T(8,128)S(1)}, f32[160,128]{1,0:T(8,128)S(1)}, u32[]{:S(2)}, u32[]{:S(2)}) collective-permute-start(f32[160,128]{1,0:T(8,128)S(1)} %shard_map.120.own_ref), channel_id=1, source_target_pairs={{0,2},{2,0},{4,6},{6,4},{8,10},{10,8},{12,14},{14,12},{16,18},{18,... | collective-permute-start | bytes 245768 | tf_op jit(solution)/shard_map/ppermute | solution.py:30
  159.7 7.2 %collective-permute-start.29 = (f32[320,128]{1,0:T(8,128)S(1)}, f32[320,128]{1,0:T(8,128)S(1)}, u32[]{:S(2)}, u32[]{:S(2)}) collective-permute-start(f32[320,128]{1,0:T(8,128)S(1)} %shard_map.121.own_ref), channel_id=1, source_target_pairs={{0,8},{2,10},{4,12},{6,14},{8,0},{10,2},{12,4},{14,6},{16,24},{18,... | collective-permute-start | bytes 491528 | tf_op jit(solution)/shard_map/ppermute | solution.py:30
  160.8 20.5 %collective-permute-start.33 = (f32[768,128]{1,0:T(8,128)S(1)}, f32[768,128]{1,0:T(8,128)S(1)}, u32[]{:S(2)}, u32[]{:S(2)}) collective-permute-start(f32[768,128]{1,0:T(8,128)S(1)} %shard_map.125.refs_5_.refs_8_), channel_id=1, source_target_pairs={{0,8},{2,10},{4,12},{6,14},{8,0},{10,2},{12,4},{14,6},{16,24},{18,... | collective-permute-start | bytes 1179656 | tf_op jit(solution)/shard_map/ppermute | solution.py:30
  164.0 17.2 %collective-permute-start.27 = (f32[640,128]{1,0:T(8,128)S(1)}, f32[640,128]{1,0:T(8,128)S(1)}, u32[]{:S(2)}, u32[]{:S(2)}) collective-permute-start(f32[640,128]{1,0:T(8,128)S(1)} %shard_map.119.refs_3_.refs_6_), channel_id=1, source_target_pairs={{0,2},{2,0},{4,6},{6,4},{8,10},{10,8},{12,14},{14,12},{16,18},{18,... | collective-permute-start | bytes 983048 | tf_op jit(solution)/shard_map/ppermute | solution.py:30
  166.9 14.3 %collective-permute-start.30 = (f32[640,128]{1,0:T(8,128)S(1)}, f32[640,128]{1,0:T(8,128)S(1)}, u32[]{:S(2)}, u32[]{:S(2)}) collective-permute-start(f32[640,128]{1,0:T(8,128)S(1)} %shard_map.122.refs_4_.refs_7_), channel_id=1, source_target_pairs={{0,4},{2,6},{4,0},{6,2},{8,12},{10,14},{12,8},{14,10},{16,20},{18,... | collective-permute-start | bytes 983048 | tf_op jit(solution)/shard_map/ppermute | solution.py:30
  (20 other events, 149.1 us)

commit v2 on v1

--- a/solution.py
+++ b/solution.py
@@ -1,3 +1,4 @@
+import dataclasses
 import functools
 
 import jax
@@ -8,6 +9,14 @@
 from jax.sharding import PartitionSpec as P
 
 BLOCK = 128
+
+SHARES = (
+    (5, (0, 1, 2, 3)),
+    (5, (1, 2, 0, 3)),
+    (6, (2, 0, 1, 3)),
+)
+BACK = {0: (3, 2, 1, 0), 1: (3, 0, 2, 1), 2: (3, 1, 0, 2)}
+TURNS = (2, 0, 1)
 
 precise = lax.Precision.HIGHEST
 epsilon = 1e-05
@@ -95,7 +104,7 @@
 
 def kernel_call(*args, **options):
     return pl.pallas_call(
-        *args, compiler_params=pltpu.CompilerParams(vmem_limit_bytes=16 * 2**20), **options
+        *args, compiler_params=pltpu.CompilerParams(vmem_limit_bytes=10 * 2**20), **options
     )
 
 
@@ -161,51 +170,55 @@
 
 
 def merge_kernel(
-    cuts, depth, start_ref, tokens_ref, squares_ref, gain_ref, grad_ref, error_ref, out_ref, held_ref, sems
+    counts, depth, starts_ref, tokens_ref, squares_ref, gain_ref, grad_ref, error_ref, *refs
 ):
-    copies = []
-    for index, (place, size) in enumerate(cuts):
-        there = pl.ds(pl.multiple_of(start_ref[0] + place, BLOCK), size)
-        here = pl.ds(place, size)
-        pair = [
-            pltpu.make_async_copy(tokens_ref.at[:, there], held_ref.at[:, here], sems.at[index, 0]),
-            pltpu.make_async_copy(error_ref.at[there, :], out_ref.at[here, :], sems.at[index, 1]),
-        ]
-        for copy in pair:
-            copy.start()
-        copies.append(pair)
+    outs, held_ref, sems = refs[: len(counts)], refs[-2], refs[-1]
+    pieces, base = [], 0
+    for s, count in counts:
+        for place, size in pieces_of(count, 2 * BLOCK):
+            there = pl.ds(pl.multiple_of(starts_ref[s] + place, BLOCK), size)
+            here, spot = pl.ds(place, size), pl.ds(base + place, size)
+            number = len(pieces)
+            copies = [
+                pltpu.make_async_copy(tokens_ref.at[:, there], held_ref.at[:, spot], sems.at[number, 0]),
+                pltpu.make_async_copy(error_ref.at[there, :], outs[s].at[here, :], sems.at[number, 1]),
+            ]
+            for copy in copies:
+                copy.start()
+            pieces.append((s, there, here, spot, copies))
+        base += count
     scale = lax.rsqrt(squares_ref[...] / depth + epsilon)[:, :1]
-    for pair, (place, size) in zip(copies, cuts):
-        here = pl.ds(place, size)
-        there = pl.ds(pl.multiple_of(start_ref[0] + place, BLOCK), size)
+    for s, there, here, spot, copies in pieces:
         gain = gain_ref[:, there].astype(jnp.float32)
-        pair[0].wait()
-        normed = (held_ref[:, here].astype(jnp.float32) * scale * gain).astype(jnp.bfloat16)
+        copies[0].wait()
+        normed = (held_ref[:, spot].astype(jnp.float32) * scale * gain).astype(jnp.bfloat16)
         change = lax.dot_general(
             normed, grad_ref[...], (((0,), (0,)), ((), ())), preferred_element_type=jnp.float32
         )
-        pair[1].wait()
-        out_ref[here, :] = change + out_ref[here, :]
-
-
-def merge(start, count, depth, tokens, square_sums, gain, grad, error):
-    cuts = pieces_of(count, 3 * BLOCK)
+        copies[1].wait()
+        outs[s][here, :] = change + outs[s][here, :]
+
+
+def merge(starts, counts, turns, depth, tokens, square_sums, gain, grad, error):
+    rows = sum(counts)
+    in_turn = [(s, counts[s]) for s in turns]
+    pieces = sum(len(pieces_of(count, 2 * BLOCK)) for count in counts)
     return kernel_call(
-        functools.partial(merge_kernel, cuts, depth),
-        out_shape=near_shape((count, grad.shape[1])),
+        functools.partial(merge_kernel, in_turn, depth),
+        out_shape=tuple(near_shape((count, grad.shape[1])) for count in counts),
         in_specs=specs(pltpu.SMEM, pltpu.HBM, pltpu.VMEM, pltpu.VMEM, pltpu.VMEM, pltpu.HBM),
-        out_specs=specs(pltpu.VMEM)[0],
+        out_specs=tuple(specs(*[pltpu.VMEM] * len(counts))),
         scratch_shapes=[
-            pltpu.VMEM((tokens.shape[0], count), tokens.dtype),
-            pltpu.SemaphoreType.DMA((len(cuts), 2)),
+            pltpu.VMEM((tokens.shape[0], rows), tokens.dtype),
+            pltpu.SemaphoreType.DMA((pieces, 2)),
         ],
         cost_estimate=pl.CostEstimate(
-            flops=2 * count * grad.shape[1] * tokens.shape[0],
-            bytes_accessed=8 * count * grad.shape[1] + 2 * tokens.shape[0] * count,
+            flops=2 * rows * grad.shape[1] * tokens.shape[0],
+            bytes_accessed=8 * rows * grad.shape[1] + 2 * tokens.shape[0] * rows,
             transcendentals=0,
         ),
     )(
-        jnp.reshape(start, (1,)).astype(jnp.int32),
+        jnp.stack(starts).astype(jnp.int32),
         distant(tokens),
         *near(square_sums, gain, grad),
         distant(error),
@@ -246,21 +259,50 @@
     )(*arrays, *after)
 
 
-def stack_kernel(count, side_ref, own_ref, got_ref, out_ref):
-    stays, goes = sides_of(side_ref[0], count)
-    out_ref[stays, :] = own_ref[...]
-    out_ref[goes, :] = got_ref[...]
-
-
-def stack(own, got, side):
-    count, width = own.shape
+def bundles(plan, step):
+    bits = sorted({stream.back[step] for stream in plan})
+    groups = [[s for s, stream in enumerate(plan) if stream.back[step] == bit] for bit in bits]
+    where = {}
+    for index, group in enumerate(groups):
+        place = 0
+        for s in group:
+            where[s] = (index, place)
+            place += plan[s].width << step
+    return bits, groups, where
+
+
+def bundle_shapes(plan, step, width):
+    _, groups, _ = bundles(plan, step)
+    return tuple(near_shape((sum(plan[s].width << step for s in group), width)) for group in groups)
+
+
+def gather_kernel(plan, step, sides_ref, *refs):
+    bits, groups, before = bundles(plan, step)
+    _, later_groups, after = bundles(plan, step + 1)
+    n = len(groups)
+    own, got, out = refs[:n], refs[n : 2 * n], refs[-len(later_groups) :]
+    for s, stream in enumerate(plan):
+        source, from_row = before[s]
+        target, to_row = after[s]
+        bit = stream.back[step]
+        place = stream.order.index(bit)
+        outer = 1 << sum(stream.order.index(b) < place for b in stream.back[:step])
+        inner = (stream.width << step) // outer
+        for i in range(outer):
+            for refs_of, side in ((own, sides_ref[bit]), (got, 1 - sides_ref[bit])):
+                row = pl.multiple_of(to_row + 2 * i * inner + side * inner, 8)
+                out[target][pl.ds(row, inner), :] = refs_of[source][pl.ds(from_row + i * inner, inner), :]
+
+
+def gather_step(plan, step, sides, own, got, after):
+    shapes = bundle_shapes(plan, step + 1, own[0].shape[1])
     return kernel_call(
-        functools.partial(stack_kernel, count),
-        out_shape=near_shape((2 * count, width)),
-        in_specs=specs(pltpu.SMEM, pltpu.VMEM, pltpu.VMEM),
-        out_specs=specs(pltpu.VMEM)[0],
+        functools.partial(gather_kernel, plan, step),
+        out_shape=shapes,
+        in_specs=specs(pltpu.SMEM, *[pltpu.VMEM] * (2 * len(own)), *[pl.ANY] * len(after)),
+        out_specs=tuple(specs(*[pltpu.VMEM] * len(shapes))),
         cost_estimate=LIGHT,
-    )(jnp.reshape(side, (1,)).astype(jnp.int32), *near(own, got))
+    )(sides, *near(*own, *got), *after)
 
 
 def gram_kernel(replicas, *refs):
@@ -318,8 +360,8 @@
     return unit, diagonal
 
 
-def first_kernel(replicas, packed_ref, basis_ref, *refs):
-    whole_ref, right_ref, left_ref = refs[-3:]
+def first_kernel(plan, replicas, packed_ref, basis_ref, *refs):
+    whole_ref, right_ref = refs[len(plan) : len(plan) + 2]
     blocks = basis_ref.shape[0] // BLOCK
     place = 0
     for a in range(blocks):
@@ -334,22 +376,22 @@
     unit, diagonal = factor(contract(basis, plain, (0, 0)))
     right = contract(plain, unit * lax.rsqrt(diagonal), (1, 1))
     right_ref[...] = right
-    rows = jnp.concatenate([ref[...] for ref in refs[:-3]], 0) / replicas
-    left_ref[...] = contract(rows, right, (1, 0))
-
-
-def first_pass(packed, basis, parts, replicas):
+    _, groups, _ = bundles(plan, 0)
+    for group, left_ref in zip(groups, refs[len(plan) + 2 :]):
+        rows = jnp.concatenate([refs[s][...] for s in group], 0) / replicas
+        left_ref[...] = contract(rows, right, (1, 0))
+
+
+def first_pass(plan, packed, basis, parts, replicas):
     width, rank = basis.shape
-    return kernel_call(
-        functools.partial(first_kernel, replicas),
-        out_shape=(
-            near_shape((width, width)),
-            near_shape((width, rank)),
-            near_shape((sum(part.shape[0] for part in parts), rank)),
-        ),
+    shapes = (near_shape((width, width)), near_shape((width, rank)), *bundle_shapes(plan, 0, rank))
+    whole, right, *lefts = kernel_call(
+        functools.partial(first_kernel, plan, replicas),
+        out_shape=shapes,
         in_specs=specs(*[pltpu.VMEM] * (2 + len(parts))),
-        out_specs=tuple(specs(*[pltpu.VMEM] * 3)),
+        out_specs=tuple(specs(*[pltpu.VMEM] * len(shapes))),
     )(*near(packed, basis, *parts))
+    return whole, right, lefts
 
 
 def product_kernel(whole_ref, right_ref, plain_ref, gram_ref):
@@ -383,147 +425,166 @@
 def low_rank(left, high, low):
     left_high, left_low = split(left)
     dot = functools.partial(jnp.dot, preferred_element_type=jnp.float32)
-    return dot(left_high, high) + (dot(left_high, low) + dot(left_low, high))
-
-
-def error_pieces(counts):
+    both = jnp.concatenate([left_high, left_low], 1)
+    return dot(both, jnp.concatenate([high, high], 0)) + dot(left_high, low)
+
+
+def error_pieces(plan, replicas):
     pieces, base = [], 0
-    for index, count in enumerate(counts):
-        pieces += [(index, place, base + place, size) for place, size in pieces_of(count, 3 * BLOCK)]
+    for s, stream in enumerate(plan):
+        count = stream.width * replicas // 2
+        pieces += [(s, place, base + place, size) for place, size in pieces_of(count, 4 * BLOCK)]
         base += count
     return pieces
 
 
-def fetch_merged(counts, refs, held_ref, sems):
-    copies = []
-    for number, (index, place, spot, size) in enumerate(error_pieces(counts)):
-        copies.append(
+def write_errors(plan, replicas, starts_ref, high, low, merged, lefts, out_ref, held_ref, sems, meanwhile=None):
+    pieces = error_pieces(plan, replicas)
+    _, _, where = bundles(plan, bit_count(replicas) - 1)
+    fetched = []
+    for number, (s, place, spot, size) in enumerate(pieces):
+        fetched.append(
             pltpu.make_async_copy(
-                refs[index].at[pl.ds(place, size), :], held_ref.at[pl.ds(spot, size), :], sems.at[0, number]
+                merged[s].at[pl.ds(place, size), :], held_ref.at[pl.ds(spot, size), :], sems.at[0, number]
             )
         )
-        copies[-1].start()
-    return copies
-
-
-def write_errors(counts, fetched, starts_ref, high, low, lefts, out_ref, held_ref, sems):
-    copies = []
-    for number, (index, place, spot, size) in enumerate(error_pieces(counts)):
-        there = pl.ds(pl.multiple_of(starts_ref[index] + place, BLOCK), size)
+        fetched[-1].start()
+    if meanwhile:
+        meanwhile()
+    written = []
+    for number, (s, place, spot, size) in enumerate(pieces):
+        index, first = where[s]
+        there = pl.ds(pl.multiple_of(starts_ref[s] + place, BLOCK), size)
         here = pl.ds(spot, size)
-        change = low_rank(lefts[index][pl.ds(place, size), :], high, low)
+        change = low_rank(lefts[index][pl.ds(first + place, size), :], high, low)
         fetched[number].wait()
         held_ref[here, :] = held_ref[here, :] - change
-        copies.append(
+        written.append(
             pltpu.make_async_copy(held_ref.at[here, :], out_ref.at[there, :], sems.at[1, number])
         )
-        copies[-1].start()
-    for copy in copies:
+        written[-1].start()
+    for copy in written:
         copy.wait()
 
 
-def error_kernel(counts, starts_ref, high_ref, low_ref, *refs):
-    n = len(counts)
-    out_ref, held_ref, sems = refs[-3:]
-    fetched = fetch_merged(counts, refs[:n], held_ref, sems)
-    high, low = high_ref[...], low_ref[...]
-    write_errors(counts, fetched, starts_ref, high, low, refs[n : 2 * n], out_ref, held_ref, sems)
-
-
-def last_error_kernel(counts, all_counts, starts_ref, high_ref, low_ref, *refs):
-    n, total = len(counts), len(all_counts)
-    lefts = refs[n : n + total]
-    weights_ref, momentum_ref = refs[n + total : n + total + 2]
+def error_kernel(plan, replicas, starts_ref, high_ref, low_ref, *refs):
+    n = len(plan)
+    write_errors(
+        plan, replicas, starts_ref, high_ref[...], low_ref[...], refs[:n], refs[n:-3], *refs[-3:]
+    )
+
+
+def last_error_kernel(plan, replicas, starts_ref, high_ref, low_ref, *refs):
+    n = len(plan)
+    _, groups, where = bundles(plan, bit_count(replicas) - 1)
+    m = len(groups)
+    merged, others, lefts = refs[:n], refs[n : n + m], refs[n + m : n + 2 * m]
+    weights_ref, momentum_ref = refs[n + 2 * m : n + 2 * m + 2]
     out_ref, weights_out, momentum_out, held_ref, left_ref, sems = refs[-6:]
-    fetched = fetch_merged(counts, refs[:n], held_ref, sems)
     high, low = high_ref[...], low_ref[...]
     rows = left_ref.shape[0]
     size = min(BLOCK, rows)
-    for place in range(0, rows, size):
-        want = starts_ref[len(all_counts)] + place
-        for index, count in enumerate(all_counts):
-            skip = want - starts_ref[index]
-
-            @pl.when((skip >= 0) & (skip < count))
-            def _(index=index, skip=skip, place=place):
-                left_ref[place : place + size, :] = lefts[index][pl.ds(pl.multiple_of(skip, 8), size), :]
-
-    own_rows = low_rank(left_ref[...], high, low)
-    momentum = momentum_rate * momentum_ref[...] + own_rows
-    momentum_out[...] = momentum
-    weights_out[...] = weights_ref[...] - outer_rate * (own_rows + momentum_rate * momentum)
-    write_errors(counts, fetched, starts_ref, high, low, lefts, out_ref, held_ref, sems)
-
-
-def error_scratch(counts, width):
-    cuts = len(error_pieces(counts))
-    return pltpu.VMEM((sum(counts), width), jnp.float32), pltpu.SemaphoreType.DMA((2, cuts))
-
-
-def error_cost(counts, width, rank):
-    return pl.CostEstimate(
-        flops=6 * sum(counts) * width * rank, bytes_accessed=8 * sum(counts) * width, transcendentals=0
-    )
-
-
-def error_rows(starts, merged, lefts, high, low, shape):
-    counts = [left.shape[0] for left in lefts]
-    n = len(counts)
+
+    def outer():
+        for place in range(0, rows, size):
+            want = starts_ref[2 * n] + place
+            for k, bundle in ((0, others), (n, lefts)):
+                for s, stream in enumerate(plan):
+                    index, first = where[s]
+                    skip = want - starts_ref[k + s]
+
+                    @pl.when((skip >= 0) & (skip < stream.width * replicas // 2))
+                    def _(bundle=bundle, index=index, first=first, skip=skip, place=place):
+                        row = pl.multiple_of(first + skip, 8)
+                        left_ref[place : place + size, :] = bundle[index][pl.ds(row, size), :]
+
+        own_rows = low_rank(left_ref[...], high, low)
+        momentum = momentum_rate * momentum_ref[...] + own_rows
+        momentum_out[...] = momentum
+        weights_out[...] = weights_ref[...] - outer_rate * (own_rows + momentum_rate * momentum)
+
+    write_errors(plan, replicas, starts_ref, high, low, merged, others, out_ref, held_ref, sems, outer)
+
+
+def error_options(plan, replicas, width, rank):
+    pieces = error_pieces(plan, replicas)
+    rows = sum(piece[3] for piece in pieces)
+    scratch = pltpu.VMEM((rows, width), jnp.float32), pltpu.SemaphoreType.DMA((2, len(pieces)))
+    cost = pl.CostEstimate(
+        flops=6 * rows * width * rank, bytes_accessed=8 * rows * width, transcendentals=0
+    )
+    return scratch, cost
+
+
+def error_rows(plan, replicas, starts, merged, lefts, high, low, shape):
+    scratch, cost = error_options(plan, replicas, shape[1], high.shape[0])
     return kernel_call(
-        functools.partial(error_kernel, counts),
+        functools.partial(error_kernel, plan, replicas),
         out_shape=jax.ShapeDtypeStruct(shape, jnp.float32),
-        in_specs=specs(pltpu.SMEM, pltpu.VMEM, pltpu.VMEM, *[pltpu.HBM] * n, *[pltpu.VMEM] * n),
+        in_specs=specs(
+            pltpu.SMEM, *[pltpu.VMEM] * 2, *[pltpu.HBM] * len(merged), *[pltpu.VMEM] * len(lefts)
+        ),
         out_specs=specs(pltpu.HBM)[0],
-        scratch_shapes=error_scratch(counts, shape[1]),
-        cost_estimate=error_cost(counts, shape[1], high.shape[0]),
+        scratch_shapes=scratch,
+        cost_estimate=cost,
     )(jnp.stack(starts).astype(jnp.int32), *near(high, low), *map(distant, merged), *near(*lefts))
 
 
-def last_rows(kept, starts, merged, lefts, other_starts, other_lefts, high, low, weights, momentum):
+def last_rows(plan, replicas, kept, starts, merged, others, lefts, high, low, weights, momentum):
     rows, width = weights.shape
-    counts = [left.shape[0] for left in lefts]
-    all_counts = counts + [left.shape[0] for left in other_lefts]
-    own = lax.axis_index("rep") * rows
+    (held, sems), cost = error_options(plan, replicas, width, high.shape[0])
     arrays = [
-        jnp.stack([*starts, *other_starts, own]).astype(jnp.int32),
+        jnp.stack([*starts, lax.axis_index("rep") * rows]).astype(jnp.int32),
         *near(high, low),
         *map(distant, merged),
-        *near(*lefts, *other_lefts),
+        *near(*others, *lefts),
         weights,
         momentum,
         kept,
     ]
     result = jax.ShapeDtypeStruct(weights.shape, jnp.float32)
-    held, sems = error_scratch(counts, width)
     return kernel_call(
-        functools.partial(last_error_kernel, counts, all_counts),
+        functools.partial(last_error_kernel, plan, replicas),
         out_shape=(jax.ShapeDtypeStruct(kept.shape, jnp.float32), result, result),
         in_specs=specs(
             pltpu.SMEM,
-            pltpu.VMEM,
-            pltpu.VMEM,
-            *[pltpu.HBM] * len(counts),
-            *[pltpu.VMEM] * (len(all_counts) + 2),
+            *[pltpu.VMEM] * 2,
+            *[pltpu.HBM] * len(merged),
+            *[pltpu.VMEM] * (2 * len(lefts) + 2),
             pltpu.HBM,
         ),
         out_specs=tuple(specs(pltpu.HBM, pltpu.VMEM, pltpu.VMEM)),
         scratch_shapes=[held, pltpu.VMEM((rows, high.shape[0]), jnp.float32), sems],
         input_output_aliases={len(arrays) - 1: 0},
-        cost_estimate=error_cost(counts, width, high.shape[0]),
+        cost_estimate=cost,
     )(*arrays)
+
+
+@dataclasses.dataclass(frozen=True)
+class Stream:
+    width: int
+    order: tuple
+    back: tuple
 
 
 def stream_plan(replicas, rows_each):
     bits = bit_count(replicas)
     grain = max(8, 2 * BLOCK // replicas)
     units = rows_each // grain
+    if bits == 4 and units % 16 == 0:
+        shares = SHARES
+        plan = [
+            Stream(share * units // 16 * grain, order, BACK[order[0]])
+            for share, order in shares
+        ]
+        return plan, TURNS
     streams = max(1, min(3, units, bits - 1))
-    widths = [units // streams + (1 if streams - 1 - s < units % streams else 0) for s in range(streams)]
+    widths = [units // streams + (1 if s < units % streams else 0) for s in range(streams)]
     lead = list(range(min(3, bits)))
     rest = list(range(len(lead), bits))
-    return [
-        (w * grain, lead[s % len(lead) :] + lead[: s % len(lead)] + rest) for s, w in enumerate(widths)
-    ]
+    orders = [tuple(lead[s % len(lead) :] + lead[: s % len(lead)] + rest) for s in range(streams)]
+    plan = [Stream(w * grain, order, order[::-1]) for w, order in zip(widths, orders)]
+    return plan, range(streams)
 
 
 def on_device(tokens_in, norm_gain, key_grad, error_in, basis_init, weights_in, momentum_in):
@@ -537,58 +598,43 @@
         depth * lax.axis_size("mp"), tokens_in, square_sums, norm_gain[None, :], key_grad, error
     )
 
-    plan = stream_plan(replicas, depth // replicas)
-    halves, places, place = [], [], 0
-    for width, order in plan:
-        half = width * replicas // 2
-        side = bit_of("rep", order[0])
+    plan, turns = stream_plan(replicas, depth // replicas)
+    halves, here, there, place = [], [], [], 0
+    for stream in plan:
+        half = stream.width * replicas // 2
+        side = bit_of("rep", stream.order[0])
         halves.append(half)
-        places.append((place + side * half, place + (1 - side) * half))
+        here.append(place + side * half)
+        there.append(place + (1 - side) * half)
         place += 2 * half
-    streams = range(len(plan))
-    order = [order for _, order in plan]
-    far, got = [None] * len(plan), [None] * len(plan)
-    turns = [len(plan) - 1, *range(len(plan) - 1)]
-    for s in turns:
-        far[s] = merge(places[s][1], halves[s], *sources)
-        got[s] = flip(far[s], "rep", 1 << order[s][0])
-    own = [merge(places[s][0], halves[s], *sources) for s in streams]
-    parts, after = list(own), [*own, basis]
+    far = merge(there, halves, turns, *sources)
+    got = [flip(part, "rep", 1 << stream.order[0]) for part, stream in zip(far, plan)]
+    own = merge(here, halves, turns, *sources)
+    parts, after = list(own), [basis]
     for step in range(steps):
-        for s in streams:
+        for s in turns:
             if step + 1 < steps:
-                side = bit_of("rep", order[s][step + 1])
-                parts[s], send = join(parts[s], got[s], side, after)
-                got[s] = flip(send, "rep", 1 << order[s][step + 1])
+                bit = plan[s].order[step + 1]
+                parts[s], send = join(parts[s], got[s], bit_of("rep", bit), after)
+                got[s] = flip(send, "rep", 1 << bit)
             else:
                 (parts[s],) = join(parts[s], got[s], None, after)
-            after = [parts[s]]
+        after = []
 
     packed = sum_everywhere(gram(parts, replicas))
-    whole, right, left = first_pass(packed, basis, parts, replicas)
+    whole, right, lefts = first_pass(plan, packed, basis, parts, replicas)
     high, low = second_pass(whole, right)
 
-    lefts, place = [], 0
-    for width, _ in plan:
-        lefts.append(left[place : place + width])
-        place += width
-    for step in reversed(range(steps)):
-        others = [None] * len(plan)
-        for bit in range(steps):
-            alike = [s for s in streams if order[s][step] == bit]
-            if alike:
-                came = flip(jnp.concatenate([lefts[s] for s in alike], 0), "rep", 1 << bit)
-                place = 0
-                for s in alike:
-                    others[s] = came[place : place + lefts[s].shape[0]]
-                    place += lefts[s].shape[0]
-        if step:
-            lefts = [stack(lefts[s], others[s], bit_of("rep", order[s][step])) for s in streams]
-
-    here, there = [p[0] for p in places], [p[1] for p in places]
-    error_out = error_rows(here, own, lefts, high, low, error.shape)
+    bit_sides = jnp.stack([bit_of("rep", bit) for bit in range(steps)]).astype(jnp.int32)
+    for step in range(steps):
+        bits, _, _ = bundles(plan, step)
+        others = [flip(left, "rep", 1 << bit) for left, bit in zip(lefts, bits)]
+        if step + 1 < steps:
+            lefts = gather_step(plan, step, bit_sides, lefts, others, [high])
+
+    error_out = error_rows(plan, replicas, here, own, lefts, high, low, error.shape)
     error_out, weights_out, momentum_out = last_rows(
-        error_out, there, far, others, here, lefts, high, low, weights_in[0], momentum_in[0]
+        plan, replicas, error_out, there + here, far, others, lefts, high, low, weights_in[0], momentum_in[0]
     )
     return (error_out[None], weights_out[None], momentum_out[None])
 

time: 188 us -> 176 us (0.936)
  Pallas kernels: 49.3 us -> 38.9 us
  waiting for transfers between devices: 93.5 us -> 91.3 us
    pallas_call x18 -> x8, Pallas kernels: 34.6 us -> 28.6 us  [the longest x2 8.86 us: merge(): kernel_call(functools.partial(merge_kernel, in_turn, depth), out_shape=tu...]
    pallas_call x12, Pallas kernels: 5.59 us -> 0.94 us  [join(): kernel_call(kernel, out_shape=shapes, in_specs=specs(*places, *[pl.ANY] *...]
    ppermute x34, waiting for transfers between devices: 93.5 us -> 91.3 us  [flip(): return lax.ppermute(value, axis, [(i, i ^ mask) for i in range(size)])]
  transfers between devices with their start and end apart: 34 -> 34, of which waited for: 26 -> 23; matrix products, arithmetic and copies ran while one was open for 0% -> 0% of each run, Pallas kernels for 15% -> 9%
where the time goes in v2:
time: 176 us
  waiting for transfers between devices  91.3 us (52%)
  starting transfers between devices  41.1 us (23%)
  Pallas kernels  38.9 us (22%)
  blocking collectives  2.16 us (1%)
    ppermute x34, waiting for transfers between devices, flip(): return lax.ppermute(value, axis, [(i, i ^ mask) for i in range(size)])  91.3 us
    ppermute x34, starting transfers between devices, flip(): return lax.ppermute(value, axis, [(i, i ^ mask) for i in range(size)])  41.1 us
    pallas_call x2, Pallas kernels, merge(): kernel_call(functools.partial(merge_kernel, in_turn, depth), out_shape=tu...  8.86 us
    pallas_call x1, Pallas kernels, first_pass(): kernel_call(functools.partial(first_kernel, plan, replicas), out_shape=sh...  7.78 us
    pallas_call x1, Pallas kernels, last_rows(): kernel_call(functools.partial(last_error_kernel, plan, replicas), out_sha...  5.56 us
    pallas_call x1, Pallas kernels, second_pass(): pair(weight_kernel, out_shape=(half, half))(*near(plain, gram_matrix))  4.81 us
    pallas_call x1, Pallas kernels, error_rows(): kernel_call(functools.partial(error_kernel, plan, replicas), out_shape=ja...  4.6 us
  transfers between devices with their start and end apart: 34, of which 23 were waited for; matrix products, arithmetic and copies ran while one was open for 0% of the time, Pallas kernels for 9%

profile of v2, /device:TPU:0, one launch (start us, length us, event | category | flops | bytes accessed | tf_op | source)
XLA Modules:
  0.0 176.3 jit_solution(6134194155498843026)
XLA Ops:
  0.7 1.8 %shard_map.94 = f32[256,128]{1,0:T(8,128)S(1)} custom-call(bf16[256,4096]{1,0:T(8,128)(2,1)} %tokens_ref.5), custom_call_target="tpu_custom_call" | custom-call | tf_op jit(solution)/shard_map/pallas_call | solution.py:160
  4.0 4.4 %shard_map.96 = (f32[640,512]{1,0:T(8,128)S(1)}, f32[640,512]{1,0:T(8,128)S(1)}, f32[768,512]{1,0:T(8,128)S(1)}) custom-call(s32[3]{0:T(128)S(1)} %get-tuple-element.95.starts_ref, bf16[256,4096]{1,0:T(8,128)(2,1)} %tokens_ref.5, f32[256,128]{1,0:T(8,128)S(1)} %add.63.squares_ref, bf16[1,4096]{1,0:T(2,128)(2,1)S(1)} %broadcast_in_dim.16.gain_ref, ...), custom_call_target="tpu_custom_call" | custom-call | flops 536870912 | bytes 9437184 | tf_op jit(solution)/shard_map/pallas_call | solution.py:206
  8.5 3.0 %collective-permute-start.9 = (f32[768,512]{1,0:T(8,128)S(1)}, f32[768,512]{1,0:T(8,128)S(1)}, u32[]{:S(2)}, u32[]{:S(2)}) collective-permute-start(f32[768,512]{1,0:T(8,128)S(1)} %get-tuple-element.63.refs_2_), channel_id=1, source_target_pairs={{0,8},{2,10},{4,12},{6,14},{8,0},{10,2},{12,4},{14,6},{16,24},{18,... | collective-permute-start | bytes 4718600 | tf_op jit(solution)/shard_map/ppermute | solution.py:39
  14.5 2.2 %all_gather.3.refs_0_.basis_ref = f32[512,128]{1,0:T(8,128)S(1)} all-gather(f32[256,128]{1,0:T(8,128)S(1)} %copy-done.9), channel_id=1, replica_groups=mesh['rep'=16,'mp'=2] {'mp'}, dimensions={0}, use_global_device_ids=true | all-gather | bytes 393216 | tf_op jit(solution)/shard_map/all_gather | solution.py:596
  16.6 4.4 %shard_map.95 = (f32[640,512]{1,0:T(8,128)S(1)}, f32[640,512]{1,0:T(8,128)S(1)}, f32[768,512]{1,0:T(8,128)S(1)}) custom-call(s32[3]{0:T(128)S(1)} %get-tuple-element.94.starts_ref, bf16[256,4096]{1,0:T(8,128)(2,1)} %tokens_ref.5, f32[256,128]{1,0:T(8,128)S(1)} %add.63.squares_ref, bf16[1,4096]{1,0:T(2,128)(2,1)S(1)} %broadcast_in_dim.16.gain_ref, ...), custom_call_target="tpu_custom_call" | custom-call | flops 536870912 | bytes 9437184 | tf_op jit(solution)/shard_map/pallas_call | solution.py:206
  21.1 25.0 %collective-permute-done.9.got_ref = f32[768,512]{1,0:T(8,128)S(1)} collective-permute-done((f32[768,512]{1,0:T(8,128)S(1)}, f32[768,512]{1,0:T(8,128)S(1)}, u32[]{:S(2)}, u32[]{:S(2)}) %collective-permute-start.9) | collective-permute-done | bytes 1572896 | tf_op jit(solution)/shard_map/ppermute | solution.py:39
  46.4 1.7 collective-permute-start.10
  52.8 12.8 %collective-permute-done.10.got_ref = f32[384,512]{1,0:T(8,128)S(1)} collective-permute-done((f32[384,512]{1,0:T(8,128)S(1)}, f32[384,512]{1,0:T(8,128)S(1)}, u32[]{:S(2)}, u32[]{:S(2)}) %collective-permute-start.10) | collective-permute-done | bytes 786464 | tf_op jit(solution)/shard_map/ppermute | solution.py:39
  70.4 5.0 %collective-permute-done.11.got_ref = f32[192,512]{1,0:T(8,128)S(1)} collective-permute-done((f32[192,512]{1,0:T(8,128)S(1)}, f32[192,512]{1,0:T(8,128)S(1)}, u32[]{:S(2)}, u32[]{:S(2)}) %collective-permute-start.11) | collective-permute-done | bytes 393248 | tf_op jit(solution)/shard_map/ppermute | solution.py:39
  75.5 2.3 %collective-permute-start.12 = (f32[96,512]{1,0:T(8,128)S(1)}, f32[96,512]{1,0:T(8,128)S(1)}, u32[]{:S(2)}, u32[]{:S(2)}) collective-permute-start(f32[96,512]{1,0:T(8,128)S(1)} %get-tuple-element.69), channel_id=1, source_target_pairs={{0,16},{2,18},{4,20},{6,22},{8,24},{10,26},{12,28},{14,30},{16,0},... | collective-permute-start | bytes 589832 | tf_op jit(solution)/shard_map/ppermute | solution.py:39
  78.6 2.3 %collective-permute-start.4 = (f32[80,512]{1,0:T(8,128)S(1)}, f32[80,512]{1,0:T(8,128)S(1)}, u32[]{:S(2)}, u32[]{:S(2)}) collective-permute-start(f32[80,512]{1,0:T(8,128)S(1)} %get-tuple-element.53), channel_id=1, source_target_pairs={{0,16},{2,18},{4,20},{6,22},{8,24},{10,26},{12,28},{14,30},{16,0},... | collective-permute-start | bytes 491528 | tf_op jit(solution)/shard_map/ppermute | solution.py:39
  80.9 16.5 %collective-permute-done.8.got_ref = f32[80,512]{1,0:T(8,128)S(1)} collective-permute-done((f32[80,512]{1,0:T(8,128)S(1)}, f32[80,512]{1,0:T(8,128)S(1)}, u32[]{:S(2)}, u32[]{:S(2)}) %collective-permute-start.8) | collective-permute-done | bytes 163872 | tf_op jit(solution)/shard_map/ppermute | solution.py:39
  97.5 1.9 %collective-permute-done.4.got_ref = f32[80,512]{1,0:T(8,128)S(1)} collective-permute-done((f32[80,512]{1,0:T(8,128)S(1)}, f32[80,512]{1,0:T(8,128)S(1)}, u32[]{:S(2)}, u32[]{:S(2)}) %collective-permute-start.4) | collective-permute-done | bytes 163872 | tf_op jit(solution)/shard_map/ppermute | solution.py:39
  110.0 3.5 %collective-permute-start.19 = (f32[160,128]{1,0:T(8,128)S(1)}, f32[160,128]{1,0:T(8,128)S(1)}, u32[]{:S(2)}, u32[]{:S(2)}) collective-permute-start(f32[160,128]{1,0:T(8,128)S(1)} %add_add_fusion.1), channel_id=1, source_target_pairs={{0,24},{2,26},{4,28},{6,30},{8,16},{10,18},{12,20},{14,22},{16,8},... | collective-permute-start | bytes 245768 | tf_op jit(solution)/shard_map/ppermute | solution.py:39
  114.5 2.3 %collective-permute-done.19 = f32[160,128]{1,0:T(8,128)S(1)} collective-permute-done((f32[160,128]{1,0:T(8,128)S(1)}, f32[160,128]{1,0:T(8,128)S(1)}, u32[]{:S(2)}, u32[]{:S(2)}) %collective-permute-start.19) | collective-permute-done | bytes 81952 | tf_op jit(solution)/shard_map/ppermute | solution.py:39
  116.7 3.1 %collective-permute-done.18 = f32[160,128]{1,0:T(8,128)S(1)} collective-permute-done((f32[160,128]{1,0:T(8,128)S(1)}, f32[160,128]{1,0:T(8,128)S(1)}, u32[]{:S(2)}, u32[]{:S(2)}) %collective-permute-start.18) | collective-permute-done | bytes 81952 | tf_op jit(solution)/shard_map/ppermute | solution.py:39
  124.5 2.0 %collective-permute-done.21 = f32[160,128]{1,0:T(8,128)S(1)} collective-permute-done((f32[160,128]{1,0:T(8,128)S(1)}, f32[160,128]{1,0:T(8,128)S(1)}, u32[]{:S(2)}, u32[]{:S(2)}) %collective-permute-start.21) | collective-permute-done | bytes 81952 | tf_op jit(solution)/shard_map/ppermute | solution.py:39
  129.1 7.8 %shard_map.110 = (f32[512,512]{1,0:T(8,128)S(1)}, f32[512,128]{1,0:T(8,128)S(1)}, f32[256,128]{1,0:T(8,128)S(1)}) custom-call(f32[1280,128]{1,0:T(8,128)S(1)} %constant_dynamic-update-slice_fusion.packed_ref, f32[512,128]{1,0:T(8,128)S(1)} %all_gather.3.refs_0_.basis_ref, f32[80,512]{1,0:T(8,128)S(1)} %shard_map.100.refs_0_, ...), custom_call_target="tpu_custom_call" | custom-call | tf_op jit(solution)/shard_map/pallas_call | solution.py:388
  138.1 1.9 %shard_map.111 = (f32[512,128]{1,0:T(8,128)S(1)}, f32[128,128]{1,0:T(8,128)S(1)}) custom-call(f32[512,512]{1,0:T(8,128)S(1)} %get-tuple-element.70.whole_ref, f32[512,128]{1,0:T(8,128)S(1)} %get-tuple-element.71.right_ref), custom_call_target="tpu_custom_call" | custom-call | tf_op jit(solution)/shard_map/pallas_call | solution.py:418
  140.0 4.8 %shard_map.112 = (bf16[128,512]{1,0:T(8,128)(2,1)S(1)}, bf16[128,512]{1,0:T(8,128)(2,1)S(1)}) custom-call(f32[512,128]{1,0:T(8,128)S(1)} %get-tuple-element.72.plain_ref, f32[128,128]{1,0:T(8,128)S(1)} %get-tuple-element.73.gram_ref), custom_call_target="tpu_custom_call" | custom-call | tf_op jit(solution)/shard_map/pallas_call | solution.py:422
  149.0 3.6 %collective-permute-done.25.refs_3_ = f32[160,128]{1,0:T(8,128)S(1)} collective-permute-done((f32[160,128]{1,0:T(8,128)S(1)}, f32[160,128]{1,0:T(8,128)S(1)}, u32[]{:S(2)}, u32[]{:S(2)}) %collective-permute-start.25) | collective-permute-done | bytes 81952 | tf_op jit(solution)/shard_map/ppermute | solution.py:39
  156.3 4.3 %collective-permute-done.29.refs_4_ = f32[320,128]{1,0:T(8,128)S(1)} collective-permute-done((f32[320,128]{1,0:T(8,128)S(1)}, f32[320,128]{1,0:T(8,128)S(1)}, u32[]{:S(2)}, u32[]{:S(2)}) %collective-permute-start.29) | collective-permute-done | bytes 163872 | tf_op jit(solution)/shard_map/ppermute | solution.py:39
  164.3 4.6 %shard_map.116.refs_11_ = f32[4096,512]{1,0:T(8,128)} custom-call(s32[3]{0:T(128)S(1)} %get-tuple-element.94.starts_ref, bf16[128,512]{1,0:T(8,128)(2,1)S(1)} %get-tuple-element.74.refs_2_.refs_6_.high_ref, bf16[128,512]{1,0:T(8,128)(2,1)S(1)} %get-tuple-element.75.low_ref, f32[640,512]{1,0:T(8,128)} %copy-done.1, f32[640,512]{1,0:T(8,128)} %copy-done.2, ...), custom_call_target="tpu_custom_call" | custom-call | flops 805306368 | bytes 8388608 | tf_op jit(solution)/shard_map/pallas_call | solution.py:521
  170.6 5.6 %shard_map.117 = (f32[4096,512]{1,0:T(8,128)}, f32[256,512]{1,0:T(8,128)}, f32[256,512]{1,0:T(8,128)}) custom-call(s32[7]{0:T(128)S(1)} %stack.54.starts_ref, bf16[128,512]{1,0:T(8,128)(2,1)S(1)} %get-tuple-element.74.refs_2_.refs_6_.high_ref, bf16[128,512]{1,0:T(8,128)(2,1)S(1)} %get-tuple-element.75.low_ref, ...), custom_call_target="tpu_custom_call", output_to_operand_aliasing={{0}: (14, {})} | custom-call | flops 805306368 | bytes 8388608 | tf_op jit(solution)/shard_map/pallas_call | solution.py:546
  (107 shorter events, 48.4 us)
Async XLA Ops:
  8.5 37.7 %collective-permute-start.9 = (f32[768,512]{1,0:T(8,128)S(1)}, f32[768,512]{1,0:T(8,128)S(1)}, u32[]{:S(2)}, u32[]{:S(2)}) collective-permute-start(f32[768,512]{1,0:T(8,128)S(1)} %get-tuple-element.63.refs_2_), channel_id=1, source_target_pairs={{0,8},{2,10},{4,12},{6,14},{8,0},{10,2},{12,4},{14,6},{16,24},{18,... | collective-permute-start | bytes 4718600 | tf_op jit(solution)/shard_map/ppermute | solution.py:39
  11.5 36.7 %collective-permute-start.5 = (f32[640,512]{1,0:T(8,128)S(1)}, f32[640,512]{1,0:T(8,128)S(1)}, u32[]{:S(2)}, u32[]{:S(2)}) collective-permute-start(f32[640,512]{1,0:T(8,128)S(1)} %get-tuple-element.55.refs_1_), channel_id=1, source_target_pairs={{0,4},{2,6},{4,0},{6,2},{8,12},{10,14},{12,8},{14,10},{16,20},{18,... | collective-permute-start | bytes 3932168 | tf_op jit(solution)/shard_map/ppermute | solution.py:39
  13.0 38.0 %collective-permute-start.1 = (f32[640,512]{1,0:T(8,128)S(1)}, f32[640,512]{1,0:T(8,128)S(1)}, u32[]{:S(2)}, u32[]{:S(2)}) collective-permute-start(f32[640,512]{1,0:T(8,128)S(1)} %get-tuple-element.47.refs_0_), channel_id=1, source_target_pairs={{0,2},{2,0},{4,6},{6,4},{8,10},{10,8},{12,14},{14,12},{16,18},{18,... | collective-permute-start | bytes 3932168 | tf_op jit(solution)/shard_map/ppermute | solution.py:39
  46.4 19.1 %collective-permute-start.10 = (f32[384,512]{1,0:T(8,128)S(1)}, f32[384,512]{1,0:T(8,128)S(1)}, u32[]{:S(2)}, u32[]{:S(2)}) collective-permute-start(f32[384,512]{1,0:T(8,128)S(1)} %get-tuple-element.65), channel_id=1, source_target_pairs={{0,2},{2,0},{4,6},{6,4},{8,10},{10,8},{12,14},{14,12},{16,18},{18,... | collective-permute-start | bytes 2359304 | tf_op jit(solution)/shard_map/ppermute | solution.py:39
  49.4 17.7 %collective-permute-start.6 = (f32[320,512]{1,0:T(8,128)S(1)}, f32[320,512]{1,0:T(8,128)S(1)}, u32[]{:S(2)}, u32[]{:S(2)}) collective-permute-start(f32[320,512]{1,0:T(8,128)S(1)} %get-tuple-element.57), channel_id=1, source_target_pairs={{0,8},{2,10},{4,12},{6,14},{8,0},{10,2},{12,4},{14,6},{16,24},{18,... | collective-permute-start | bytes 1966088 | tf_op jit(solution)/shard_map/ppermute | solution.py:39
  51.2 17.5 %collective-permute-start.2 = (f32[320,512]{1,0:T(8,128)S(1)}, f32[320,512]{1,0:T(8,128)S(1)}, u32[]{:S(2)}, u32[]{:S(2)}) collective-permute-start(f32[320,512]{1,0:T(8,128)S(1)} %get-tuple-element.49), channel_id=1, source_target_pairs={{0,4},{2,6},{4,0},{6,2},{8,12},{10,14},{12,8},{14,10},{16,20},{18,... | collective-permute-start | bytes 1966088 | tf_op jit(solution)/shard_map/ppermute | solution.py:39
  65.6 9.8 %collective-permute-start.11 = (f32[192,512]{1,0:T(8,128)S(1)}, f32[192,512]{1,0:T(8,128)S(1)}, u32[]{:S(2)}, u32[]{:S(2)}) collective-permute-start(f32[192,512]{1,0:T(8,128)S(1)} %get-tuple-element.67), channel_id=1, source_target_pairs={{0,4},{2,6},{4,0},{6,2},{8,12},{10,14},{12,8},{14,10},{16,20},{18,... | collective-permute-start | bytes 1179656 | tf_op jit(solution)/shard_map/ppermute | solution.py:39
  67.1 10.6 %collective-permute-start.7 = (f32[160,512]{1,0:T(8,128)S(1)}, f32[160,512]{1,0:T(8,128)S(1)}, u32[]{:S(2)}, u32[]{:S(2)}) collective-permute-start(f32[160,512]{1,0:T(8,128)S(1)} %get-tuple-element.59), channel_id=1, source_target_pairs={{0,2},{2,0},{4,6},{6,4},{8,10},{10,8},{12,14},{14,12},{16,18},{18,... | collective-permute-start | bytes 983048 | tf_op jit(solution)/shard_map/ppermute | solution.py:39
  68.8 9.8 %collective-permute-start.3 = (f32[160,512]{1,0:T(8,128)S(1)}, f32[160,512]{1,0:T(8,128)S(1)}, u32[]{:S(2)}, u32[]{:S(2)}) collective-permute-start(f32[160,512]{1,0:T(8,128)S(1)} %get-tuple-element.51), channel_id=1, source_target_pairs={{0,8},{2,10},{4,12},{6,14},{8,0},{10,2},{12,4},{14,6},{16,24},{18,... | collective-permute-start | bytes 983048 | tf_op jit(solution)/shard_map/ppermute | solution.py:39
  75.5 23.9 %collective-permute-start.12 = (f32[96,512]{1,0:T(8,128)S(1)}, f32[96,512]{1,0:T(8,128)S(1)}, u32[]{:S(2)}, u32[]{:S(2)}) collective-permute-start(f32[96,512]{1,0:T(8,128)S(1)} %get-tuple-element.69), channel_id=1, source_target_pairs={{0,16},{2,18},{4,20},{6,22},{8,24},{10,26},{12,28},{14,30},{16,0},... | collective-permute-start | bytes 589832 | tf_op jit(solution)/shard_map/ppermute | solution.py:39
  77.8 19.6 %collective-permute-start.8 = (f32[80,512]{1,0:T(8,128)S(1)}, f32[80,512]{1,0:T(8,128)S(1)}, u32[]{:S(2)}, u32[]{:S(2)}) collective-permute-start(f32[80,512]{1,0:T(8,128)S(1)} %get-tuple-element.61), channel_id=1, source_target_pairs={{0,16},{2,18},{4,20},{6,22},{8,24},{10,26},{12,28},{14,30},{16,0},... | collective-permute-start | bytes 491528 | tf_op jit(solution)/shard_map/ppermute | solution.py:39
  78.6 20.7 %collective-permute-start.4 = (f32[80,512]{1,0:T(8,128)S(1)}, f32[80,512]{1,0:T(8,128)S(1)}, u32[]{:S(2)}, u32[]{:S(2)}) collective-permute-start(f32[80,512]{1,0:T(8,128)S(1)} %get-tuple-element.53), channel_id=1, source_target_pairs={{0,16},{2,18},{4,20},{6,22},{8,24},{10,26},{12,28},{14,30},{16,0},... | collective-permute-start | bytes 491528 | tf_op jit(solution)/shard_map/ppermute | solution.py:39
  102.9 6.0 %collective-permute-start.16 = (f32[160,128]{1,0:T(8,128)S(1)}, f32[160,128]{1,0:T(8,128)S(1)}, u32[]{:S(2)}, u32[]{:S(2)}) collective-permute-start(f32[160,128]{1,0:T(8,128)S(1)} %get-tuple-element.92), channel_id=1, source_target_pairs={{0,6},{2,4},{4,2},{6,0},{8,14},{10,12},{12,10},{14,8},{16,22},{18,... | collective-permute-start | bytes 245768 | tf_op jit(solution)/shard_map/ppermute | solution.py:39
  104.6 5.4 %collective-permute-start.15 = (f32[160,128]{1,0:T(8,128)S(1)}, f32[160,128]{1,0:T(8,128)S(1)}, u32[]{:S(2)}, u32[]{:S(2)}) collective-permute-start(f32[160,128]{1,0:T(8,128)S(1)} %get-tuple-element.93), channel_id=1, source_target_pairs={{0,4},{2,6},{4,0},{6,2},{8,12},{10,14},{12,8},{14,10},{16,20},{18,... | collective-permute-start | bytes 245768 | tf_op jit(solution)/shard_map/ppermute | solution.py:39
  110.0 6.7 %collective-permute-start.19 = (f32[160,128]{1,0:T(8,128)S(1)}, f32[160,128]{1,0:T(8,128)S(1)}, u32[]{:S(2)}, u32[]{:S(2)}) collective-permute-start(f32[160,128]{1,0:T(8,128)S(1)} %add_add_fusion.1), channel_id=1, source_target_pairs={{0,24},{2,26},{4,28},{6,30},{8,16},{10,18},{12,20},{14,22},{16,8},... | collective-permute-start | bytes 245768 | tf_op jit(solution)/shard_map/ppermute | solution.py:39
  113.5 6.3 %collective-permute-start.18 = (f32[160,128]{1,0:T(8,128)S(1)}, f32[160,128]{1,0:T(8,128)S(1)}, u32[]{:S(2)}, u32[]{:S(2)}) collective-permute-start(f32[160,128]{1,0:T(8,128)S(1)} %add_add_fusion.1), channel_id=1, source_target_pairs={{0,16},{2,18},{4,20},{6,22},{8,24},{10,26},{12,28},{14,30},{16,0},... | collective-permute-start | bytes 245768 | tf_op jit(solution)/shard_map/ppermute | solution.py:39
  113.5 6.3 %collective-permute-start.17 = (f32[160,128]{1,0:T(8,128)S(1)}, f32[160,128]{1,0:T(8,128)S(1)}, u32[]{:S(2)}, u32[]{:S(2)}) collective-permute-start(f32[160,128]{1,0:T(8,128)S(1)} %add_add_fusion.1), channel_id=1, source_target_pairs={{0,8},{2,10},{4,12},{6,14},{8,0},{10,2},{12,4},{14,6},{16,24},{18,... | collective-permute-start | bytes 245768 | tf_op jit(solution)/shard_map/ppermute | solution.py:39
  122.0 5.4 %collective-permute-start.22 = (f32[160,128]{1,0:T(8,128)S(1)}, f32[160,128]{1,0:T(8,128)S(1)}, u32[]{:S(2)}, u32[]{:S(2)}) collective-permute-start(f32[160,128]{1,0:T(8,128)S(1)} %get-tuple-element.90), channel_id=1, source_target_pairs={{0,6},{2,4},{4,2},{6,0},{8,14},{10,12},{12,10},{14,8},{16,22},{18,... | collective-permute-start | bytes 245768 | tf_op jit(solution)/shard_map/ppermute | solution.py:39
  136.9 9.3 %collective-permute-start.24 = (f32[256,128]{1,0:T(8,128)S(1)}, f32[256,128]{1,0:T(8,128)S(1)}, u32[]{:S(2)}, u32[]{:S(2)}) collective-permute-start(f32[256,128]{1,0:T(8,128)S(1)} %get-tuple-element.76.refs_0_), channel_id=1, source_target_pairs={{0,16},{2,18},{4,20},{6,22},{8,24},{10,26},{12,28},{14,30},{16,0},... | collective-permute-start | bytes 393224 | tf_op jit(solution)/shard_map/ppermute | solution.py:39
  146.8 6.5 %collective-permute-start.26 = (f32[192,128]{1,0:T(8,128)S(1)}, f32[192,128]{1,0:T(8,128)S(1)}, u32[]{:S(2)}, u32[]{:S(2)}) collective-permute-start(f32[192,128]{1,0:T(8,128)S(1)} %get-tuple-element.78.refs_1_), channel_id=1, source_target_pairs={{0,4},{2,6},{4,0},{6,2},{8,12},{10,14},{12,8},{14,10},{16,20},{18,... | collective-permute-start | bytes 294920 | tf_op jit(solution)/shard_map/ppermute | solution.py:39
  153.9 7.5 %collective-permute-start.28 = (f32[384,128]{1,0:T(8,128)S(1)}, f32[384,128]{1,0:T(8,128)S(1)}, u32[]{:S(2)}, u32[]{:S(2)}) collective-permute-start(f32[384,128]{1,0:T(8,128)S(1)} %get-tuple-element.80.refs_0_), channel_id=1, source_target_pairs={{0,2},{2,0},{4,6},{6,4},{8,10},{10,8},{12,14},{14,12},{16,18},{18,... | collective-permute-start | bytes 589832 | tf_op jit(solution)/shard_map/ppermute | solution.py:39
  162.0 8.6 %collective-permute-start.33 = (f32[768,128]{1,0:T(8,128)S(1)}, f32[768,128]{1,0:T(8,128)S(1)}, u32[]{:S(2)}, u32[]{:S(2)}) collective-permute-start(f32[768,128]{1,0:T(8,128)S(1)} %get-tuple-element.85.refs_5_.refs_8_), channel_id=1, source_target_pairs={{0,8},{2,10},{4,12},{6,14},{8,0},{10,2},{12,4},{14,6},{16,24},{18,... | collective-permute-start | bytes 1179656 | tf_op jit(solution)/shard_map/ppermute | solution.py:39
  162.3 7.1 %collective-permute-start.31 = (f32[640,128]{1,0:T(8,128)S(1)}, f32[640,128]{1,0:T(8,128)S(1)}, u32[]{:S(2)}, u32[]{:S(2)}) collective-permute-start(f32[640,128]{1,0:T(8,128)S(1)} %get-tuple-element.83.refs_3_.refs_6_), channel_id=1, source_target_pairs={{0,2},{2,0},{4,6},{6,4},{8,10},{10,8},{12,14},{14,12},{16,18},{18,... | collective-permute-start | bytes 983048 | tf_op jit(solution)/shard_map/ppermute | solution.py:39
  163.5 7.1 %collective-permute-start.32 = (f32[640,128]{1,0:T(8,128)S(1)}, f32[640,128]{1,0:T(8,128)S(1)}, u32[]{:S(2)}, u32[]{:S(2)}) collective-permute-start(f32[640,128]{1,0:T(8,128)S(1)} %get-tuple-element.84.refs_4_.refs_7_), channel_id=1, source_target_pairs={{0,4},{2,6},{4,0},{6,2},{8,12},{10,14},{12,8},{14,10},{16,20},{18,... | collective-permute-start | bytes 983048 | tf_op jit(solution)/shard_map/ppermute | solution.py:39
  (21 other events, 162.2 us)

commit v3 on v2

--- a/solution.py
+++ b/solution.py
@@ -11,12 +11,14 @@
 BLOCK = 128
 
 SHARES = (
-    (5, (0, 1, 2, 3)),
+    (5, (2, 0, 1, 3)),
+    (3, (0, 1, 3, 2)),
+    (3, (0, 1, 3, 2)),
     (5, (1, 2, 0, 3)),
-    (6, (2, 0, 1, 3)),
 )
 BACK = {0: (3, 2, 1, 0), 1: (3, 0, 2, 1), 2: (3, 1, 0, 2)}
-TURNS = (2, 0, 1)
+ARRIVALS = (1, 3, 0, 2, 1, 3, 2, 1, 0, 3, 1, 2, 0, 2, 3, 0)
+TURNS = (3, 1, 0, 2)
 
 precise = lax.Precision.HIGHEST
 epsilon = 1e-05
@@ -170,25 +172,32 @@
 
 
 def merge_kernel(
-    counts, depth, starts_ref, tokens_ref, squares_ref, gain_ref, grad_ref, error_ref, *refs
+    counts, leaves, depth, starts_ref, tokens_ref, squares_ref, gain_ref, grad_ref, error_ref, *refs
 ):
-    outs, held_ref, sems = refs[: len(counts)], refs[-2], refs[-1]
+    n = len(counts)
+    *refs, held_ref, sems, out_sems = refs
+    if leaves:
+        *outs, sum_ref = refs
+    else:
+        outs, whole_ref = refs[-n - 1 : -1], refs[-1]
     pieces, base = [], 0
-    for s, count in counts:
-        for place, size in pieces_of(count, 2 * BLOCK):
+    for s, count in enumerate(counts):
+        for place, size in pieces_of(count, 4 * BLOCK):
             there = pl.ds(pl.multiple_of(starts_ref[s] + place, BLOCK), size)
             here, spot = pl.ds(place, size), pl.ds(base + place, size)
             number = len(pieces)
+            target = sum_ref.at[spot, :] if leaves else outs[s].at[here, :]
             copies = [
                 pltpu.make_async_copy(tokens_ref.at[:, there], held_ref.at[:, spot], sems.at[number, 0]),
-                pltpu.make_async_copy(error_ref.at[there, :], outs[s].at[here, :], sems.at[number, 1]),
+                pltpu.make_async_copy(error_ref.at[there, :], target, sems.at[number, 1]),
             ]
             for copy in copies:
                 copy.start()
-            pieces.append((s, there, here, spot, copies))
+            pieces.append((s, there, here, spot, target, copies))
         base += count
     scale = lax.rsqrt(squares_ref[...] / depth + epsilon)[:, :1]
-    for s, there, here, spot, copies in pieces:
+    written = []
+    for s, there, here, spot, target, copies in pieces:
         gain = gain_ref[:, there].astype(jnp.float32)
         copies[0].wait()
         normed = (held_ref[:, spot].astype(jnp.float32) * scale * gain).astype(jnp.bfloat16)
@@ -196,25 +205,42 @@
             normed, grad_ref[...], (((0,), (0,)), ((), ())), preferred_element_type=jnp.float32
         )
         copies[1].wait()
-        outs[s][here, :] = change + outs[s][here, :]
-
-
-def merge(starts, counts, turns, depth, tokens, square_sums, gain, grad, error):
-    rows = sum(counts)
-    in_turn = [(s, counts[s]) for s in turns]
-    pieces = sum(len(pieces_of(count, 2 * BLOCK)) for count in counts)
+        target[...] = change + target[...]
+        away = outs[s].at[here, :] if leaves else whole_ref.at[spot, :]
+        written.append(pltpu.make_async_copy(target, away, out_sems.at[len(written)]))
+        written[-1].start()
+    for copy in written:
+        copy.wait()
+
+
+def merge(leaves, starts, counts, depth, tokens, square_sums, gain, grad, error, after=()):
+    rows, width = sum(counts), grad.shape[1]
+    pieces = sum(len(pieces_of(count, 4 * BLOCK)) for count in counts)
+    if leaves:
+        shapes = [pltpu.HBM((count, width), jnp.float32) for count in counts]
+        places = [pltpu.HBM] * len(counts)
+        scratch = [pltpu.VMEM((rows, width), jnp.float32)]
+    else:
+        shapes = [near_shape((count, width)) for count in counts]
+        shapes.append(pltpu.HBM((rows, width), jnp.float32))
+        places = [*[pltpu.VMEM] * len(counts), pltpu.HBM]
+        scratch = []
     return kernel_call(
-        functools.partial(merge_kernel, in_turn, depth),
-        out_shape=tuple(near_shape((count, grad.shape[1])) for count in counts),
-        in_specs=specs(pltpu.SMEM, pltpu.HBM, pltpu.VMEM, pltpu.VMEM, pltpu.VMEM, pltpu.HBM),
-        out_specs=tuple(specs(*[pltpu.VMEM] * len(counts))),
+        functools.partial(merge_kernel, counts, leaves, depth),
+        out_shape=tuple(shapes),
+        in_specs=specs(
+            pltpu.SMEM, pltpu.HBM, *[pltpu.VMEM] * 3, pltpu.HBM, *[pl.ANY] * len(after)
+        ),
+        out_specs=tuple(specs(*places)),
         scratch_shapes=[
+            *scratch,
             pltpu.VMEM((tokens.shape[0], rows), tokens.dtype),
             pltpu.SemaphoreType.DMA((pieces, 2)),
+            pltpu.SemaphoreType.DMA((pieces,)),
         ],
         cost_estimate=pl.CostEstimate(
-            flops=2 * rows * grad.shape[1] * tokens.shape[0],
-            bytes_accessed=8 * rows * grad.shape[1] + 2 * tokens.shape[0] * rows,
+            flops=2 * rows * width * tokens.shape[0],
+            bytes_accessed=8 * rows * width + 2 * tokens.shape[0] * rows,
             transcendentals=0,
         ),
     )(
@@ -222,6 +248,7 @@
         distant(tokens),
         *near(square_sums, gain, grad),
         distant(error),
+        *after,
     )
 
 
@@ -240,7 +267,7 @@
     refs[-1][...] = own_ref[...] + got_ref[...]
 
 
-def join(own, got, side, after):
+def join(own, got, side, after, held):
     count, width = own.shape
     arrays, places = near(own, got), [pltpu.VMEM] * 2
     if side is None:
@@ -253,10 +280,10 @@
     return kernel_call(
         kernel,
         out_shape=shapes,
-        in_specs=specs(*places, *[pl.ANY] * len(after)),
+        in_specs=specs(*places, *[pl.ANY] * len(after), *[pltpu.VMEM] * len(held)),
         out_specs=tuple(specs(*[pltpu.VMEM] * len(shapes))),
         cost_estimate=LIGHT,
-    )(*arrays, *after)
+    )(*arrays, *after, *near(*held))
 
 
 def bundles(plan, step):
@@ -305,27 +332,79 @@
     )(sides, *near(*own, *got), *after)
 
 
+def packed_rows(width, share):
+    blocks = width // BLOCK
+    rows = (blocks * (blocks - 1) // 2 + (blocks + 1) // 2) * BLOCK + 8 * (blocks // 2)
+    return -(-rows // share) * share
+
+
+def block_grid():
+    row = lax.broadcasted_iota(jnp.int32, (BLOCK, BLOCK), 0)
+    column = lax.broadcasted_iota(jnp.int32, (BLOCK, BLOCK), 1)
+    return row, column
+
+
 def gram_kernel(replicas, *refs):
     out_ref = refs[-1]
     rows = jnp.concatenate([ref[...] for ref in refs[:-1]], 0) / replicas
     blocks = rows.shape[1] // BLOCK
-    place = 0
+    row, column = block_grid()
+    place, diagonals = 0, []
     for a in range(blocks):
         left = rows[:, a * BLOCK : (a + 1) * BLOCK]
         band = contract(left, rows[:, a * BLOCK :], (0, 0))
-        for b in range(blocks - a):
-            out_ref[place * BLOCK : (place + 1) * BLOCK, :] = band[:, b * BLOCK : (b + 1) * BLOCK]
-            place += 1
-
-
-def gram(parts, replicas):
-    blocks = parts[0].shape[1] // BLOCK
+        diagonals.append(band[:, :BLOCK])
+        for b in range(1, blocks - a):
+            out_ref[place : place + BLOCK, :] = band[:, b * BLOCK : (b + 1) * BLOCK]
+            place += BLOCK
+    for a in range(0, blocks, 2):
+        both = diagonals[a]
+        if a + 1 < blocks:
+            both = jnp.where(row <= column, both, diagonals[a + 1])
+        out_ref[place : place + BLOCK, :] = both
+        place += BLOCK
+    for a in range(1, blocks, 2):
+        line = jnp.sum(jnp.where(row == column, diagonals[a], 0.0), axis=0, keepdims=True)
+        out_ref[place : place + 8, :] = jnp.broadcast_to(line, (8, BLOCK))
+        place += 8
+    if place < out_ref.shape[0]:
+        out_ref[place:, :] = jnp.zeros((out_ref.shape[0] - place, BLOCK), jnp.float32)
+
+
+def gram(parts, replicas, share):
+    rows = packed_rows(parts[0].shape[1], share)
     return kernel_call(
         functools.partial(gram_kernel, replicas),
-        out_shape=near_shape((blocks * (blocks + 1) // 2 * BLOCK, BLOCK)),
+        out_shape=near_shape((rows, BLOCK)),
         in_specs=specs(*[pltpu.VMEM] * len(parts)),
         out_specs=specs(pltpu.VMEM)[0],
     )(*near(*parts))
+
+
+def unpack(packed_ref, whole_ref):
+    blocks = whole_ref.shape[0] // BLOCK
+    row, column = block_grid()
+    place = 0
+
+    def put(a, b, tile):
+        whole_ref[a * BLOCK : (a + 1) * BLOCK, b * BLOCK : (b + 1) * BLOCK] = tile
+
+    for a in range(blocks):
+        for b in range(a + 1, blocks):
+            tile = packed_ref[place : place + BLOCK, :]
+            put(a, b, tile)
+            put(b, a, tile.T)
+            place += BLOCK
+    line_place = place + (blocks + 1) // 2 * BLOCK
+    for a in range(0, blocks, 2):
+        tile = packed_ref[place : place + BLOCK, :]
+        turned = tile.T
+        place += BLOCK
+        put(a, a, jnp.where(row <= column, tile, turned))
+        if a + 1 < blocks:
+            line = packed_ref[line_place : line_place + 1, :]
+            line_place += 8
+            put(a + 1, a + 1, jnp.where(row > column, tile, jnp.where(row < column, turned, line)))
 
 
 def factor(matrix):
@@ -362,15 +441,7 @@
 
 def first_kernel(plan, replicas, packed_ref, basis_ref, *refs):
     whole_ref, right_ref = refs[len(plan) : len(plan) + 2]
-    blocks = basis_ref.shape[0] // BLOCK
-    place = 0
-    for a in range(blocks):
-        for b in range(a, blocks):
-            tile = packed_ref[place * BLOCK : (place + 1) * BLOCK, :]
-            whole_ref[a * BLOCK : (a + 1) * BLOCK, b * BLOCK : (b + 1) * BLOCK] = tile
-            if b > a:
-                whole_ref[b * BLOCK : (b + 1) * BLOCK, a * BLOCK : (a + 1) * BLOCK] = tile.T
-            place += 1
+    unpack(packed_ref, whole_ref)
     basis = basis_ref[...]
     plain = contract(whole_ref[...], basis, (1, 0))
     unit, diagonal = factor(contract(basis, plain, (0, 0)))
@@ -438,96 +509,107 @@
     return pieces
 
 
-def write_errors(plan, replicas, starts_ref, high, low, merged, lefts, out_ref, held_ref, sems, meanwhile=None):
-    pieces = error_pieces(plan, replicas)
+def write_errors(plan, replicas, starts_ref, high, low, merged, lefts, out_ref, held_ref, sems, fetched):
     _, _, where = bundles(plan, bit_count(replicas) - 1)
-    fetched = []
-    for number, (s, place, spot, size) in enumerate(pieces):
-        fetched.append(
-            pltpu.make_async_copy(
-                merged[s].at[pl.ds(place, size), :], held_ref.at[pl.ds(spot, size), :], sems.at[0, number]
-            )
-        )
-        fetched[-1].start()
-    if meanwhile:
-        meanwhile()
     written = []
-    for number, (s, place, spot, size) in enumerate(pieces):
+    for number, (s, place, spot, size) in enumerate(error_pieces(plan, replicas)):
         index, first = where[s]
         there = pl.ds(pl.multiple_of(starts_ref[s] + place, BLOCK), size)
         here = pl.ds(spot, size)
         change = low_rank(lefts[index][pl.ds(first + place, size), :], high, low)
-        fetched[number].wait()
-        held_ref[here, :] = held_ref[here, :] - change
+        if fetched:
+            fetched[number].wait()
+        held_ref[here, :] = merged[here, :] - change
         written.append(
-            pltpu.make_async_copy(held_ref.at[here, :], out_ref.at[there, :], sems.at[1, number])
+            pltpu.make_async_copy(held_ref.at[here, :], out_ref.at[there, :], sems.at[number])
         )
         written[-1].start()
-    for copy in written:
+    return written
+
+
+def error_kernel(plan, replicas, starts_ref, high_ref, low_ref, own_ref, *refs):
+    n = len(plan)
+    out_ref, near_ref, held_ref, fetch_sems, sems, near_sems = refs[-6:]
+    fetched = []
+    for number, (_, _, spot, size) in enumerate(error_pieces(plan, replicas)):
+        here = pl.ds(spot, size)
+        fetched.append(
+            pltpu.make_async_copy(own_ref.at[here, :], held_ref.at[here, :], fetch_sems.at[number])
+        )
+        fetched[-1].start()
+    others, base = [], 0
+    for s, stream in enumerate(plan):
+        count = stream.width * replicas // 2
+        others.append(
+            pltpu.make_async_copy(refs[s], near_ref.at[pl.ds(base, count), :], near_sems.at[s])
+        )
+        others[-1].start()
+        base += count
+    written = write_errors(
+        plan, replicas, starts_ref, high_ref[...], low_ref[...], held_ref, refs[n:-6], out_ref, held_ref,
+        sems, fetched,
+    )
+    for copy in written + others:
         copy.wait()
 
 
-def error_kernel(plan, replicas, starts_ref, high_ref, low_ref, *refs):
-    n = len(plan)
-    write_errors(
-        plan, replicas, starts_ref, high_ref[...], low_ref[...], refs[:n], refs[n:-3], *refs[-3:]
-    )
-
-
-def last_error_kernel(plan, replicas, starts_ref, high_ref, low_ref, *refs):
+def last_error_kernel(plan, replicas, starts_ref, high_ref, low_ref, merged_ref, *refs):
     n = len(plan)
     _, groups, where = bundles(plan, bit_count(replicas) - 1)
     m = len(groups)
-    merged, others, lefts = refs[:n], refs[n : n + m], refs[n + m : n + 2 * m]
-    weights_ref, momentum_ref = refs[n + 2 * m : n + 2 * m + 2]
+    others, lefts = refs[:m], refs[m : 2 * m]
+    weights_ref, momentum_ref = refs[2 * m : 2 * m + 2]
     out_ref, weights_out, momentum_out, held_ref, left_ref, sems = refs[-6:]
     high, low = high_ref[...], low_ref[...]
+    written = write_errors(
+        plan, replicas, starts_ref, high, low, merged_ref, others, out_ref, held_ref, sems, None
+    )
     rows = left_ref.shape[0]
     size = min(BLOCK, rows)
-
-    def outer():
-        for place in range(0, rows, size):
-            want = starts_ref[2 * n] + place
-            for k, bundle in ((0, others), (n, lefts)):
-                for s, stream in enumerate(plan):
-                    index, first = where[s]
-                    skip = want - starts_ref[k + s]
-
-                    @pl.when((skip >= 0) & (skip < stream.width * replicas // 2))
-                    def _(bundle=bundle, index=index, first=first, skip=skip, place=place):
-                        row = pl.multiple_of(first + skip, 8)
-                        left_ref[place : place + size, :] = bundle[index][pl.ds(row, size), :]
-
-        own_rows = low_rank(left_ref[...], high, low)
-        momentum = momentum_rate * momentum_ref[...] + own_rows
-        momentum_out[...] = momentum
-        weights_out[...] = weights_ref[...] - outer_rate * (own_rows + momentum_rate * momentum)
-
-    write_errors(plan, replicas, starts_ref, high, low, merged, others, out_ref, held_ref, sems, outer)
+    for place in range(0, rows, size):
+        want = starts_ref[2 * n] + place
+        for k, bundle in ((0, others), (n, lefts)):
+            for s, stream in enumerate(plan):
+                index, first = where[s]
+                skip = want - starts_ref[k + s]
+
+                @pl.when((skip >= 0) & (skip < stream.width * replicas // 2))
+                def _(bundle=bundle, index=index, first=first, skip=skip, place=place):
+                    row = pl.multiple_of(first + skip, 8)
+                    left_ref[place : place + size, :] = bundle[index][pl.ds(row, size), :]
+
+    own_rows = low_rank(left_ref[...], high, low)
+    momentum = momentum_rate * momentum_ref[...] + own_rows
+    momentum_out[...] = momentum
+    weights_out[...] = weights_ref[...] - outer_rate * (own_rows + momentum_rate * momentum)
+    for copy in written:
+        copy.wait()
 
 
 def error_options(plan, replicas, width, rank):
     pieces = error_pieces(plan, replicas)
     rows = sum(piece[3] for piece in pieces)
-    scratch = pltpu.VMEM((rows, width), jnp.float32), pltpu.SemaphoreType.DMA((2, len(pieces)))
+    scratch = pltpu.VMEM((rows, width), jnp.float32), pltpu.SemaphoreType.DMA((len(pieces),))
     cost = pl.CostEstimate(
         flops=6 * rows * width * rank, bytes_accessed=8 * rows * width, transcendentals=0
     )
     return scratch, cost
 
 
-def error_rows(plan, replicas, starts, merged, lefts, high, low, shape):
+def error_rows(plan, replicas, starts, own, far, lefts, high, low, shape):
     scratch, cost = error_options(plan, replicas, shape[1], high.shape[0])
     return kernel_call(
         functools.partial(error_kernel, plan, replicas),
-        out_shape=jax.ShapeDtypeStruct(shape, jnp.float32),
+        out_shape=(jax.ShapeDtypeStruct(shape, jnp.float32), near_shape(own.shape)),
         in_specs=specs(
-            pltpu.SMEM, *[pltpu.VMEM] * 2, *[pltpu.HBM] * len(merged), *[pltpu.VMEM] * len(lefts)
+            pltpu.SMEM, *[pltpu.VMEM] * 2, *[pltpu.HBM] * (1 + len(far)), *[pltpu.VMEM] * len(lefts)
         ),
-        out_specs=specs(pltpu.HBM)[0],
-        scratch_shapes=scratch,
+        out_specs=tuple(specs(pltpu.HBM, pltpu.VMEM)),
+        scratch_shapes=[*scratch, scratch[1], pltpu.SemaphoreType.DMA((len(far),))],
         cost_estimate=cost,
-    )(jnp.stack(starts).astype(jnp.int32), *near(high, low), *map(distant, merged), *near(*lefts))
+    )(
+        jnp.stack(starts).astype(jnp.int32), *near(high, low), distant(own), *map(distant, far), *near(*lefts)
+    )
 
 
 def last_rows(plan, replicas, kept, starts, merged, others, lefts, high, low, weights, momentum):
@@ -535,9 +617,7 @@
     (held, sems), cost = error_options(plan, replicas, width, high.shape[0])
     arrays = [
         jnp.stack([*starts, lax.axis_index("rep") * rows]).astype(jnp.int32),
-        *near(high, low),
-        *map(distant, merged),
-        *near(*others, *lefts),
+        *near(high, low, merged, *others, *lefts),
         weights,
         momentum,
         kept,
@@ -546,13 +626,7 @@
     return kernel_call(
         functools.partial(last_error_kernel, plan, replicas),
         out_shape=(jax.ShapeDtypeStruct(kept.shape, jnp.float32), result, result),
-        in_specs=specs(
-            pltpu.SMEM,
-            *[pltpu.VMEM] * 2,
-            *[pltpu.HBM] * len(merged),
-            *[pltpu.VMEM] * (2 * len(lefts) + 2),
-            pltpu.HBM,
-        ),
+        in_specs=specs(pltpu.SMEM, *[pltpu.VMEM] * (2 * len(lefts) + 5), pltpu.HBM),
         out_specs=tuple(specs(pltpu.HBM, pltpu.VMEM, pltpu.VMEM)),
         scratch_shapes=[held, pltpu.VMEM((rows, high.shape[0]), jnp.float32), sems],
         input_output_aliases={len(arrays) - 1: 0},
@@ -577,14 +651,14 @@
             Stream(share * units // 16 * grain, order, BACK[order[0]])
             for share, order in shares
         ]
-        return plan, TURNS
+        return plan, TURNS, ARRIVALS
     streams = max(1, min(3, units, bits - 1))
     widths = [units // streams + (1 if s < units % streams else 0) for s in range(streams)]
     lead = list(range(min(3, bits)))
     rest = list(range(len(lead), bits))
     orders = [tuple(lead[s % len(lead) :] + lead[: s % len(lead)] + rest) for s in range(streams)]
     plan = [Stream(w * grain, order, order[::-1]) for w, order in zip(widths, orders)]
-    return plan, range(streams)
+    return plan, range(streams), [s for _ in range(bits) for s in range(streams)]
 
 
 def on_device(tokens_in, norm_gain, key_grad, error_in, basis_init, weights_in, momentum_in):
@@ -598,7 +672,7 @@
         depth * lax.axis_size("mp"), tokens_in, square_sums, norm_gain[None, :], key_grad, error
     )
 
-    plan, turns = stream_plan(replicas, depth // replicas)
+    plan, turns, arrivals = stream_plan(replicas, depth // replicas)
     halves, here, there, place = [], [], [], 0
     for stream in plan:
         half = stream.width * replicas // 2
@@ -607,21 +681,22 @@
         here.append(place + side * half)
         there.append(place + (1 - side) * half)
         place += 2 * half
-    far = merge(there, halves, turns, *sources)
+    far = merge(True, there, halves, *sources)
     got = [flip(part, "rep", 1 << stream.order[0]) for part, stream in zip(far, plan)]
-    own = merge(here, halves, turns, *sources)
-    parts, after = list(own), [basis]
-    for step in range(steps):
-        for s in turns:
-            if step + 1 < steps:
-                bit = plan[s].order[step + 1]
-                parts[s], send = join(parts[s], got[s], bit_of("rep", bit), after)
-                got[s] = flip(send, "rep", 1 << bit)
-            else:
-                (parts[s],) = join(parts[s], got[s], None, after)
-        after = []
-
-    packed = sum_everywhere(gram(parts, replicas))
+    *own, own_kept = merge(False, here, halves, *sources, after=[basis])
+    parts, after, done = list(own), [], [0] * len(plan)
+    for s in arrivals:
+        done[s] += 1
+        came = got[s]
+        if done[s] < steps:
+            bit = plan[s].order[done[s]]
+            parts[s], send = join(parts[s], came, bit_of("rep", bit), after, [p for k, p in enumerate(parts) if k != s])
+            got[s] = flip(send, "rep", 1 << bit)
+        else:
+            (parts[s],) = join(parts[s], came, None, after, [])
+        after = [came]
+
+    packed = sum_everywhere(gram(parts, replicas, 32 * lax.axis_size("mp")))
     whole, right, lefts = first_pass(plan, packed, basis, parts, replicas)
     high, low = second_pass(whole, right)
 
@@ -632,9 +707,12 @@
         if step + 1 < steps:
             lefts = gather_step(plan, step, bit_sides, lefts, others, [high])
 
-    error_out = error_rows(plan, replicas, here, own, lefts, high, low, error.shape)
+    error_out, far_near = error_rows(
+        plan, replicas, here, own_kept, far, lefts, high, low, error.shape
+    )
     error_out, weights_out, momentum_out = last_rows(
-        plan, replicas, error_out, there + here, far, others, lefts, high, low, weights_in[0], momentum_in[0]
+        plan, replicas, error_out, there + here, far_near, others, lefts, high, low, weights_in[0],
+        momentum_in[0],
     )
     return (error_out[None], weights_out[None], momentum_out[None])
 

time: 176 us -> 169 us (0.960)
  waiting for transfers between devices: 91.3 us -> 66.6 us
  Pallas kernels: 38.9 us -> 47.5 us
  starting transfers between devices: 41.1 us -> 48.5 us
    ppermute x34 -> x38, waiting for transfers between devices: 91.3 us -> 66.6 us  [flip(): return lax.ppermute(value, axis, [(i, i ^ mask) for i in range(size)])]
    pallas_call x12 -> x16, Pallas kernels: 0.94 us -> 9.47 us  [join(): kernel_call(kernel, out_shape=shapes, in_specs=specs(*places, *[pl.ANY] *...]
    ppermute x34 -> x38, starting transfers between devices: 41.1 us -> 48.5 us  [flip(): return lax.ppermute(value, axis, [(i, i ^ mask) for i in range(size)])]
  transfers between devices with their start and end apart: 34 -> 38, of which waited for: 23 -> 24; matrix products, arithmetic and copies ran while one was open for 0% -> 0% of each run, Pallas kernels for 9% -> 16%
where the time goes in v3:
time: 169 us
  waiting for transfers between devices  66.6 us (39%)
  starting transfers between devices  48.5 us (29%)
  Pallas kernels  47.5 us (28%)
  local copies, waits for them, and re-layouts  2.62 us (2%)
  blocking collectives  2.16 us (1%)
    ppermute x38, waiting for transfers between devices, flip(): return lax.ppermute(value, axis, [(i, i ^ mask) for i in range(size)])  66.6 us
    ppermute x38, starting transfers between devices, flip(): return lax.ppermute(value, axis, [(i, i ^ mask) for i in range(size)])  48.5 us
    pallas_call x2, Pallas kernels, merge(): kernel_call(functools.partial(merge_kernel, counts, leaves, depth), out_s...  9.64 us
    pallas_call x16, Pallas kernels, join(): kernel_call(kernel, out_shape=shapes, in_specs=specs(*places, *[pl.ANY] *...  9.47 us
    pallas_call x1, Pallas kernels, first_pass(): kernel_call(functools.partial(first_kernel, plan, replicas), out_shape=sh...  7.81 us
    pallas_call x1, Pallas kernels, error_rows(): kernel_call(functools.partial(error_kernel, plan, replicas), out_shape=(j...  5.44 us
    pallas_call x1, Pallas kernels, second_pass(): pair(weight_kernel, out_shape=(half, half))(*near(plain, gram_matrix))  4.8 us
    pallas_call x1, Pallas kernels, last_rows(): kernel_call(functools.partial(last_error_kernel, plan, replicas), out_sha...  3.99 us
  transfers between devices with their start and end apart: 38, of which 24 were waited for; matrix products, arithmetic and copies ran while one was open for 0% of the time, Pallas kernels for 16%

profile of v3, /device:TPU:0, one launch (start us, length us, event | category | flops | bytes accessed | tf_op | source)
XLA Modules:
  0.0 169.0 jit_solution(10870715400527512734)
XLA Ops:
  4.0 4.8 %shard_map.96 = (f32[640,512]{1,0:T(8,128)}, f32[384,512]{1,0:T(8,128)}, f32[384,512]{1,0:T(8,128)}, f32[640,512]{1,0:T(8,128)}) custom-call(s32[4]{0:T(128)S(1)} %pad_add_fusion.1.starts_ref, bf16[256,4096]{1,0:T(8,128)(2,1)} %tokens_ref.5, f32[256,128]{1,0:T(8,128)S(1)} %add.71.squares_ref, bf16[1,4096]{1,0:T(2,128)(2,1)S(1)} %broadcast_in_dim.16.gain_ref, ...), custom_call_target="tpu_custom_call" | custom-call | flops 536870912 | bytes 9437184 | tf_op jit(solution)/shard_map/pallas_call | solution.py:228
  8.8 2.9 %collective-permute-start.2 = (f32[640,512]{1,0:T(8,128)}, f32[640,512]{1,0:T(8,128)S(1)}, u32[]{:S(2)}, u32[]{:S(2)}) collective-permute-start(f32[640,512]{1,0:T(8,128)} %get-tuple-element.59.refs_3_), channel_id=1, source_target_pairs={{0,4},{2,6},{4,0},{6,2},{8,12},{10,14},{12,8},{14,10},{16,20},{18,... | collective-permute-start | bytes 3932168 | tf_op jit(solution)/shard_map/ppermute | solution.py:41
  15.4 2.2 %all_gather.3.refs_0_.basis_ref = f32[512,128]{1,0:T(8,128)S(1)} all-gather(f32[256,128]{1,0:T(8,128)S(1)} %copy-done.7), channel_id=1, replica_groups=mesh['rep'=16,'mp'=2] {'mp'}, dimensions={0}, use_global_device_ids=true | all-gather | bytes 393216 | tf_op jit(solution)/shard_map/all_gather | solution.py:670
  17.6 4.8 %shard_map.95 = (f32[640,512]{1,0:T(8,128)S(1)}, f32[384,512]{1,0:T(8,128)S(1)}, f32[384,512]{1,0:T(8,128)S(1)}, f32[640,512]{1,0:T(8,128)S(1)}, f32[2048,512]{1,0:T(8,128)}) custom-call(s32[4]{0:T(128)S(1)} %pad_add_fusion.starts_ref, bf16[256,4096]{1,0:T(8,128)(2,1)} %tokens_ref.5, f32[256,128]{1,0:T(8,128)S(1)} %add.71.squares_ref, ...), custom_call_target="tpu_custom_call" | custom-call | flops 536870912 | bytes 9437184 | tf_op jit(solution)/shard_map/pallas_call | solution.py:228
  22.5 11.7 %collective-permute-done.3.got_ref.refs_0_ = f32[384,512]{1,0:T(8,128)} collective-permute-done((f32[384,512]{1,0:T(8,128)}, f32[384,512]{1,0:T(8,128)}, u32[]{:S(2)}, u32[]{:S(2)}) %collective-permute-start.3) | collective-permute-done | bytes 786464 | tf_op jit(solution)/shard_map/ppermute | solution.py:41
  36.1 5.0 %collective-permute-done.2.got_ref.refs_0_ = f32[640,512]{1,0:T(8,128)S(1)} collective-permute-done((f32[640,512]{1,0:T(8,128)}, f32[640,512]{1,0:T(8,128)S(1)}, u32[]{:S(2)}, u32[]{:S(2)}) %collective-permute-start.2) | collective-permute-done | bytes 1310752 | tf_op jit(solution)/shard_map/ppermute | solution.py:41
  50.2 2.0 %shard_map.100 = (f32[192,512]{1,0:T(8,128)S(1)}, f32[192,512]{1,0:T(8,128)}) custom-call(s32[1]{0:T(128)} %bitcast.10.side_ref, f32[384,512]{1,0:T(8,128)S(1)} %get-tuple-element.62.refs_1_.refs_3_.refs_2_.own_ref, f32[384,512]{1,0:T(8,128)} %collective-permute-done.6.got_ref.refs_0_, f32[640,512]{1,0:T(8,128)S(1)} %collective-permute-done.1.got_ref.refs_0_, ...), custom_call_target="tpu_custom_call" | custom-call | flops 1 | bytes 1 | tf_op jit(solution)/shard_map/pallas_call | solution.py:280
  52.7 8.4 %collective-permute-done.5.got_ref.refs_0_ = f32[192,512]{1,0:T(8,128)} collective-permute-done((f32[192,512]{1,0:T(8,128)}, f32[192,512]{1,0:T(8,128)}, u32[]{:S(2)}, u32[]{:S(2)}) %collective-permute-start.5) | collective-permute-done | bytes 393248 | tf_op jit(solution)/shard_map/ppermute | solution.py:41
  62.1 2.7 %collective-permute-start.7 = (f32[96,512]{1,0:T(8,128)S(1)}, f32[96,512]{1,0:T(8,128)S(1)}, u32[]{:S(2)}, u32[]{:S(2)}) collective-permute-start(f32[96,512]{1,0:T(8,128)S(1)} %get-tuple-element.71), channel_id=1, source_target_pairs={{0,16},{2,18},{4,20},{6,22},{8,24},{10,26},{12,28},{14,30},{16,0},... | collective-permute-start | bytes 589832 | tf_op jit(solution)/shard_map/ppermute | solution.py:41
  67.3 3.5 %collective-permute-done.7.got_ref.refs_0_ = f32[96,512]{1,0:T(8,128)S(1)} collective-permute-done((f32[96,512]{1,0:T(8,128)S(1)}, f32[96,512]{1,0:T(8,128)S(1)}, u32[]{:S(2)}, u32[]{:S(2)}) %collective-permute-start.7) | collective-permute-done | bytes 196640 | tf_op jit(solution)/shard_map/ppermute | solution.py:41
  71.9 4.0 %collective-permute-start.10 = (f32[160,512]{1,0:T(8,128)S(1)}, f32[160,512]{1,0:T(8,128)S(1)}, u32[]{:S(2)}, u32[]{:S(2)}) collective-permute-start(f32[160,512]{1,0:T(8,128)S(1)} %get-tuple-element.79), channel_id=1, source_target_pairs={{0,4},{2,6},{4,0},{6,2},{8,12},{10,14},{12,8},{14,10},{16,20},{18,... | collective-permute-start | bytes 983048 | tf_op jit(solution)/shard_map/ppermute | solution.py:41
  79.0 3.8 %collective-permute-done.12.got_ref.refs_0_ = f32[48,512]{1,0:T(8,128)S(1)} collective-permute-done((f32[48,512]{1,0:T(8,128)S(1)}, f32[48,512]{1,0:T(8,128)S(1)}, u32[]{:S(2)}, u32[]{:S(2)}) %collective-permute-start.12) | collective-permute-done | bytes 98336 | tf_op jit(solution)/shard_map/ppermute | solution.py:41
  82.8 5.4 %collective-permute-done.11.got_ref.refs_0_ = f32[96,512]{1,0:T(8,128)S(1)} collective-permute-done((f32[96,512]{1,0:T(8,128)S(1)}, f32[96,512]{1,0:T(8,128)S(1)}, u32[]{:S(2)}, u32[]{:S(2)}) %collective-permute-start.11) | collective-permute-done | bytes 196640 | tf_op jit(solution)/shard_map/ppermute | solution.py:41
  88.4 3.2 %collective-permute-start.16 = (f32[48,512]{1,0:T(8,128)S(1)}, f32[48,512]{1,0:T(8,128)S(1)}, u32[]{:S(2)}, u32[]{:S(2)}) collective-permute-start(f32[48,512]{1,0:T(8,128)S(1)} %get-tuple-element.88), channel_id=1, source_target_pairs={{0,8},{2,10},{4,12},{6,14},{8,0},{10,2},{12,4},{14,6},{16,24},{18,... | collective-permute-start | bytes 294920 | tf_op jit(solution)/shard_map/ppermute | solution.py:41
  91.6 2.7 %collective-permute-done.16.got_ref.refs_0_ = f32[48,512]{1,0:T(8,128)S(1)} collective-permute-done((f32[48,512]{1,0:T(8,128)S(1)}, f32[48,512]{1,0:T(8,128)S(1)}, u32[]{:S(2)}, u32[]{:S(2)}) %collective-permute-start.16) | collective-permute-done | bytes 98336 | tf_op jit(solution)/shard_map/ppermute | solution.py:41
  107.4 2.7 %collective-permute-start.21 = (f32[136,128]{1,0:T(8,128)S(1)}, f32[136,128]{1,0:T(8,128)S(1)}, u32[]{:S(2)}, u32[]{:S(2)}) collective-permute-start(f32[136,128]{1,0:T(8,128)S(1)} %add_add_fusion.1), channel_id=1, source_target_pairs={{0,8},{2,10},{4,12},{6,14},{8,0},{10,2},{12,4},{14,6},{16,24},{18,... | collective-permute-start | bytes 208904 | tf_op jit(solution)/shard_map/ppermute | solution.py:41
  110.1 2.6 %collective-permute-done.23 = f32[136,128]{1,0:T(8,128)S(1)} collective-permute-done((f32[136,128]{1,0:T(8,128)S(1)}, f32[136,128]{1,0:T(8,128)S(1)}, u32[]{:S(2)}, u32[]{:S(2)}) %collective-permute-start.23) | collective-permute-done | bytes 69664 | tf_op jit(solution)/shard_map/ppermute | solution.py:41
  119.2 2.2 %collective-permute-done.26 = f32[136,128]{1,0:T(8,128)S(1)} collective-permute-done((f32[136,128]{1,0:T(8,128)S(1)}, f32[136,128]{1,0:T(8,128)S(1)}, u32[]{:S(2)}, u32[]{:S(2)}) %collective-permute-start.26) | collective-permute-done | bytes 69664 | tf_op jit(solution)/shard_map/ppermute | solution.py:41
  123.1 7.8 %shard_map.114 = (f32[512,512]{1,0:T(8,128)S(1)}, f32[512,128]{1,0:T(8,128)S(1)}, f32[256,128]{1,0:T(8,128)S(1)}) custom-call(f32[1088,128]{1,0:T(8,128)S(1)} %constant_dynamic-update-slice_fusion.packed_ref, f32[512,128]{1,0:T(8,128)S(1)} %copy-done.3, f32[80,512]{1,0:T(8,128)S(1)} %shard_map.110.refs_0_, f32[48,512]{1,0:T(8,128)S(1)} %shard_map.106.refs_2_.refs_1_, ...), custom_call_target="tpu_custom_call" | custom-call | tf_op jit(solution)/shard_map/pallas_call | solution.py:459
  133.5 4.8 %shard_map.116 = (bf16[128,512]{1,0:T(8,128)(2,1)S(1)}, bf16[128,512]{1,0:T(8,128)(2,1)S(1)}) custom-call(f32[512,128]{1,0:T(8,128)S(1)} %get-tuple-element.91.plain_ref, f32[128,128]{1,0:T(8,128)S(1)} %get-tuple-element.92.gram_ref), custom_call_target="tpu_custom_call" | custom-call | tf_op jit(solution)/shard_map/pallas_call | solution.py:493
  142.8 2.3 %collective-permute-done.29.refs_3_ = f32[160,128]{1,0:T(8,128)S(1)} collective-permute-done((f32[160,128]{1,0:T(8,128)S(1)}, f32[160,128]{1,0:T(8,128)S(1)}, u32[]{:S(2)}, u32[]{:S(2)}) %collective-permute-start.29) | collective-permute-done | bytes 81952 | tf_op jit(solution)/shard_map/ppermute | solution.py:41
  150.6 2.6 %collective-permute-done.32.refs_3_ = f32[320,128]{1,0:T(8,128)S(1)} collective-permute-done((f32[320,128]{1,0:T(8,128)S(1)}, f32[320,128]{1,0:T(8,128)S(1)}, u32[]{:S(2)}, u32[]{:S(2)}) %collective-permute-start.32) | collective-permute-done | bytes 163872 | tf_op jit(solution)/shard_map/ppermute | solution.py:41
  159.4 5.4 %shard_map.120 = (f32[4096,512]{1,0:T(8,128)}, f32[2048,512]{1,0:T(8,128)S(1)}) custom-call(s32[4]{0:T(128)S(1)} %pad_add_fusion.starts_ref, bf16[128,512]{1,0:T(8,128)(2,1)S(1)} %get-tuple-element.93.refs_2_.refs_6_.high_ref, bf16[128,512]{1,0:T(8,128)(2,1)S(1)} %get-tuple-element.94.low_ref, f32[2048,512]{1,0:T(8,128)} %get-tuple-element.95.own_ref, ...), custom_call_target="tpu_custom_call" | custom-call | flops 805306368 | bytes 8388608 | tf_op jit(solution)/shard_map/pallas_call | solution.py:601
  164.9 4.0 %shard_map.121 = (f32[4096,512]{1,0:T(8,128)}, f32[256,512]{1,0:T(8,128)}, f32[256,512]{1,0:T(8,128)}) custom-call(s32[9]{0:T(128)S(1)} %stack.65.starts_ref, bf16[128,512]{1,0:T(8,128)(2,1)S(1)} %get-tuple-element.93.refs_2_.refs_6_.high_ref, bf16[128,512]{1,0:T(8,128)(2,1)S(1)} %get-tuple-element.94.low_ref, ...), custom_call_target="tpu_custom_call", output_to_operand_aliasing={{0}: (12, {})} | custom-call | flops 805306368 | bytes 8388608 | tf_op jit(solution)/shard_map/pallas_call | solution.py:626
  (116 shorter events, 66.3 us)
Async XLA Ops:
  8.8 32.2 %collective-permute-start.2 = (f32[640,512]{1,0:T(8,128)}, f32[640,512]{1,0:T(8,128)S(1)}, u32[]{:S(2)}, u32[]{:S(2)}) collective-permute-start(f32[640,512]{1,0:T(8,128)} %get-tuple-element.59.refs_3_), channel_id=1, source_target_pairs={{0,4},{2,6},{4,0},{6,2},{8,12},{10,14},{12,8},{14,10},{16,20},{18,... | collective-permute-start | bytes 3932168 | tf_op jit(solution)/shard_map/ppermute | solution.py:41
  11.8 34.4 %collective-permute-start.1 = (f32[640,512]{1,0:T(8,128)}, f32[640,512]{1,0:T(8,128)S(1)}, u32[]{:S(2)}, u32[]{:S(2)}) collective-permute-start(f32[640,512]{1,0:T(8,128)} %get-tuple-element.58.refs_0_), channel_id=1, source_target_pairs={{0,8},{2,10},{4,12},{6,14},{8,0},{10,2},{12,4},{14,6},{16,24},{18,... | collective-permute-start | bytes 3932168 | tf_op jit(solution)/shard_map/ppermute | solution.py:41
  13.3 20.8 %collective-permute-start.3 = (f32[384,512]{1,0:T(8,128)}, f32[384,512]{1,0:T(8,128)}, u32[]{:S(2)}, u32[]{:S(2)}) collective-permute-start(f32[384,512]{1,0:T(8,128)} %get-tuple-element.61.refs_1_), channel_id=1, source_target_pairs={{0,2},{2,0},{4,6},{6,4},{8,10},{10,8},{12,14},{14,12},{16,18},{18,... | collective-permute-start | bytes 2359304 | tf_op jit(solution)/shard_map/ppermute | solution.py:41
  14.8 35.4 %collective-permute-start.6 = (f32[384,512]{1,0:T(8,128)}, f32[384,512]{1,0:T(8,128)}, u32[]{:S(2)}, u32[]{:S(2)}) collective-permute-start(f32[384,512]{1,0:T(8,128)} %get-tuple-element.69.refs_2_), channel_id=1, source_target_pairs={{0,2},{2,0},{4,6},{6,4},{8,10},{10,8},{12,14},{14,12},{16,18},{18,... | collective-permute-start | bytes 2359304 | tf_op jit(solution)/shard_map/ppermute | solution.py:41
  44.4 20.4 %collective-permute-start.9 = (f32[320,512]{1,0:T(8,128)}, f32[320,512]{1,0:T(8,128)}, u32[]{:S(2)}, u32[]{:S(2)}) collective-permute-start(f32[320,512]{1,0:T(8,128)} %get-tuple-element.74), channel_id=1, source_target_pairs={{0,8},{2,10},{4,12},{6,14},{8,0},{10,2},{12,4},{14,6},{16,24},{18,... | collective-permute-start | bytes 1966088 | tf_op jit(solution)/shard_map/ppermute | solution.py:41
  47.2 23.6 %collective-permute-start.4 = (f32[320,512]{1,0:T(8,128)}, f32[320,512]{1,0:T(8,128)}, u32[]{:S(2)}, u32[]{:S(2)}) collective-permute-start(f32[320,512]{1,0:T(8,128)} %get-tuple-element.67), channel_id=1, source_target_pairs={{0,2},{2,0},{4,6},{6,4},{8,10},{10,8},{12,14},{14,12},{16,18},{18,... | collective-permute-start | bytes 1966088 | tf_op jit(solution)/shard_map/ppermute | solution.py:41
  48.7 12.4 %collective-permute-start.5 = (f32[192,512]{1,0:T(8,128)}, f32[192,512]{1,0:T(8,128)}, u32[]{:S(2)}, u32[]{:S(2)}) collective-permute-start(f32[192,512]{1,0:T(8,128)} %get-tuple-element.68), channel_id=1, source_target_pairs={{0,4},{2,6},{4,0},{6,2},{8,12},{10,14},{12,8},{14,10},{16,20},{18,... | collective-permute-start | bytes 1179656 | tf_op jit(solution)/shard_map/ppermute | solution.py:41
  52.2 15.0 %collective-permute-start.8 = (f32[192,512]{1,0:T(8,128)}, f32[192,512]{1,0:T(8,128)S(1)}, u32[]{:S(2)}, u32[]{:S(2)}) collective-permute-start(f32[192,512]{1,0:T(8,128)} %get-tuple-element.73), channel_id=1, source_target_pairs={{0,4},{2,6},{4,0},{6,2},{8,12},{10,14},{12,8},{14,10},{16,20},{18,... | collective-permute-start | bytes 1179656 | tf_op jit(solution)/shard_map/ppermute | solution.py:41
  62.1 8.6 %collective-permute-start.7 = (f32[96,512]{1,0:T(8,128)S(1)}, f32[96,512]{1,0:T(8,128)S(1)}, u32[]{:S(2)}, u32[]{:S(2)}) collective-permute-start(f32[96,512]{1,0:T(8,128)S(1)} %get-tuple-element.71), channel_id=1, source_target_pairs={{0,16},{2,18},{4,20},{6,22},{8,24},{10,26},{12,28},{14,30},{16,0},... | collective-permute-start | bytes 589832 | tf_op jit(solution)/shard_map/ppermute | solution.py:41
  65.9 11.1 %collective-permute-start.13 = (f32[160,512]{1,0:T(8,128)S(1)}, f32[160,512]{1,0:T(8,128)S(1)}, u32[]{:S(2)}, u32[]{:S(2)}) collective-permute-start(f32[160,512]{1,0:T(8,128)S(1)} %get-tuple-element.82), channel_id=1, source_target_pairs={{0,2},{2,0},{4,6},{6,4},{8,10},{10,8},{12,14},{14,12},{16,18},{18,... | collective-permute-start | bytes 983048 | tf_op jit(solution)/shard_map/ppermute | solution.py:41
  71.9 16.3 %collective-permute-start.10 = (f32[160,512]{1,0:T(8,128)S(1)}, f32[160,512]{1,0:T(8,128)S(1)}, u32[]{:S(2)}, u32[]{:S(2)}) collective-permute-start(f32[160,512]{1,0:T(8,128)S(1)} %get-tuple-element.79), channel_id=1, source_target_pairs={{0,4},{2,6},{4,0},{6,2},{8,12},{10,14},{12,8},{14,10},{16,20},{18,... | collective-permute-start | bytes 983048 | tf_op jit(solution)/shard_map/ppermute | solution.py:41
  76.0 12.2 %collective-permute-start.11 = (f32[96,512]{1,0:T(8,128)S(1)}, f32[96,512]{1,0:T(8,128)S(1)}, u32[]{:S(2)}, u32[]{:S(2)}) collective-permute-start(f32[96,512]{1,0:T(8,128)S(1)} %get-tuple-element.80), channel_id=1, source_target_pairs={{0,16},{2,18},{4,20},{6,22},{8,24},{10,26},{12,28},{14,30},{16,0},... | collective-permute-start | bytes 589832 | tf_op jit(solution)/shard_map/ppermute | solution.py:41
  76.0 6.8 %collective-permute-start.12 = (f32[48,512]{1,0:T(8,128)S(1)}, f32[48,512]{1,0:T(8,128)S(1)}, u32[]{:S(2)}, u32[]{:S(2)}) collective-permute-start(f32[48,512]{1,0:T(8,128)S(1)} %get-tuple-element.81), channel_id=1, source_target_pairs={{0,8},{2,10},{4,12},{6,14},{8,0},{10,2},{12,4},{14,6},{16,24},{18,... | collective-permute-start | bytes 294920 | tf_op jit(solution)/shard_map/ppermute | solution.py:41
  77.1 17.2 %collective-permute-start.15 = (f32[80,512]{1,0:T(8,128)S(1)}, f32[80,512]{1,0:T(8,128)S(1)}, u32[]{:S(2)}, u32[]{:S(2)}) collective-permute-start(f32[80,512]{1,0:T(8,128)S(1)} %get-tuple-element.87), channel_id=1, source_target_pairs={{0,16},{2,18},{4,20},{6,22},{8,24},{10,26},{12,28},{14,30},{16,0},... | collective-permute-start | bytes 491528 | tf_op jit(solution)/shard_map/ppermute | solution.py:41
  88.3 7.7 %collective-permute-start.14 = (f32[80,512]{1,0:T(8,128)S(1)}, f32[80,512]{1,0:T(8,128)S(1)}, u32[]{:S(2)}, u32[]{:S(2)}) collective-permute-start(f32[80,512]{1,0:T(8,128)S(1)} %get-tuple-element.86), channel_id=1, source_target_pairs={{0,16},{2,18},{4,20},{6,22},{8,24},{10,26},{12,28},{14,30},{16,0},... | collective-permute-start | bytes 491528 | tf_op jit(solution)/shard_map/ppermute | solution.py:41
  105.7 7.0 %collective-permute-start.23 = (f32[136,128]{1,0:T(8,128)S(1)}, f32[136,128]{1,0:T(8,128)S(1)}, u32[]{:S(2)}, u32[]{:S(2)}) collective-permute-start(f32[136,128]{1,0:T(8,128)S(1)} %add_add_fusion.1), channel_id=1, source_target_pairs={{0,24},{2,26},{4,28},{6,30},{8,16},{10,18},{12,20},{14,22},{16,8},... | collective-permute-start | bytes 208904 | tf_op jit(solution)/shard_map/ppermute | solution.py:41
  107.2 7.1 %collective-permute-start.22 = (f32[136,128]{1,0:T(8,128)S(1)}, f32[136,128]{1,0:T(8,128)S(1)}, u32[]{:S(2)}, u32[]{:S(2)}) collective-permute-start(f32[136,128]{1,0:T(8,128)S(1)} %add_add_fusion.1), channel_id=1, source_target_pairs={{0,16},{2,18},{4,20},{6,22},{8,24},{10,26},{12,28},{14,30},{16,0},... | collective-permute-start | bytes 208904 | tf_op jit(solution)/shard_map/ppermute | solution.py:41
  107.4 6.9 %collective-permute-start.21 = (f32[136,128]{1,0:T(8,128)S(1)}, f32[136,128]{1,0:T(8,128)S(1)}, u32[]{:S(2)}, u32[]{:S(2)}) collective-permute-start(f32[136,128]{1,0:T(8,128)S(1)} %add_add_fusion.1), channel_id=1, source_target_pairs={{0,8},{2,10},{4,12},{6,14},{8,0},{10,2},{12,4},{14,6},{16,24},{18,... | collective-permute-start | bytes 208904 | tf_op jit(solution)/shard_map/ppermute | solution.py:41
  131.0 9.0 %collective-permute-start.28 = (f32[256,128]{1,0:T(8,128)S(1)}, f32[256,128]{1,0:T(8,128)S(1)}, u32[]{:S(2)}, u32[]{:S(2)}) collective-permute-start(f32[256,128]{1,0:T(8,128)S(1)} %get-tuple-element.96.refs_0_), channel_id=1, source_target_pairs={{0,16},{2,18},{4,20},{6,22},{8,24},{10,26},{12,28},{14,30},{16,0},... | collective-permute-start | bytes 393224 | tf_op jit(solution)/shard_map/ppermute | solution.py:41
  140.6 6.0 %collective-permute-start.31 = (f32[192,128]{1,0:T(8,128)S(1)}, f32[192,128]{1,0:T(8,128)S(1)}, u32[]{:S(2)}, u32[]{:S(2)}) collective-permute-start(f32[192,128]{1,0:T(8,128)S(1)} %get-tuple-element.99.refs_2_), channel_id=1, source_target_pairs={{0,8},{2,10},{4,12},{6,14},{8,0},{10,2},{12,4},{14,6},{16,24},{18,... | collective-permute-start | bytes 294920 | tf_op jit(solution)/shard_map/ppermute | solution.py:41
  147.2 6.8 %collective-permute-start.33 = (f32[384,128]{1,0:T(8,128)S(1)}, f32[384,128]{1,0:T(8,128)S(1)}, u32[]{:S(2)}, u32[]{:S(2)}) collective-permute-start(f32[384,128]{1,0:T(8,128)S(1)} %get-tuple-element.101.refs_1_), channel_id=1, source_target_pairs={{0,4},{2,6},{4,0},{6,2},{8,12},{10,14},{12,8},{14,10},{16,20},{18,... | collective-permute-start | bytes 589832 | tf_op jit(solution)/shard_map/ppermute | solution.py:41
  154.6 10.2 %collective-permute-start.35 = (f32[768,128]{1,0:T(8,128)S(1)}, f32[768,128]{1,0:T(8,128)S(1)}, u32[]{:S(2)}, u32[]{:S(2)}) collective-permute-start(f32[768,128]{1,0:T(8,128)S(1)} %get-tuple-element.103.refs_4_.refs_3_), channel_id=1, source_target_pairs={{0,2},{2,0},{4,6},{6,4},{8,10},{10,8},{12,14},{14,12},{16,18},{18,... | collective-permute-start | bytes 1179656 | tf_op jit(solution)/shard_map/ppermute | solution.py:41
  155.9 8.9 %collective-permute-start.36 = (f32[640,128]{1,0:T(8,128)S(1)}, f32[640,128]{1,0:T(8,128)S(1)}, u32[]{:S(2)}, u32[]{:S(2)}) collective-permute-start(f32[640,128]{1,0:T(8,128)S(1)} %get-tuple-element.104.refs_5_.refs_4_), channel_id=1, source_target_pairs={{0,4},{2,6},{4,0},{6,2},{8,12},{10,14},{12,8},{14,10},{16,20},{18,... | collective-permute-start | bytes 983048 | tf_op jit(solution)/shard_map/ppermute | solution.py:41
  157.3 7.5 %collective-permute-start.37 = (f32[640,128]{1,0:T(8,128)S(1)}, f32[640,128]{1,0:T(8,128)S(1)}, u32[]{:S(2)}, u32[]{:S(2)}) collective-permute-start(f32[640,128]{1,0:T(8,128)S(1)} %get-tuple-element.105.refs_6_.refs_5_), channel_id=1, source_target_pairs={{0,8},{2,10},{4,12},{6,14},{8,0},{10,2},{12,4},{14,6},{16,24},{18,... | collective-permute-start | bytes 983048 | tf_op jit(solution)/shard_map/ppermute | solution.py:41
  (23 other events, 121.8 us)

commit v4 on v3

--- a/solution.py
+++ b/solution.py
@@ -11,14 +11,15 @@
 BLOCK = 128
 
 SHARES = (
-    (5, (2, 0, 1, 3)),
+    (3, (0, 2, 3, 1)),
+    (4, (2, 0, 1, 3)),
     (3, (0, 1, 3, 2)),
-    (3, (0, 1, 3, 2)),
-    (5, (1, 2, 0, 3)),
+    (3, (1, 2, 0, 3)),
+    (3, (1, 3, 0, 2)),
 )
 BACK = {0: (3, 2, 1, 0), 1: (3, 0, 2, 1), 2: (3, 1, 0, 2)}
-ARRIVALS = (1, 3, 0, 2, 1, 3, 2, 1, 0, 3, 1, 2, 0, 2, 3, 0)
-TURNS = (3, 1, 0, 2)
+ARRIVALS = (0, 4, 1, 2, 3, 0, 4, 1, 2, 4, 0, 3, 1, 0, 2, 3, 4, 1, 2, 3)
+TURNS = (0, 4, 2, 1, 3)
 
 precise = lax.Precision.HIGHEST
 epsilon = 1e-05

time: 169 us -> 165 us (0.976)
  Pallas kernels: 47.5 us -> 39.9 us
  starting transfers between devices: 48.5 us -> 53.5 us
  waiting for transfers between devices: 66.6 us -> 63.3 us
    pallas_call x16 -> x20, Pallas kernels: 9.47 us -> 2 us  [join(): kernel_call(kernel, out_shape=shapes, in_specs=specs(*places, *[pl.ANY] *...]
    ppermute x38 -> x42, starting transfers between devices: 48.5 us -> 53.5 us  [flip(): return lax.ppermute(value, axis, [(i, i ^ mask) for i in range(size)])]
    ppermute x38 -> x42, waiting for transfers between devices: 66.6 us -> 63.3 us  [flip(): return lax.ppermute(value, axis, [(i, i ^ mask) for i in range(size)])]
  transfers between devices with their start and end apart: 38 -> 42, of which waited for: 24 -> 25; matrix products, arithmetic and copies ran while one was open for 0% -> 1% of each run, Pallas kernels for 16% -> 12%
where the time goes in v4:
time: 165 us
  waiting for transfers between devices  63.3 us (38%)
  starting transfers between devices  53.5 us (32%)
  Pallas kernels  39.9 us (24%)
  local copies, waits for them, and re-layouts  4.28 us (3%)
  blocking collectives  2.37 us (1%)
    ppermute x42, waiting for transfers between devices, flip(): return lax.ppermute(value, axis, [(i, i ^ mask) for i in range(size)])  63.3 us
    ppermute x42, starting transfers between devices, flip(): return lax.ppermute(value, axis, [(i, i ^ mask) for i in range(size)])  53.5 us
    pallas_call x2, Pallas kernels, merge(): kernel_call(functools.partial(merge_kernel, counts, leaves, depth), out_s...  9.44 us
    pallas_call x1, Pallas kernels, first_pass(): kernel_call(functools.partial(first_kernel, plan, replicas), out_shape=sh...  7.81 us
    pallas_call x1, Pallas kernels, error_rows(): kernel_call(functools.partial(error_kernel, plan, replicas), out_shape=(j...  5.62 us
    pallas_call x1, Pallas kernels, second_pass(): pair(weight_kernel, out_shape=(half, half))(*near(plain, gram_matrix))  4.81 us
    pallas_call x1, Pallas kernels, last_rows(): kernel_call(functools.partial(last_error_kernel, plan, replicas), out_sha...  3.92 us
  transfers between devices with their start and end apart: 42, of which 25 were waited for; matrix products, arithmetic and copies ran while one was open for 1% of the time, Pallas kernels for 12%

profile of v4, /device:TPU:0, one launch (start us, length us, event | category | flops | bytes accessed | tf_op | source)
XLA Modules:
  0.0 164.8 jit_solution(9249589638778431132)
XLA Ops:
  4.9 4.8 %shard_map.96 = (f32[384,512]{1,0:T(8,128)}, f32[512,512]{1,0:T(8,128)}, f32[384,512]{1,0:T(8,128)}, f32[384,512]{1,0:T(8,128)}, f32[384,512]{1,0:T(8,128)}) custom-call(s32[5]{0:T(128)S(1)} %stack.78.starts_ref, bf16[256,4096]{1,0:T(8,128)(2,1)} %tokens_ref.5, f32[256,128]{1,0:T(8,128)S(1)} %add.79.squares_ref, ...), custom_call_target="tpu_custom_call" | custom-call | flops 536870912 | bytes 9437184 | tf_op jit(solution)/shard_map/pallas_call | solution.py:229
  9.6 3.0 %collective-permute-start.4 = (f32[512,512]{1,0:T(8,128)}, f32[512,512]{1,0:T(8,128)S(1)}, u32[]{:S(2)}, u32[]{:S(2)}) collective-permute-start(f32[512,512]{1,0:T(8,128)} %get-tuple-element.74.refs_1_), channel_id=1, source_target_pairs={{0,8},{2,10},{4,12},{6,14},{8,0},{10,2},{12,4},{14,6},{16,24},{18,... | collective-permute-start | bytes 3145736 | tf_op jit(solution)/shard_map/ppermute | solution.py:42
  17.4 2.4 %all_gather.3.refs_0_.basis_ref = f32[512,128]{1,0:T(8,128)S(1)} all-gather(f32[256,128]{1,0:T(8,128)} %param.11), channel_id=1, replica_groups=mesh['rep'=16,'mp'=2] {'mp'}, dimensions={0}, use_global_device_ids=true | all-gather | bytes 393216 | tf_op jit(solution)/shard_map/all_gather | solution.py:671
  21.4 4.7 %shard_map.95 = (f32[384,512]{1,0:T(8,128)S(1)}, f32[512,512]{1,0:T(8,128)S(1)}, f32[384,512]{1,0:T(8,128)S(1)}, f32[384,512]{1,0:T(8,128)S(1)}, f32[384,512]{1,0:T(8,128)S(1)}, /*index=5*/f32[2048,512]{1,0:T(8,128)}) custom-call(s32[5]{0:T(128)S(1)} %copy-done.6, bf16[256,4096]{1,0:T(8,128)(2,1)} %tokens_ref.5, f32[256,128]{1,0:T(8,128)S(1)} %add.79.squares_ref, ...), custom_call_target="tpu_custom_call" | custom-call | flops 536870912 | bytes 9437184 | tf_op jit(solution)/shard_map/pallas_call | solution.py:229
  26.1 7.2 %collective-permute-done.1.got_ref.refs_0_ = f32[384,512]{1,0:T(8,128)S(1)} collective-permute-done((f32[384,512]{1,0:T(8,128)}, f32[384,512]{1,0:T(8,128)S(1)}, u32[]{:S(2)}, u32[]{:S(2)}) %collective-permute-start.1) | collective-permute-done | bytes 786464 | tf_op jit(solution)/shard_map/ppermute | solution.py:42
  39.7 2.6 %collective-permute-start.8 = (f32[192,512]{1,0:T(8,128)S(1)}, f32[192,512]{1,0:T(8,128)S(1)}, u32[]{:S(2)}, u32[]{:S(2)}) collective-permute-start(f32[192,512]{1,0:T(8,128)S(1)} %get-tuple-element.83), channel_id=1, source_target_pairs={{0,16},{2,18},{4,20},{6,22},{8,24},{10,26},{12,28},{14,30},{16,0},... | collective-permute-start | bytes 1179656 | tf_op jit(solution)/shard_map/ppermute | solution.py:42
  42.3 7.8 %collective-permute-done.6.got_ref.refs_0_ = f32[384,512]{1,0:T(8,128)S(1)} collective-permute-done((f32[384,512]{1,0:T(8,128)}, f32[384,512]{1,0:T(8,128)S(1)}, u32[]{:S(2)}, u32[]{:S(2)}) %collective-permute-start.6) | collective-permute-done | bytes 786464 | tf_op jit(solution)/shard_map/ppermute | solution.py:42
  52.4 6.2 %collective-permute-done.2.got_ref.refs_0_ = f32[192,512]{1,0:T(8,128)S(1)} collective-permute-done((f32[192,512]{1,0:T(8,128)S(1)}, f32[192,512]{1,0:T(8,128)S(1)}, u32[]{:S(2)}, u32[]{:S(2)}) %collective-permute-start.2) | collective-permute-done | bytes 393248 | tf_op jit(solution)/shard_map/ppermute | solution.py:42
  59.2 2.6 %collective-permute-start.7 = (f32[96,512]{1,0:T(8,128)S(1)}, f32[96,512]{1,0:T(8,128)S(1)}, u32[]{:S(2)}, u32[]{:S(2)}) collective-permute-start(f32[96,512]{1,0:T(8,128)S(1)} %get-tuple-element.82), channel_id=1, source_target_pairs={{0,16},{2,18},{4,20},{6,22},{8,24},{10,26},{12,28},{14,30},{16,0},... | collective-permute-start | bytes 589832 | tf_op jit(solution)/shard_map/ppermute | solution.py:42
  63.5 2.2 %collective-permute-start.17 = (f32[96,512]{1,0:T(8,128)S(1)}, f32[96,512]{1,0:T(8,128)S(1)}, u32[]{:S(2)}, u32[]{:S(2)}) collective-permute-start(f32[96,512]{1,0:T(8,128)S(1)} %get-tuple-element.99), channel_id=1, source_target_pairs={{0,16},{2,18},{4,20},{6,22},{8,24},{10,26},{12,28},{14,30},{16,0},... | collective-permute-start | bytes 589832 | tf_op jit(solution)/shard_map/ppermute | solution.py:42
  65.7 11.5 %collective-permute-done.7.got_ref.refs_0_ = f32[96,512]{1,0:T(8,128)S(1)} collective-permute-done((f32[96,512]{1,0:T(8,128)S(1)}, f32[96,512]{1,0:T(8,128)S(1)}, u32[]{:S(2)}, u32[]{:S(2)}) %collective-permute-start.7) | collective-permute-done | bytes 196640 | tf_op jit(solution)/shard_map/ppermute | solution.py:42
  81.1 2.9 %collective-permute-start.16 = (f32[48,512]{1,0:T(8,128)S(1)}, f32[48,512]{1,0:T(8,128)S(1)}, u32[]{:S(2)}, u32[]{:S(2)}) collective-permute-start(f32[48,512]{1,0:T(8,128)S(1)} %get-tuple-element.98), channel_id=1, source_target_pairs={{0,8},{2,10},{4,12},{6,14},{8,0},{10,2},{12,4},{14,6},{16,24},{18,... | collective-permute-start | bytes 294920 | tf_op jit(solution)/shard_map/ppermute | solution.py:42
  84.3 2.8 %collective-permute-start.18 = (f32[48,512]{1,0:T(8,128)S(1)}, f32[48,512]{1,0:T(8,128)S(1)}, u32[]{:S(2)}, u32[]{:S(2)}) collective-permute-start(f32[48,512]{1,0:T(8,128)S(1)} %get-tuple-element.101), channel_id=1, source_target_pairs={{0,8},{2,10},{4,12},{6,14},{8,0},{10,2},{12,4},{14,6},{16,24},{18,... | collective-permute-start | bytes 294920 | tf_op jit(solution)/shard_map/ppermute | solution.py:42
  88.1 2.3 %collective-permute-done.20.got_ref = f32[48,512]{1,0:T(8,128)S(1)} collective-permute-done((f32[48,512]{1,0:T(8,128)S(1)}, f32[48,512]{1,0:T(8,128)S(1)}, u32[]{:S(2)}, u32[]{:S(2)}) %collective-permute-start.20) | collective-permute-done | bytes 98336 | tf_op jit(solution)/shard_map/ppermute | solution.py:42
  97.8 3.1 %collective-permute-done.24 = f32[136,128]{1,0:T(8,128)S(1)} collective-permute-done((f32[136,128]{1,0:T(8,128)S(1)}, f32[136,128]{1,0:T(8,128)S(1)}, u32[]{:S(2)}, u32[]{:S(2)}) %collective-permute-start.24) | collective-permute-done | bytes 69664 | tf_op jit(solution)/shard_map/ppermute | solution.py:42
  101.9 2.1 %collective-permute-start.27 = (f32[136,128]{1,0:T(8,128)S(1)}, f32[136,128]{1,0:T(8,128)S(1)}, u32[]{:S(2)}, u32[]{:S(2)}) collective-permute-start(f32[136,128]{1,0:T(8,128)S(1)} %add_add_fusion.1), channel_id=1, source_target_pairs={{0,24},{2,26},{4,28},{6,30},{8,16},{10,18},{12,20},{14,22},{16,8},... | collective-permute-start | bytes 208904 | tf_op jit(solution)/shard_map/ppermute | solution.py:42
  106.3 2.0 %collective-permute-done.27 = f32[136,128]{1,0:T(8,128)S(1)} collective-permute-done((f32[136,128]{1,0:T(8,128)S(1)}, f32[136,128]{1,0:T(8,128)S(1)}, u32[]{:S(2)}, u32[]{:S(2)}) %collective-permute-start.27) | collective-permute-done | bytes 69664 | tf_op jit(solution)/shard_map/ppermute | solution.py:42
  108.4 2.8 %collective-permute-done.26 = f32[136,128]{1,0:T(8,128)S(1)} collective-permute-done((f32[136,128]{1,0:T(8,128)S(1)}, f32[136,128]{1,0:T(8,128)S(1)}, u32[]{:S(2)}, u32[]{:S(2)}) %collective-permute-start.26) | collective-permute-done | bytes 69664 | tf_op jit(solution)/shard_map/ppermute | solution.py:42
  119.9 7.8 %shard_map.118 = (f32[512,512]{1,0:T(8,128)S(1)}, f32[512,128]{1,0:T(8,128)S(1)}, f32[256,128]{1,0:T(8,128)S(1)}) custom-call(f32[1088,128]{1,0:T(8,128)S(1)} %constant_dynamic-update-slice_fusion.packed_ref, f32[512,128]{1,0:T(8,128)S(1)} %copy-done.1, f32[48,512]{1,0:T(8,128)S(1)} %shard_map.108.refs_1_.refs_0_, f32[64,512]{1,0:T(8,128)S(1)} %shard_map.111.refs_1_, ...), custom_call_target="tpu_custom_call" | custom-call | tf_op jit(solution)/shard_map/pallas_call | solution.py:460
  130.2 4.8 %shard_map.120 = (bf16[128,512]{1,0:T(8,128)(2,1)S(1)}, bf16[128,512]{1,0:T(8,128)(2,1)S(1)}) custom-call(f32[512,128]{1,0:T(8,128)S(1)} %get-tuple-element.107.plain_ref, f32[128,128]{1,0:T(8,128)S(1)} %get-tuple-element.108.gram_ref), custom_call_target="tpu_custom_call" | custom-call | tf_op jit(solution)/shard_map/pallas_call | solution.py:494
  139.5 2.9 %collective-permute-done.34.refs_4_ = f32[128,128]{1,0:T(8,128)S(1)} collective-permute-done((f32[128,128]{1,0:T(8,128)S(1)}, f32[128,128]{1,0:T(8,128)S(1)}, u32[]{:S(2)}, u32[]{:S(2)}) %collective-permute-start.34) | collective-permute-done | bytes 65568 | tf_op jit(solution)/shard_map/ppermute | solution.py:42
  147.1 4.0 %collective-permute-done.36.refs_3_ = f32[256,128]{1,0:T(8,128)S(1)} collective-permute-done((f32[256,128]{1,0:T(8,128)S(1)}, f32[256,128]{1,0:T(8,128)S(1)}, u32[]{:S(2)}, u32[]{:S(2)}) %collective-permute-start.36) | collective-permute-done | bytes 131104 | tf_op jit(solution)/shard_map/ppermute | solution.py:42
  154.5 5.6 %shard_map.124 = (f32[4096,512]{1,0:T(8,128)}, f32[2048,512]{1,0:T(8,128)S(1)}) custom-call(s32[5]{0:T(128)S(1)} %copy-done.7, bf16[128,512]{1,0:T(8,128)(2,1)S(1)} %get-tuple-element.109.refs_2_.refs_6_.high_ref, bf16[128,512]{1,0:T(8,128)(2,1)S(1)} %get-tuple-element.110.low_ref, f32[2048,512]{1,0:T(8,128)} %get-tuple-element.111.own_ref, ...), custom_call_target="tpu_custom_call" | custom-call | flops 805306368 | bytes 8388608 | tf_op jit(solution)/shard_map/pallas_call | solution.py:602
  160.7 3.9 %shard_map.125 = (f32[4096,512]{1,0:T(8,128)}, f32[256,512]{1,0:T(8,128)}, f32[256,512]{1,0:T(8,128)}) custom-call(s32[11]{0:T(128)S(1)} %stack.76.starts_ref, bf16[128,512]{1,0:T(8,128)(2,1)S(1)} %get-tuple-element.109.refs_2_.refs_6_.high_ref, bf16[128,512]{1,0:T(8,128)(2,1)S(1)} %get-tuple-element.110.low_ref, ...), custom_call_target="tpu_custom_call", output_to_operand_aliasing={{0}: (12, {})} | custom-call | flops 805306368 | bytes 8388608 | tf_op jit(solution)/shard_map/pallas_call | solution.py:627
  (126 shorter events, 61.7 us)
Async XLA Ops:
  9.6 26.7 %collective-permute-start.4 = (f32[512,512]{1,0:T(8,128)}, f32[512,512]{1,0:T(8,128)S(1)}, u32[]{:S(2)}, u32[]{:S(2)}) collective-permute-start(f32[512,512]{1,0:T(8,128)} %get-tuple-element.74.refs_1_), channel_id=1, source_target_pairs={{0,8},{2,10},{4,12},{6,14},{8,0},{10,2},{12,4},{14,6},{16,24},{18,... | collective-permute-start | bytes 3145736 | tf_op jit(solution)/shard_map/ppermute | solution.py:42
  12.6 20.6 %collective-permute-start.1 = (f32[384,512]{1,0:T(8,128)}, f32[384,512]{1,0:T(8,128)S(1)}, u32[]{:S(2)}, u32[]{:S(2)}) collective-permute-start(f32[384,512]{1,0:T(8,128)} %get-tuple-element.66.refs_0_), channel_id=1, source_target_pairs={{0,2},{2,0},{4,6},{6,4},{8,10},{10,8},{12,14},{14,12},{16,18},{18,... | collective-permute-start | bytes 2359304 | tf_op jit(solution)/shard_map/ppermute | solution.py:42
  14.1 20.8 %collective-permute-start.5 = (f32[384,512]{1,0:T(8,128)}, f32[384,512]{1,0:T(8,128)}, u32[]{:S(2)}, u32[]{:S(2)}) collective-permute-start(f32[384,512]{1,0:T(8,128)} %get-tuple-element.75.refs_4_), channel_id=1, source_target_pairs={{0,4},{2,6},{4,0},{6,2},{8,12},{10,14},{12,8},{14,10},{16,20},{18,... | collective-permute-start | bytes 2359304 | tf_op jit(solution)/shard_map/ppermute | solution.py:42
  15.6 34.5 %collective-permute-start.6 = (f32[384,512]{1,0:T(8,128)}, f32[384,512]{1,0:T(8,128)S(1)}, u32[]{:S(2)}, u32[]{:S(2)}) collective-permute-start(f32[384,512]{1,0:T(8,128)} %get-tuple-element.78.refs_2_), channel_id=1, source_target_pairs={{0,2},{2,0},{4,6},{6,4},{8,10},{10,8},{12,14},{14,12},{16,18},{18,... | collective-permute-start | bytes 2359304 | tf_op jit(solution)/shard_map/ppermute | solution.py:42
  16.2 35.6 %collective-permute-start.3 = (f32[384,512]{1,0:T(8,128)}, f32[384,512]{1,0:T(8,128)S(1)}, u32[]{:S(2)}, u32[]{:S(2)}) collective-permute-start(f32[384,512]{1,0:T(8,128)} %get-tuple-element.73.refs_3_), channel_id=1, source_target_pairs={{0,4},{2,6},{4,0},{6,2},{8,12},{10,14},{12,8},{14,10},{16,20},{18,... | collective-permute-start | bytes 2359304 | tf_op jit(solution)/shard_map/ppermute | solution.py:42
  36.4 25.4 %collective-permute-start.10 = (f32[256,512]{1,0:T(8,128)S(1)}, f32[256,512]{1,0:T(8,128)S(1)}, u32[]{:S(2)}, u32[]{:S(2)}) collective-permute-start(f32[256,512]{1,0:T(8,128)S(1)} %get-tuple-element.85), channel_id=1, source_target_pairs={{0,2},{2,0},{4,6},{6,4},{8,10},{10,8},{12,14},{14,12},{16,18},{18,... | collective-permute-start | bytes 1572872 | tf_op jit(solution)/shard_map/ppermute | solution.py:42
  38.1 20.5 %collective-permute-start.2 = (f32[192,512]{1,0:T(8,128)S(1)}, f32[192,512]{1,0:T(8,128)S(1)}, u32[]{:S(2)}, u32[]{:S(2)}) collective-permute-start(f32[192,512]{1,0:T(8,128)S(1)} %get-tuple-element.72), channel_id=1, source_target_pairs={{0,8},{2,10},{4,12},{6,14},{8,0},{10,2},{12,4},{14,6},{16,24},{18,... | collective-permute-start | bytes 1179656 | tf_op jit(solution)/shard_map/ppermute | solution.py:42
  39.7 18.9 %collective-permute-start.8 = (f32[192,512]{1,0:T(8,128)S(1)}, f32[192,512]{1,0:T(8,128)S(1)}, u32[]{:S(2)}, u32[]{:S(2)}) collective-permute-start(f32[192,512]{1,0:T(8,128)S(1)} %get-tuple-element.83), channel_id=1, source_target_pairs={{0,16},{2,18},{4,20},{6,22},{8,24},{10,26},{12,28},{14,30},{16,0},... | collective-permute-start | bytes 1179656 | tf_op jit(solution)/shard_map/ppermute | solution.py:42
  50.2 13.2 %collective-permute-start.11 = (f32[192,512]{1,0:T(8,128)S(1)}, f32[192,512]{1,0:T(8,128)S(1)}, u32[]{:S(2)}, u32[]{:S(2)}) collective-permute-start(f32[192,512]{1,0:T(8,128)S(1)} %get-tuple-element.88), channel_id=1, source_target_pairs={{0,4},{2,6},{4,0},{6,2},{8,12},{10,14},{12,8},{14,10},{16,20},{18,... | collective-permute-start | bytes 1179656 | tf_op jit(solution)/shard_map/ppermute | solution.py:42
  51.9 25.3 %collective-permute-start.14 = (f32[192,512]{1,0:T(8,128)S(1)}, f32[192,512]{1,0:T(8,128)S(1)}, u32[]{:S(2)}, u32[]{:S(2)}) collective-permute-start(f32[192,512]{1,0:T(8,128)S(1)} %get-tuple-element.94), channel_id=1, source_target_pairs={{0,8},{2,10},{4,12},{6,14},{8,0},{10,2},{12,4},{14,6},{16,24},{18,... | collective-permute-start | bytes 1179656 | tf_op jit(solution)/shard_map/ppermute | solution.py:42
  58.7 7.0 %collective-permute-start.9 = (f32[96,512]{1,0:T(8,128)S(1)}, f32[96,512]{1,0:T(8,128)S(1)}, u32[]{:S(2)}, u32[]{:S(2)}) collective-permute-start(f32[96,512]{1,0:T(8,128)S(1)} %get-tuple-element.84), channel_id=1, source_target_pairs={{0,2},{2,0},{4,6},{6,4},{8,10},{10,8},{12,14},{14,12},{16,18},{18,... | collective-permute-start | bytes 589832 | tf_op jit(solution)/shard_map/ppermute | solution.py:42
  59.2 18.0 %collective-permute-start.7 = (f32[96,512]{1,0:T(8,128)S(1)}, f32[96,512]{1,0:T(8,128)S(1)}, u32[]{:S(2)}, u32[]{:S(2)}) collective-permute-start(f32[96,512]{1,0:T(8,128)S(1)} %get-tuple-element.82), channel_id=1, source_target_pairs={{0,16},{2,18},{4,20},{6,22},{8,24},{10,26},{12,28},{14,30},{16,0},... | collective-permute-start | bytes 589832 | tf_op jit(solution)/shard_map/ppermute | solution.py:42
  61.8 19.2 %collective-permute-start.13 = (f32[128,512]{1,0:T(8,128)S(1)}, f32[128,512]{1,0:T(8,128)S(1)}, u32[]{:S(2)}, u32[]{:S(2)}) collective-permute-start(f32[128,512]{1,0:T(8,128)S(1)} %get-tuple-element.93), channel_id=1, source_target_pairs={{0,4},{2,6},{4,0},{6,2},{8,12},{10,14},{12,8},{14,10},{16,20},{18,... | collective-permute-start | bytes 786440 | tf_op jit(solution)/shard_map/ppermute | solution.py:42
  63.5 20.6 %collective-permute-start.17 = (f32[96,512]{1,0:T(8,128)S(1)}, f32[96,512]{1,0:T(8,128)S(1)}, u32[]{:S(2)}, u32[]{:S(2)}) collective-permute-start(f32[96,512]{1,0:T(8,128)S(1)} %get-tuple-element.99), channel_id=1, source_target_pairs={{0,16},{2,18},{4,20},{6,22},{8,24},{10,26},{12,28},{14,30},{16,0},... | collective-permute-start | bytes 589832 | tf_op jit(solution)/shard_map/ppermute | solution.py:42
  77.3 6.9 %collective-permute-start.19 = (f32[96,512]{1,0:T(8,128)S(1)}, f32[96,512]{1,0:T(8,128)S(1)}, u32[]{:S(2)}, u32[]{:S(2)}) collective-permute-start(f32[96,512]{1,0:T(8,128)S(1)} %get-tuple-element.102), channel_id=1, source_target_pairs={{0,2},{2,0},{4,6},{6,4},{8,10},{10,8},{12,14},{14,12},{16,18},{18,... | collective-permute-start | bytes 589832 | tf_op jit(solution)/shard_map/ppermute | solution.py:42
  81.1 9.7 %collective-permute-start.15 = (f32[64,512]{1,0:T(8,128)S(1)}, f32[64,512]{1,0:T(8,128)S(1)}, u32[]{:S(2)}, u32[]{:S(2)}) collective-permute-start(f32[64,512]{1,0:T(8,128)S(1)} %get-tuple-element.97), channel_id=1, source_target_pairs={{0,16},{2,18},{4,20},{6,22},{8,24},{10,26},{12,28},{14,30},{16,0},... | collective-permute-start | bytes 393224 | tf_op jit(solution)/shard_map/ppermute | solution.py:42
  81.1 6.9 %collective-permute-start.16 = (f32[48,512]{1,0:T(8,128)S(1)}, f32[48,512]{1,0:T(8,128)S(1)}, u32[]{:S(2)}, u32[]{:S(2)}) collective-permute-start(f32[48,512]{1,0:T(8,128)S(1)} %get-tuple-element.98), channel_id=1, source_target_pairs={{0,8},{2,10},{4,12},{6,14},{8,0},{10,2},{12,4},{14,6},{16,24},{18,... | collective-permute-start | bytes 294920 | tf_op jit(solution)/shard_map/ppermute | solution.py:42
  101.9 6.5 %collective-permute-start.27 = (f32[136,128]{1,0:T(8,128)S(1)}, f32[136,128]{1,0:T(8,128)S(1)}, u32[]{:S(2)}, u32[]{:S(2)}) collective-permute-start(f32[136,128]{1,0:T(8,128)S(1)} %add_add_fusion.1), channel_id=1, source_target_pairs={{0,24},{2,26},{4,28},{6,30},{8,16},{10,18},{12,20},{14,22},{16,8},... | collective-permute-start | bytes 208904 | tf_op jit(solution)/shard_map/ppermute | solution.py:42
  104.0 7.1 %collective-permute-start.26 = (f32[136,128]{1,0:T(8,128)S(1)}, f32[136,128]{1,0:T(8,128)S(1)}, u32[]{:S(2)}, u32[]{:S(2)}) collective-permute-start(f32[136,128]{1,0:T(8,128)S(1)} %add_add_fusion.1), channel_id=1, source_target_pairs={{0,16},{2,18},{4,20},{6,22},{8,24},{10,26},{12,28},{14,30},{16,0},... | collective-permute-start | bytes 208904 | tf_op jit(solution)/shard_map/ppermute | solution.py:42
  127.7 8.6 %collective-permute-start.32 = (f32[256,128]{1,0:T(8,128)S(1)}, f32[256,128]{1,0:T(8,128)S(1)}, u32[]{:S(2)}, u32[]{:S(2)}) collective-permute-start(f32[256,128]{1,0:T(8,128)S(1)} %get-tuple-element.112.refs_0_), channel_id=1, source_target_pairs={{0,16},{2,18},{4,20},{6,22},{8,24},{10,26},{12,28},{14,30},{16,0},... | collective-permute-start | bytes 393224 | tf_op jit(solution)/shard_map/ppermute | solution.py:42
  143.1 8.0 %collective-permute-start.37 = (f32[384,128]{1,0:T(8,128)S(1)}, f32[384,128]{1,0:T(8,128)S(1)}, u32[]{:S(2)}, u32[]{:S(2)}) collective-permute-start(f32[384,128]{1,0:T(8,128)S(1)} %get-tuple-element.117.refs_1_), channel_id=1, source_target_pairs={{0,4},{2,6},{4,0},{6,2},{8,12},{10,14},{12,8},{14,10},{16,20},{18,... | collective-permute-start | bytes 589832 | tf_op jit(solution)/shard_map/ppermute | solution.py:42
  144.4 6.7 %collective-permute-start.38 = (f32[384,128]{1,0:T(8,128)S(1)}, f32[384,128]{1,0:T(8,128)S(1)}, u32[]{:S(2)}, u32[]{:S(2)}) collective-permute-start(f32[384,128]{1,0:T(8,128)S(1)} %get-tuple-element.118.refs_2_), channel_id=1, source_target_pairs={{0,8},{2,10},{4,12},{6,14},{8,0},{10,2},{12,4},{14,6},{16,24},{18,... | collective-permute-start | bytes 589832 | tf_op jit(solution)/shard_map/ppermute | solution.py:42
  151.7 8.4 %collective-permute-start.39 = (f32[768,128]{1,0:T(8,128)S(1)}, f32[768,128]{1,0:T(8,128)S(1)}, u32[]{:S(2)}, u32[]{:S(2)}) collective-permute-start(f32[768,128]{1,0:T(8,128)S(1)} %get-tuple-element.119.refs_5_.refs_3_), channel_id=1, source_target_pairs={{0,2},{2,0},{4,6},{6,4},{8,10},{10,8},{12,14},{14,12},{16,18},{18,... | collective-permute-start | bytes 1179656 | tf_op jit(solution)/shard_map/ppermute | solution.py:42
  152.8 7.9 %collective-permute-start.40 = (f32[768,128]{1,0:T(8,128)S(1)}, f32[768,128]{1,0:T(8,128)S(1)}, u32[]{:S(2)}, u32[]{:S(2)}) collective-permute-start(f32[768,128]{1,0:T(8,128)S(1)} %get-tuple-element.120.refs_6_.refs_4_), channel_id=1, source_target_pairs={{0,4},{2,6},{4,0},{6,2},{8,12},{10,14},{12,8},{14,10},{16,20},{18,... | collective-permute-start | bytes 1179656 | tf_op jit(solution)/shard_map/ppermute | solution.py:42
  (26 other events, 317.8 us)

commit v5 on v4

--- a/solution.py
+++ b/solution.py
@@ -141,7 +141,7 @@
     return high, (value - high.astype(jnp.float32)).astype(jnp.bfloat16)
 
 
-def squares_kernel(cuts, tokens_ref, out_ref, held_ref, sems):
+def squares_kernel(cuts, tokens_ref, grad_ref, out_ref, near_ref, held_ref, sems):
     copies = []
     for index, (start, size) in enumerate(cuts):
         at = pl.ds(start, size)
@@ -149,6 +149,8 @@
             pltpu.make_async_copy(tokens_ref.at[:, at], held_ref.at[:, at], sems.at[index])
         )
         copies[-1].start()
+    near_copy = pltpu.make_async_copy(grad_ref, near_ref, sems.at[len(cuts)])
+    near_copy.start()
     total = None
     for copy, (start, size) in zip(copies, cuts):
         copy.wait()
@@ -156,20 +158,21 @@
             wide = held_ref[:, place : place + BLOCK].astype(jnp.float32)
             total = wide * wide if total is None else total + wide * wide
     out_ref[...] = jnp.broadcast_to(jnp.sum(total, axis=1, keepdims=True), out_ref.shape)
-
-
-def squares(tokens):
+    near_copy.wait()
+
+
+def squares(tokens, grad):
     cuts = pieces_of(tokens.shape[1], max(BLOCK, tokens.shape[1] // 4))
     return kernel_call(
         functools.partial(squares_kernel, cuts),
-        out_shape=near_shape((tokens.shape[0], BLOCK)),
-        in_specs=specs(pltpu.HBM),
-        out_specs=specs(pltpu.VMEM)[0],
+        out_shape=(near_shape((tokens.shape[0], BLOCK)), near_shape(grad.shape, grad.dtype)),
+        in_specs=specs(pltpu.HBM, pltpu.HBM),
+        out_specs=tuple(specs(pltpu.VMEM, pltpu.VMEM)),
         scratch_shapes=[
             pltpu.VMEM(tokens.shape, tokens.dtype),
-            pltpu.SemaphoreType.DMA((len(cuts),)),
+            pltpu.SemaphoreType.DMA((len(cuts) + 1,)),
         ],
-    )(distant(tokens))
+    )(distant(tokens), distant(grad))
 
 
 def merge_kernel(
@@ -441,57 +444,79 @@
 
 
 def first_kernel(plan, replicas, packed_ref, basis_ref, *refs):
-    whole_ref, right_ref = refs[len(plan) : len(plan) + 2]
+    whole_ref, right_ref, gram_ref = refs[len(plan) : len(plan) + 3]
     unpack(packed_ref, whole_ref)
     basis = basis_ref[...]
     plain = contract(whole_ref[...], basis, (1, 0))
-    unit, diagonal = factor(contract(basis, plain, (0, 0)))
-    right = contract(plain, unit * lax.rsqrt(diagonal), (1, 1))
+    gram_matrix = contract(basis, plain, (0, 0))
+    row = lax.broadcasted_iota(jnp.int32, gram_matrix.shape, 0)
+    column = lax.broadcasted_iota(jnp.int32, gram_matrix.shape, 1)
+    diagonal = jnp.where(row == column, gram_matrix, 0.0)
+    across = lax.rsqrt(jnp.sum(diagonal, axis=0, keepdims=True))
+    gram_ref[...] = gram_matrix * across * lax.rsqrt(jnp.sum(diagonal, axis=1, keepdims=True))
+    right = plain * across
     right_ref[...] = right
     _, groups, _ = bundles(plan, 0)
-    for group, left_ref in zip(groups, refs[len(plan) + 2 :]):
+    for group, left_ref in zip(groups, refs[len(plan) + 3 :]):
         rows = jnp.concatenate([refs[s][...] for s in group], 0) / replicas
         left_ref[...] = contract(rows, right, (1, 0))
 
 
 def first_pass(plan, packed, basis, parts, replicas):
     width, rank = basis.shape
-    shapes = (near_shape((width, width)), near_shape((width, rank)), *bundle_shapes(plan, 0, rank))
-    whole, right, *lefts = kernel_call(
+    shapes = (
+        near_shape((width, width)),
+        near_shape((width, rank)),
+        near_shape((rank, rank)),
+        *bundle_shapes(plan, 0, rank),
+    )
+    whole, right, gram_matrix, *lefts = kernel_call(
         functools.partial(first_kernel, plan, replicas),
         out_shape=shapes,
         in_specs=specs(*[pltpu.VMEM] * (2 + len(parts))),
         out_specs=tuple(specs(*[pltpu.VMEM] * len(shapes))),
     )(*near(packed, basis, *parts))
-    return whole, right, lefts
-
-
-def product_kernel(whole_ref, right_ref, plain_ref, gram_ref):
-    right = right_ref[...]
+    return whole, right, gram_matrix, lefts
+
+
+def inverse_factor(matrix):
+    unit, diagonal = factor(matrix)
+    return unit * lax.rsqrt(diagonal)
+
+
+def product_kernel(whole_ref, right_ref, gram_ref, inverse_ref, plain_ref, second_ref):
+    inverse = inverse_factor(gram_ref[...])
+    inverse_ref[...] = inverse
+    right = contract(right_ref[...], inverse, (1, 1))
     plain = contract(whole_ref[...], right, (1, 0))
     plain_ref[...] = plain
-    gram_ref[...] = contract(right, plain, (0, 0))
-
-
-def weight_kernel(plain_ref, gram_ref, high_ref, low_ref):
-    unit, diagonal = factor(gram_ref[...])
-    inverse = unit * lax.rsqrt(diagonal)
+    second_ref[...] = contract(right, plain, (0, 0))
+
+
+def weight_kernel(first_ref, plain_ref, gram_ref, high_ref, low_ref):
+    inverse = inverse_factor(gram_ref[...])
     turned = contract(inverse, plain_ref[...], (1, 1))
-    high_ref[...], low_ref[...] = split(contract(inverse, turned, (0, 0)))
-
-
-def second_pass(whole, right):
+    weights = contract(first_ref[...], contract(inverse, turned, (0, 0)), (0, 0))
+    high_ref[...], low_ref[...] = split(weights)
+
+
+def second_pass(whole, right, gram_matrix):
     width, rank = right.shape
-    pair = functools.partial(
-        kernel_call,
-        in_specs=specs(pltpu.VMEM, pltpu.VMEM),
-        out_specs=tuple(specs(pltpu.VMEM, pltpu.VMEM)),
-    )
-    plain, gram_matrix = pair(
-        product_kernel, out_shape=(near_shape((width, rank)), near_shape((rank, rank)))
-    )(*near(whole, right))
+    square = near_shape((rank, rank))
+    inverse, plain, second = kernel_call(
+        product_kernel,
+        out_shape=(square, near_shape((width, rank)), square),
+        in_specs=specs(*[pltpu.VMEM] * 3),
+        out_specs=tuple(specs(*[pltpu.VMEM] * 3)),
+    )(*near(whole, right, gram_matrix))
     half = near_shape((rank, width), jnp.bfloat16)
-    return pair(weight_kernel, out_shape=(half, half))(*near(plain, gram_matrix))
+    weights = kernel_call(
+        weight_kernel,
+        out_shape=(half, half),
+        in_specs=specs(*[pltpu.VMEM] * 3),
+        out_specs=tuple(specs(*[pltpu.VMEM] * 2)),
+    )(*near(inverse, plain, second))
+    return second, weights
 
 
 def low_rank(left, high, low):
@@ -667,10 +692,11 @@
     steps = bit_count(replicas)
     depth = tokens_in.shape[1]
     error = error_in[0]
-    square_sums = sum_over(squares(tokens_in), "mp")
+    square_sums, grad = squares(tokens_in, key_grad)
+    square_sums = sum_over(square_sums, "mp")
     basis = lax.all_gather(basis_init, "mp", axis=0, tiled=True)
     sources = (
-        depth * lax.axis_size("mp"), tokens_in, square_sums, norm_gain[None, :], key_grad, error
+        depth * lax.axis_size("mp"), tokens_in, square_sums, norm_gain[None, :], grad, error
     )
 
     plan, turns, arrivals = stream_plan(replicas, depth // replicas)
@@ -698,15 +724,15 @@
         after = [came]
 
     packed = sum_everywhere(gram(parts, replicas, 32 * lax.axis_size("mp")))
-    whole, right, lefts = first_pass(plan, packed, basis, parts, replicas)
-    high, low = second_pass(whole, right)
+    whole, right, gram_matrix, lefts = first_pass(plan, packed, basis, parts, replicas)
+    second, (high, low) = second_pass(whole, right, gram_matrix)
 
     bit_sides = jnp.stack([bit_of("rep", bit) for bit in range(steps)]).astype(jnp.int32)
     for step in range(steps):
         bits, _, _ = bundles(plan, step)
         others = [flip(left, "rep", 1 << bit) for left, bit in zip(lefts, bits)]
         if step + 1 < steps:
-            lefts = gather_step(plan, step, bit_sides, lefts, others, [high])
+            lefts = gather_step(plan, step, bit_sides, lefts, others, [high if step + 2 >= steps else second])
 
     error_out, far_near = error_rows(
         plan, replicas, here, own_kept, far, lefts, high, low, error.shape

time: 165 us -> 161 us (0.976)
  waiting for transfers between devices: 63.3 us -> 60.7 us
    pallas_call x3, Pallas kernels: 8.44 us -> 13.6 us  [the longest x1 6.66 us: second_pass(): kernel_call(product_kernel, out_shape=(square, near_shape((width, rank)),...]
    pallas_call x1, Pallas kernels: 7.81 us -> 3.12 us  [first_pass(): kernel_call(functools.partial(first_kernel, plan, replicas), out_shape=sh...]
    ppermute x42, waiting for transfers between devices: 63.3 us -> 60.7 us  [flip(): return lax.ppermute(value, axis, [(i, i ^ mask) for i in range(size)])]
  transfers between devices with their start and end apart: 42 -> 42, of which waited for: 25 -> 26; matrix products, arithmetic and copies ran while one was open for 1% -> 1% of each run, Pallas kernels for 12% -> 15%
where the time goes in v5:
time: 161 us
  waiting for transfers between devices  60.7 us (38%)
  starting transfers between devices  53 us (33%)
  Pallas kernels  40.4 us (25%)
  local copies, waits for them, and re-layouts  3.19 us (2%)
  blocking collectives  2.37 us (1%)
    ppermute x42, waiting for transfers between devices, flip(): return lax.ppermute(value, axis, [(i, i ^ mask) for i in range(size)])  60.7 us
    ppermute x42, starting transfers between devices, flip(): return lax.ppermute(value, axis, [(i, i ^ mask) for i in range(size)])  53 us
    pallas_call x2, Pallas kernels, merge(): kernel_call(functools.partial(merge_kernel, counts, leaves, depth), out_s...  9.43 us
    pallas_call x1, Pallas kernels, second_pass(): kernel_call(product_kernel, out_shape=(square, near_shape((width, rank)),...  6.66 us
    pallas_call x1, Pallas kernels, error_rows(): kernel_call(functools.partial(error_kernel, plan, replicas), out_shape=(j...  5.62 us
    pallas_call x1, Pallas kernels, second_pass(): kernel_call(weight_kernel, out_shape=(half, half), in_specs=specs(*[pltpu...  5.16 us
    pallas_call x1, Pallas kernels, last_rows(): kernel_call(functools.partial(last_error_kernel, plan, replicas), out_sha...  3.92 us
  transfers between devices with their start and end apart: 42, of which 26 were waited for; matrix products, arithmetic and copies ran while one was open for 1% of the time, Pallas kernels for 15%

profile of v5, /device:TPU:0, one launch (start us, length us, event | category | flops | bytes accessed | tf_op | source)
XLA Modules:
  0.0 161.0 jit_solution(3144901461955787049)
XLA Ops:
  3.9 4.8 %shard_map.96 = (f32[384,512]{1,0:T(8,128)}, f32[512,512]{1,0:T(8,128)}, f32[384,512]{1,0:T(8,128)}, f32[384,512]{1,0:T(8,128)}, f32[384,512]{1,0:T(8,128)}) custom-call(s32[5]{0:T(128)S(1)} %stack.78.starts_ref, bf16[256,4096]{1,0:T(8,128)(2,1)} %tokens_ref.5, f32[256,128]{1,0:T(8,128)S(1)} %add.79.squares_ref, ...), custom_call_target="tpu_custom_call" | custom-call | flops 536870912 | bytes 9437184 | tf_op jit(solution)/shard_map/pallas_call | solution.py:232
  8.7 3.0 %collective-permute-start.4 = (f32[512,512]{1,0:T(8,128)}, f32[512,512]{1,0:T(8,128)S(1)}, u32[]{:S(2)}, u32[]{:S(2)}) collective-permute-start(f32[512,512]{1,0:T(8,128)} %get-tuple-element.80.refs_1_), channel_id=1, source_target_pairs={{0,8},{2,10},{4,12},{6,14},{8,0},{10,2},{12,4},{14,6},{16,24},{18,... | collective-permute-start | bytes 3145736 | tf_op jit(solution)/shard_map/ppermute | solution.py:42
  16.4 2.4 %all_gather.3.refs_0_.basis_ref = f32[512,128]{1,0:T(8,128)S(1)} all-gather(f32[256,128]{1,0:T(8,128)} %param.11), channel_id=1, replica_groups=mesh['rep'=16,'mp'=2] {'mp'}, dimensions={0}, use_global_device_ids=true | all-gather | bytes 393216 | tf_op jit(solution)/shard_map/all_gather | solution.py:697
  20.3 4.7 %shard_map.95 = (f32[384,512]{1,0:T(8,128)S(1)}, f32[512,512]{1,0:T(8,128)S(1)}, f32[384,512]{1,0:T(8,128)S(1)}, f32[384,512]{1,0:T(8,128)S(1)}, f32[384,512]{1,0:T(8,128)S(1)}, /*index=5*/f32[2048,512]{1,0:T(8,128)}) custom-call(s32[5]{0:T(128)S(1)} %copy-done.6, bf16[256,4096]{1,0:T(8,128)(2,1)} %tokens_ref.5, f32[256,128]{1,0:T(8,128)S(1)} %add.79.squares_ref, ...), custom_call_target="tpu_custom_call" | custom-call | flops 536870912 | bytes 9437184 | tf_op jit(solution)/shard_map/pallas_call | solution.py:232
  25.0 7.4 %collective-permute-done.1.got_ref.refs_0_ = f32[384,512]{1,0:T(8,128)S(1)} collective-permute-done((f32[384,512]{1,0:T(8,128)}, f32[384,512]{1,0:T(8,128)S(1)}, u32[]{:S(2)}, u32[]{:S(2)}) %collective-permute-start.1) | collective-permute-done | bytes 786464 | tf_op jit(solution)/shard_map/ppermute | solution.py:42
  38.8 2.6 %collective-permute-start.8 = (f32[192,512]{1,0:T(8,128)S(1)}, f32[192,512]{1,0:T(8,128)S(1)}, u32[]{:S(2)}, u32[]{:S(2)}) collective-permute-start(f32[192,512]{1,0:T(8,128)S(1)} %get-tuple-element.89), channel_id=1, source_target_pairs={{0,16},{2,18},{4,20},{6,22},{8,24},{10,26},{12,28},{14,30},{16,0},... | collective-permute-start | bytes 1179656 | tf_op jit(solution)/shard_map/ppermute | solution.py:42
  41.4 7.8 %collective-permute-done.6.got_ref.refs_0_ = f32[384,512]{1,0:T(8,128)S(1)} collective-permute-done((f32[384,512]{1,0:T(8,128)}, f32[384,512]{1,0:T(8,128)S(1)}, u32[]{:S(2)}, u32[]{:S(2)}) %collective-permute-start.6) | collective-permute-done | bytes 786464 | tf_op jit(solution)/shard_map/ppermute | solution.py:42
  51.5 6.2 %collective-permute-done.2.got_ref.refs_0_ = f32[192,512]{1,0:T(8,128)S(1)} collective-permute-done((f32[192,512]{1,0:T(8,128)S(1)}, f32[192,512]{1,0:T(8,128)S(1)}, u32[]{:S(2)}, u32[]{:S(2)}) %collective-permute-start.2) | collective-permute-done | bytes 393248 | tf_op jit(solution)/shard_map/ppermute | solution.py:42
  58.2 2.6 %collective-permute-start.7 = (f32[96,512]{1,0:T(8,128)S(1)}, f32[96,512]{1,0:T(8,128)S(1)}, u32[]{:S(2)}, u32[]{:S(2)}) collective-permute-start(f32[96,512]{1,0:T(8,128)S(1)} %get-tuple-element.88), channel_id=1, source_target_pairs={{0,16},{2,18},{4,20},{6,22},{8,24},{10,26},{12,28},{14,30},{16,0},... | collective-permute-start | bytes 589832 | tf_op jit(solution)/shard_map/ppermute | solution.py:42
  62.6 2.2 %collective-permute-start.17 = (f32[96,512]{1,0:T(8,128)S(1)}, f32[96,512]{1,0:T(8,128)S(1)}, u32[]{:S(2)}, u32[]{:S(2)}) collective-permute-start(f32[96,512]{1,0:T(8,128)S(1)} %get-tuple-element.105), channel_id=1, source_target_pairs={{0,16},{2,18},{4,20},{6,22},{8,24},{10,26},{12,28},{14,30},{16,0},... | collective-permute-start | bytes 589832 | tf_op jit(solution)/shard_map/ppermute | solution.py:42
  64.8 11.4 %collective-permute-done.7.got_ref.refs_0_ = f32[96,512]{1,0:T(8,128)S(1)} collective-permute-done((f32[96,512]{1,0:T(8,128)S(1)}, f32[96,512]{1,0:T(8,128)S(1)}, u32[]{:S(2)}, u32[]{:S(2)}) %collective-permute-start.7) | collective-permute-done | bytes 196640 | tf_op jit(solution)/shard_map/ppermute | solution.py:42
  80.2 2.9 %collective-permute-start.16 = (f32[48,512]{1,0:T(8,128)S(1)}, f32[48,512]{1,0:T(8,128)S(1)}, u32[]{:S(2)}, u32[]{:S(2)}) collective-permute-start(f32[48,512]{1,0:T(8,128)S(1)} %get-tuple-element.104), channel_id=1, source_target_pairs={{0,8},{2,10},{4,12},{6,14},{8,0},{10,2},{12,4},{14,6},{16,24},{18,... | collective-permute-start | bytes 294920 | tf_op jit(solution)/shard_map/ppermute | solution.py:42
  83.4 2.8 %collective-permute-start.18 = (f32[48,512]{1,0:T(8,128)S(1)}, f32[48,512]{1,0:T(8,128)S(1)}, u32[]{:S(2)}, u32[]{:S(2)}) collective-permute-start(f32[48,512]{1,0:T(8,128)S(1)} %get-tuple-element.107), channel_id=1, source_target_pairs={{0,8},{2,10},{4,12},{6,14},{8,0},{10,2},{12,4},{14,6},{16,24},{18,... | collective-permute-start | bytes 294920 | tf_op jit(solution)/shard_map/ppermute | solution.py:42
  87.2 2.3 %collective-permute-done.20.got_ref = f32[48,512]{1,0:T(8,128)S(1)} collective-permute-done((f32[48,512]{1,0:T(8,128)S(1)}, f32[48,512]{1,0:T(8,128)S(1)}, u32[]{:S(2)}, u32[]{:S(2)}) %collective-permute-start.20) | collective-permute-done | bytes 98336 | tf_op jit(solution)/shard_map/ppermute | solution.py:42
  96.9 3.1 %collective-permute-done.24 = f32[136,128]{1,0:T(8,128)S(1)} collective-permute-done((f32[136,128]{1,0:T(8,128)S(1)}, f32[136,128]{1,0:T(8,128)S(1)}, u32[]{:S(2)}, u32[]{:S(2)}) %collective-permute-start.24) | collective-permute-done | bytes 69664 | tf_op jit(solution)/shard_map/ppermute | solution.py:42
  101.0 2.1 %collective-permute-start.27 = (f32[136,128]{1,0:T(8,128)S(1)}, f32[136,128]{1,0:T(8,128)S(1)}, u32[]{:S(2)}, u32[]{:S(2)}) collective-permute-start(f32[136,128]{1,0:T(8,128)S(1)} %add_add_fusion.1), channel_id=1, source_target_pairs={{0,24},{2,26},{4,28},{6,30},{8,16},{10,18},{12,20},{14,22},{16,8},... | collective-permute-start | bytes 208904 | tf_op jit(solution)/shard_map/ppermute | solution.py:42
  105.4 2.0 %collective-permute-done.27 = f32[136,128]{1,0:T(8,128)S(1)} collective-permute-done((f32[136,128]{1,0:T(8,128)S(1)}, f32[136,128]{1,0:T(8,128)S(1)}, u32[]{:S(2)}, u32[]{:S(2)}) %collective-permute-start.27) | collective-permute-done | bytes 69664 | tf_op jit(solution)/shard_map/ppermute | solution.py:42
  107.4 2.8 %collective-permute-done.26 = f32[136,128]{1,0:T(8,128)S(1)} collective-permute-done((f32[136,128]{1,0:T(8,128)S(1)}, f32[136,128]{1,0:T(8,128)S(1)}, u32[]{:S(2)}, u32[]{:S(2)}) %collective-permute-start.26) | collective-permute-done | bytes 69664 | tf_op jit(solution)/shard_map/ppermute | solution.py:42
  119.0 3.1 %shard_map.118 = (f32[512,512]{1,0:T(8,128)S(1)}, f32[512,128]{1,0:T(8,128)S(1)}, f32[128,128]{1,0:T(8,128)S(1)}, f32[256,128]{1,0:T(8,128)S(1)}) custom-call(f32[1088,128]{1,0:T(8,128)S(1)} %constant_dynamic-update-slice_fusion.packed_ref, f32[512,128]{1,0:T(8,128)S(1)} %copy-done.1, f32[48,512]{1,0:T(8,128)S(1)} %shard_map.108.refs_1_.refs_0_, ...), custom_call_target="tpu_custom_call" | custom-call | tf_op jit(solution)/shard_map/pallas_call | solution.py:473
  122.6 6.7 %shard_map.119 = (f32[128,128]{1,0:T(8,128)S(1)}, f32[512,128]{1,0:T(8,128)S(1)}, f32[128,128]{1,0:T(8,128)S(1)}) custom-call(f32[512,512]{1,0:T(8,128)S(1)} %get-tuple-element.111.whole_ref, f32[512,128]{1,0:T(8,128)S(1)} %get-tuple-element.112.right_ref, f32[128,128]{1,0:T(8,128)S(1)} %get-tuple-element.113.gram_ref), custom_call_target="tpu_custom_call" | custom-call | tf_op jit(solution)/shard_map/pallas_call | solution.py:506
  133.8 2.9 %collective-permute-done.34.refs_4_ = f32[128,128]{1,0:T(8,128)S(1)} collective-permute-done((f32[128,128]{1,0:T(8,128)S(1)}, f32[128,128]{1,0:T(8,128)S(1)}, u32[]{:S(2)}, u32[]{:S(2)}) %collective-permute-start.34) | collective-permute-done | bytes 65568 | tf_op jit(solution)/shard_map/ppermute | solution.py:42
  141.5 5.2 %shard_map.120 = (bf16[128,512]{1,0:T(8,128)(2,1)S(1)}, bf16[128,512]{1,0:T(8,128)(2,1)S(1)}) custom-call(f32[128,128]{1,0:T(8,128)S(1)} %get-tuple-element.114.first_ref, f32[512,128]{1,0:T(8,128)S(1)} %get-tuple-element.115.plain_ref, f32[128,128]{1,0:T(8,128)S(1)} %get-tuple-element.116.gram_ref.refs_2_.refs_6_), custom_call_target="tpu_custom_call" | custom-call | tf_op jit(solution)/shard_map/pallas_call | solution.py:513
  149.6 5.6 %shard_map.124 = (f32[4096,512]{1,0:T(8,128)}, f32[2048,512]{1,0:T(8,128)S(1)}) custom-call(s32[5]{0:T(128)S(1)} %copy-done.7, bf16[128,512]{1,0:T(8,128)(2,1)S(1)} %get-tuple-element.117.refs_6_.high_ref, bf16[128,512]{1,0:T(8,128)(2,1)S(1)} %get-tuple-element.118.low_ref, f32[2048,512]{1,0:T(8,128)} %get-tuple-element.119.own_ref, ...), custom_call_target="tpu_custom_call" | custom-call | flops 805306368 | bytes 8388608 | tf_op jit(solution)/shard_map/pallas_call | solution.py:627
  156.9 3.9 %shard_map.125 = (f32[4096,512]{1,0:T(8,128)}, f32[256,512]{1,0:T(8,128)}, f32[256,512]{1,0:T(8,128)}) custom-call(s32[11]{0:T(128)S(1)} %stack.76.starts_ref, bf16[128,512]{1,0:T(8,128)(2,1)S(1)} %get-tuple-element.117.refs_6_.high_ref, bf16[128,512]{1,0:T(8,128)(2,1)S(1)} %get-tuple-element.118.low_ref, ...), custom_call_target="tpu_custom_call", output_to_operand_aliasing={{0}: (12, {})} | custom-call | flops 805306368 | bytes 8388608 | tf_op jit(solution)/shard_map/pallas_call | solution.py:652
  (126 shorter events, 59.4 us)
Async XLA Ops:
  8.7 26.7 %collective-permute-start.4 = (f32[512,512]{1,0:T(8,128)}, f32[512,512]{1,0:T(8,128)S(1)}, u32[]{:S(2)}, u32[]{:S(2)}) collective-permute-start(f32[512,512]{1,0:T(8,128)} %get-tuple-element.80.refs_1_), channel_id=1, source_target_pairs={{0,8},{2,10},{4,12},{6,14},{8,0},{10,2},{12,4},{14,6},{16,24},{18,... | collective-permute-start | bytes 3145736 | tf_op jit(solution)/shard_map/ppermute | solution.py:42
  11.7 20.6 %collective-permute-start.1 = (f32[384,512]{1,0:T(8,128)}, f32[384,512]{1,0:T(8,128)S(1)}, u32[]{:S(2)}, u32[]{:S(2)}) collective-permute-start(f32[384,512]{1,0:T(8,128)} %get-tuple-element.72.refs_0_), channel_id=1, source_target_pairs={{0,2},{2,0},{4,6},{6,4},{8,10},{10,8},{12,14},{14,12},{16,18},{18,... | collective-permute-start | bytes 2359304 | tf_op jit(solution)/shard_map/ppermute | solution.py:42
  13.2 20.8 %collective-permute-start.5 = (f32[384,512]{1,0:T(8,128)}, f32[384,512]{1,0:T(8,128)}, u32[]{:S(2)}, u32[]{:S(2)}) collective-permute-start(f32[384,512]{1,0:T(8,128)} %get-tuple-element.81.refs_4_), channel_id=1, source_target_pairs={{0,4},{2,6},{4,0},{6,2},{8,12},{10,14},{12,8},{14,10},{16,20},{18,... | collective-permute-start | bytes 2359304 | tf_op jit(solution)/shard_map/ppermute | solution.py:42
  14.7 34.5 %collective-permute-start.6 = (f32[384,512]{1,0:T(8,128)}, f32[384,512]{1,0:T(8,128)S(1)}, u32[]{:S(2)}, u32[]{:S(2)}) collective-permute-start(f32[384,512]{1,0:T(8,128)} %get-tuple-element.84.refs_2_), channel_id=1, source_target_pairs={{0,2},{2,0},{4,6},{6,4},{8,10},{10,8},{12,14},{14,12},{16,18},{18,... | collective-permute-start | bytes 2359304 | tf_op jit(solution)/shard_map/ppermute | solution.py:42
  15.3 35.6 %collective-permute-start.3 = (f32[384,512]{1,0:T(8,128)}, f32[384,512]{1,0:T(8,128)S(1)}, u32[]{:S(2)}, u32[]{:S(2)}) collective-permute-start(f32[384,512]{1,0:T(8,128)} %get-tuple-element.79.refs_3_), channel_id=1, source_target_pairs={{0,4},{2,6},{4,0},{6,2},{8,12},{10,14},{12,8},{14,10},{16,20},{18,... | collective-permute-start | bytes 2359304 | tf_op jit(solution)/shard_map/ppermute | solution.py:42
  35.5 25.4 %collective-permute-start.10 = (f32[256,512]{1,0:T(8,128)S(1)}, f32[256,512]{1,0:T(8,128)S(1)}, u32[]{:S(2)}, u32[]{:S(2)}) collective-permute-start(f32[256,512]{1,0:T(8,128)S(1)} %get-tuple-element.91), channel_id=1, source_target_pairs={{0,2},{2,0},{4,6},{6,4},{8,10},{10,8},{12,14},{14,12},{16,18},{18,... | collective-permute-start | bytes 1572872 | tf_op jit(solution)/shard_map/ppermute | solution.py:42
  37.2 20.5 %collective-permute-start.2 = (f32[192,512]{1,0:T(8,128)S(1)}, f32[192,512]{1,0:T(8,128)S(1)}, u32[]{:S(2)}, u32[]{:S(2)}) collective-permute-start(f32[192,512]{1,0:T(8,128)S(1)} %get-tuple-element.78), channel_id=1, source_target_pairs={{0,8},{2,10},{4,12},{6,14},{8,0},{10,2},{12,4},{14,6},{16,24},{18,... | collective-permute-start | bytes 1179656 | tf_op jit(solution)/shard_map/ppermute | solution.py:42
  38.8 19.0 %collective-permute-start.8 = (f32[192,512]{1,0:T(8,128)S(1)}, f32[192,512]{1,0:T(8,128)S(1)}, u32[]{:S(2)}, u32[]{:S(2)}) collective-permute-start(f32[192,512]{1,0:T(8,128)S(1)} %get-tuple-element.89), channel_id=1, source_target_pairs={{0,16},{2,18},{4,20},{6,22},{8,24},{10,26},{12,28},{14,30},{16,0},... | collective-permute-start | bytes 1179656 | tf_op jit(solution)/shard_map/ppermute | solution.py:42
  49.3 13.2 %collective-permute-start.11 = (f32[192,512]{1,0:T(8,128)S(1)}, f32[192,512]{1,0:T(8,128)S(1)}, u32[]{:S(2)}, u32[]{:S(2)}) collective-permute-start(f32[192,512]{1,0:T(8,128)S(1)} %get-tuple-element.94), channel_id=1, source_target_pairs={{0,4},{2,6},{4,0},{6,2},{8,12},{10,14},{12,8},{14,10},{16,20},{18,... | collective-permute-start | bytes 1179656 | tf_op jit(solution)/shard_map/ppermute | solution.py:42
  51.0 25.3 %collective-permute-start.14 = (f32[192,512]{1,0:T(8,128)S(1)}, f32[192,512]{1,0:T(8,128)S(1)}, u32[]{:S(2)}, u32[]{:S(2)}) collective-permute-start(f32[192,512]{1,0:T(8,128)S(1)} %get-tuple-element.100), channel_id=1, source_target_pairs={{0,8},{2,10},{4,12},{6,14},{8,0},{10,2},{12,4},{14,6},{16,24},{18,... | collective-permute-start | bytes 1179656 | tf_op jit(solution)/shard_map/ppermute | solution.py:42
  57.8 7.0 %collective-permute-start.9 = (f32[96,512]{1,0:T(8,128)S(1)}, f32[96,512]{1,0:T(8,128)S(1)}, u32[]{:S(2)}, u32[]{:S(2)}) collective-permute-start(f32[96,512]{1,0:T(8,128)S(1)} %get-tuple-element.90), channel_id=1, source_target_pairs={{0,2},{2,0},{4,6},{6,4},{8,10},{10,8},{12,14},{14,12},{16,18},{18,... | collective-permute-start | bytes 589832 | tf_op jit(solution)/shard_map/ppermute | solution.py:42
  58.2 18.0 %collective-permute-start.7 = (f32[96,512]{1,0:T(8,128)S(1)}, f32[96,512]{1,0:T(8,128)S(1)}, u32[]{:S(2)}, u32[]{:S(2)}) collective-permute-start(f32[96,512]{1,0:T(8,128)S(1)} %get-tuple-element.88), channel_id=1, source_target_pairs={{0,16},{2,18},{4,20},{6,22},{8,24},{10,26},{12,28},{14,30},{16,0},... | collective-permute-start | bytes 589832 | tf_op jit(solution)/shard_map/ppermute | solution.py:42
  60.9 19.2 %collective-permute-start.13 = (f32[128,512]{1,0:T(8,128)S(1)}, f32[128,512]{1,0:T(8,128)S(1)}, u32[]{:S(2)}, u32[]{:S(2)}) collective-permute-start(f32[128,512]{1,0:T(8,128)S(1)} %get-tuple-element.99), channel_id=1, source_target_pairs={{0,4},{2,6},{4,0},{6,2},{8,12},{10,14},{12,8},{14,10},{16,20},{18,... | collective-permute-start | bytes 786440 | tf_op jit(solution)/shard_map/ppermute | solution.py:42
  62.6 20.6 %collective-permute-start.17 = (f32[96,512]{1,0:T(8,128)S(1)}, f32[96,512]{1,0:T(8,128)S(1)}, u32[]{:S(2)}, u32[]{:S(2)}) collective-permute-start(f32[96,512]{1,0:T(8,128)S(1)} %get-tuple-element.105), channel_id=1, source_target_pairs={{0,16},{2,18},{4,20},{6,22},{8,24},{10,26},{12,28},{14,30},{16,0},... | collective-permute-start | bytes 589832 | tf_op jit(solution)/shard_map/ppermute | solution.py:42
  76.4 6.9 %collective-permute-start.19 = (f32[96,512]{1,0:T(8,128)S(1)}, f32[96,512]{1,0:T(8,128)S(1)}, u32[]{:S(2)}, u32[]{:S(2)}) collective-permute-start(f32[96,512]{1,0:T(8,128)S(1)} %get-tuple-element.108), channel_id=1, source_target_pairs={{0,2},{2,0},{4,6},{6,4},{8,10},{10,8},{12,14},{14,12},{16,18},{18,... | collective-permute-start | bytes 589832 | tf_op jit(solution)/shard_map/ppermute | solution.py:42
  80.2 9.7 %collective-permute-start.15 = (f32[64,512]{1,0:T(8,128)S(1)}, f32[64,512]{1,0:T(8,128)S(1)}, u32[]{:S(2)}, u32[]{:S(2)}) collective-permute-start(f32[64,512]{1,0:T(8,128)S(1)} %get-tuple-element.103), channel_id=1, source_target_pairs={{0,16},{2,18},{4,20},{6,22},{8,24},{10,26},{12,28},{14,30},{16,0},... | collective-permute-start | bytes 393224 | tf_op jit(solution)/shard_map/ppermute | solution.py:42
  80.2 6.9 %collective-permute-start.16 = (f32[48,512]{1,0:T(8,128)S(1)}, f32[48,512]{1,0:T(8,128)S(1)}, u32[]{:S(2)}, u32[]{:S(2)}) collective-permute-start(f32[48,512]{1,0:T(8,128)S(1)} %get-tuple-element.104), channel_id=1, source_target_pairs={{0,8},{2,10},{4,12},{6,14},{8,0},{10,2},{12,4},{14,6},{16,24},{18,... | collective-permute-start | bytes 294920 | tf_op jit(solution)/shard_map/ppermute | solution.py:42
  101.0 6.5 %collective-permute-start.27 = (f32[136,128]{1,0:T(8,128)S(1)}, f32[136,128]{1,0:T(8,128)S(1)}, u32[]{:S(2)}, u32[]{:S(2)}) collective-permute-start(f32[136,128]{1,0:T(8,128)S(1)} %add_add_fusion.1), channel_id=1, source_target_pairs={{0,24},{2,26},{4,28},{6,30},{8,16},{10,18},{12,20},{14,22},{16,8},... | collective-permute-start | bytes 208904 | tf_op jit(solution)/shard_map/ppermute | solution.py:42
  103.1 7.1 %collective-permute-start.26 = (f32[136,128]{1,0:T(8,128)S(1)}, f32[136,128]{1,0:T(8,128)S(1)}, u32[]{:S(2)}, u32[]{:S(2)}) collective-permute-start(f32[136,128]{1,0:T(8,128)S(1)} %add_add_fusion.1), channel_id=1, source_target_pairs={{0,16},{2,18},{4,20},{6,22},{8,24},{10,26},{12,28},{14,30},{16,0},... | collective-permute-start | bytes 208904 | tf_op jit(solution)/shard_map/ppermute | solution.py:42
  122.1 8.6 %collective-permute-start.32 = (f32[256,128]{1,0:T(8,128)S(1)}, f32[256,128]{1,0:T(8,128)S(1)}, u32[]{:S(2)}, u32[]{:S(2)}) collective-permute-start(f32[256,128]{1,0:T(8,128)S(1)} %get-tuple-element.120.refs_0_), channel_id=1, source_target_pairs={{0,16},{2,18},{4,20},{6,22},{8,24},{10,26},{12,28},{14,30},{16,0},... | collective-permute-start | bytes 393224 | tf_op jit(solution)/shard_map/ppermute | solution.py:42
  137.5 9.2 %collective-permute-start.37 = (f32[384,128]{1,0:T(8,128)S(1)}, f32[384,128]{1,0:T(8,128)S(1)}, u32[]{:S(2)}, u32[]{:S(2)}) collective-permute-start(f32[384,128]{1,0:T(8,128)S(1)} %get-tuple-element.125.refs_1_), channel_id=1, source_target_pairs={{0,4},{2,6},{4,0},{6,2},{8,12},{10,14},{12,8},{14,10},{16,20},{18,... | collective-permute-start | bytes 589832 | tf_op jit(solution)/shard_map/ppermute | solution.py:42
  138.8 7.9 %collective-permute-start.38 = (f32[384,128]{1,0:T(8,128)S(1)}, f32[384,128]{1,0:T(8,128)S(1)}, u32[]{:S(2)}, u32[]{:S(2)}) collective-permute-start(f32[384,128]{1,0:T(8,128)S(1)} %get-tuple-element.126.refs_2_), channel_id=1, source_target_pairs={{0,8},{2,10},{4,12},{6,14},{8,0},{10,2},{12,4},{14,6},{16,24},{18,... | collective-permute-start | bytes 589832 | tf_op jit(solution)/shard_map/ppermute | solution.py:42
  147.3 8.9 %collective-permute-start.39 = (f32[768,128]{1,0:T(8,128)S(1)}, f32[768,128]{1,0:T(8,128)S(1)}, u32[]{:S(2)}, u32[]{:S(2)}) collective-permute-start(f32[768,128]{1,0:T(8,128)S(1)} %get-tuple-element.127.refs_5_.refs_3_), channel_id=1, source_target_pairs={{0,2},{2,0},{4,6},{6,4},{8,10},{10,8},{12,14},{14,12},{16,18},{18,... | collective-permute-start | bytes 1179656 | tf_op jit(solution)/shard_map/ppermute | solution.py:42
  148.4 8.5 %collective-permute-start.40 = (f32[768,128]{1,0:T(8,128)S(1)}, f32[768,128]{1,0:T(8,128)S(1)}, u32[]{:S(2)}, u32[]{:S(2)}) collective-permute-start(f32[768,128]{1,0:T(8,128)S(1)} %get-tuple-element.128.refs_6_.refs_4_), channel_id=1, source_target_pairs={{0,4},{2,6},{4,0},{6,2},{8,12},{10,14},{12,8},{14,10},{16,20},{18,... | collective-permute-start | bytes 1179656 | tf_op jit(solution)/shard_map/ppermute | solution.py:42
  (26 other events, 314.7 us)

commit v6 on v5

--- a/solution.py
+++ b/solution.py
@@ -11,14 +11,14 @@
 BLOCK = 128
 
 SHARES = (
-    (3, (0, 2, 3, 1)),
+    (3, (0, 2, 1, 3)),
     (4, (2, 0, 1, 3)),
     (3, (0, 1, 3, 2)),
     (3, (1, 2, 0, 3)),
     (3, (1, 3, 0, 2)),
 )
 BACK = {0: (3, 2, 1, 0), 1: (3, 0, 2, 1), 2: (3, 1, 0, 2)}
-ARRIVALS = (0, 4, 1, 2, 3, 0, 4, 1, 2, 4, 0, 3, 1, 0, 2, 3, 4, 1, 2, 3)
+ARRIVALS = (0, 4, 1, 2, 3, 0, 4, 1, 2, 4, 0, 3, 1, 2, 4, 3, 0, 2, 1, 3)
 TURNS = (0, 4, 2, 1, 3)
 
 precise = lax.Precision.HIGHEST

time: 161 us -> 156 us (0.969)
  waiting for transfers between devices: 60.7 us -> 54.3 us
    ppermute x42, waiting for transfers between devices: 60.7 us -> 54.3 us  [flip(): return lax.ppermute(value, axis, [(i, i ^ mask) for i in range(size)])]
  transfers between devices with their start and end apart: 42 -> 42, of which waited for: 26 -> 28; matrix products, arithmetic and copies ran while one was open for 1% -> 1% of each run, Pallas kernels for 15% -> 15%
where the time goes in v6:
time: 156 us
  starting transfers between devices  54.4 us (35%)
  waiting for transfers between devices  54.3 us (35%)
  Pallas kernels  40.3 us (26%)
  local copies, waits for them, and re-layouts  3.19 us (2%)
  blocking collectives  2.37 us (2%)
    ppermute x42, starting transfers between devices, flip(): return lax.ppermute(value, axis, [(i, i ^ mask) for i in range(size)])  54.4 us
    ppermute x42, waiting for transfers between devices, flip(): return lax.ppermute(value, axis, [(i, i ^ mask) for i in range(size)])  54.3 us
    pallas_call x2, Pallas kernels, merge(): kernel_call(functools.partial(merge_kernel, counts, leaves, depth), out_s...  9.43 us
    pallas_call x1, Pallas kernels, second_pass(): kernel_call(product_kernel, out_shape=(square, near_shape((width, rank)),...  6.66 us
    pallas_call x1, Pallas kernels, error_rows(): kernel_call(functools.partial(error_kernel, plan, replicas), out_shape=(j...  5.62 us
    pallas_call x1, Pallas kernels, second_pass(): kernel_call(weight_kernel, out_shape=(half, half), in_specs=specs(*[pltpu...  5.16 us
    pallas_call x1, Pallas kernels, last_rows(): kernel_call(functools.partial(last_error_kernel, plan, replicas), out_sha...  3.92 us
  transfers between devices with their start and end apart: 42, of which 28 were waited for; matrix products, arithmetic and copies ran while one was open for 1% of the time, Pallas kernels for 15%

profile of v6, /device:TPU:0, one launch (start us, length us, event | category | flops | bytes accessed | tf_op | source)
XLA Modules:
  0.0 156.0 jit_solution(638051978787016132)
XLA Ops:
  3.9 4.8 %shard_map.96 = (f32[384,512]{1,0:T(8,128)}, f32[512,512]{1,0:T(8,128)}, f32[384,512]{1,0:T(8,128)}, f32[384,512]{1,0:T(8,128)}, f32[384,512]{1,0:T(8,128)}) custom-call(s32[5]{0:T(128)S(1)} %stack.78.starts_ref, bf16[256,4096]{1,0:T(8,128)(2,1)} %tokens_ref.5, f32[256,128]{1,0:T(8,128)S(1)} %add.79.squares_ref, ...), custom_call_target="tpu_custom_call" | custom-call | flops 536870912 | bytes 9437184 | tf_op jit(solution)/shard_map/pallas_call | solution.py:232
  8.7 3.0 %collective-permute-start.4 = (f32[512,512]{1,0:T(8,128)}, f32[512,512]{1,0:T(8,128)S(1)}, u32[]{:S(2)}, u32[]{:S(2)}) collective-permute-start(f32[512,512]{1,0:T(8,128)} %get-tuple-element.80.refs_1_), channel_id=1, source_target_pairs={{0,8},{2,10},{4,12},{6,14},{8,0},{10,2},{12,4},{14,6},{16,24},{18,... | collective-permute-start | bytes 3145736 | tf_op jit(solution)/shard_map/ppermute | solution.py:42
  16.4 2.4 %all_gather.3.refs_0_.basis_ref = f32[512,128]{1,0:T(8,128)S(1)} all-gather(f32[256,128]{1,0:T(8,128)} %param.11), channel_id=1, replica_groups=mesh['rep'=16,'mp'=2] {'mp'}, dimensions={0}, use_global_device_ids=true | all-gather | bytes 393216 | tf_op jit(solution)/shard_map/all_gather | solution.py:697
  20.3 4.7 %shard_map.95 = (f32[384,512]{1,0:T(8,128)S(1)}, f32[512,512]{1,0:T(8,128)S(1)}, f32[384,512]{1,0:T(8,128)S(1)}, f32[384,512]{1,0:T(8,128)S(1)}, f32[384,512]{1,0:T(8,128)S(1)}, /*index=5*/f32[2048,512]{1,0:T(8,128)}) custom-call(s32[5]{0:T(128)S(1)} %copy-done.6, bf16[256,4096]{1,0:T(8,128)(2,1)} %tokens_ref.5, f32[256,128]{1,0:T(8,128)S(1)} %add.79.squares_ref, ...), custom_call_target="tpu_custom_call" | custom-call | flops 536870912 | bytes 9437184 | tf_op jit(solution)/shard_map/pallas_call | solution.py:232
  25.0 7.4 %collective-permute-done.1.got_ref.refs_0_ = f32[384,512]{1,0:T(8,128)S(1)} collective-permute-done((f32[384,512]{1,0:T(8,128)}, f32[384,512]{1,0:T(8,128)S(1)}, u32[]{:S(2)}, u32[]{:S(2)}) %collective-permute-start.1) | collective-permute-done | bytes 786464 | tf_op jit(solution)/shard_map/ppermute | solution.py:42
  38.8 2.6 %collective-permute-start.8 = (f32[192,512]{1,0:T(8,128)S(1)}, f32[192,512]{1,0:T(8,128)S(1)}, u32[]{:S(2)}, u32[]{:S(2)}) collective-permute-start(f32[192,512]{1,0:T(8,128)S(1)} %get-tuple-element.89), channel_id=1, source_target_pairs={{0,16},{2,18},{4,20},{6,22},{8,24},{10,26},{12,28},{14,30},{16,0},... | collective-permute-start | bytes 1179656 | tf_op jit(solution)/shard_map/ppermute | solution.py:42
  41.4 7.8 %collective-permute-done.6.got_ref.refs_0_ = f32[384,512]{1,0:T(8,128)S(1)} collective-permute-done((f32[384,512]{1,0:T(8,128)}, f32[384,512]{1,0:T(8,128)S(1)}, u32[]{:S(2)}, u32[]{:S(2)}) %collective-permute-start.6) | collective-permute-done | bytes 786464 | tf_op jit(solution)/shard_map/ppermute | solution.py:42
  51.5 6.2 %collective-permute-done.2.got_ref.refs_0_ = f32[192,512]{1,0:T(8,128)S(1)} collective-permute-done((f32[192,512]{1,0:T(8,128)S(1)}, f32[192,512]{1,0:T(8,128)S(1)}, u32[]{:S(2)}, u32[]{:S(2)}) %collective-permute-start.2) | collective-permute-done | bytes 393248 | tf_op jit(solution)/shard_map/ppermute | solution.py:42
  62.1 2.7 %collective-permute-start.17 = (f32[96,512]{1,0:T(8,128)S(1)}, f32[96,512]{1,0:T(8,128)S(1)}, u32[]{:S(2)}, u32[]{:S(2)}) collective-permute-start(f32[96,512]{1,0:T(8,128)S(1)} %get-tuple-element.105), channel_id=1, source_target_pairs={{0,16},{2,18},{4,20},{6,22},{8,24},{10,26},{12,28},{14,30},{16,0},... | collective-permute-start | bytes 589832 | tf_op jit(solution)/shard_map/ppermute | solution.py:42
  68.8 2.7 %collective-permute-start.16 = (f32[64,512]{1,0:T(8,128)S(1)}, f32[64,512]{1,0:T(8,128)S(1)}, u32[]{:S(2)}, u32[]{:S(2)}) collective-permute-start(f32[64,512]{1,0:T(8,128)S(1)} %get-tuple-element.104), channel_id=1, source_target_pairs={{0,16},{2,18},{4,20},{6,22},{8,24},{10,26},{12,28},{14,30},{16,0},... | collective-permute-start | bytes 393224 | tf_op jit(solution)/shard_map/ppermute | solution.py:42
  73.4 1.9 %collective-permute-done.17.got_ref.refs_0_ = f32[96,512]{1,0:T(8,128)S(1)} collective-permute-done((f32[96,512]{1,0:T(8,128)S(1)}, f32[96,512]{1,0:T(8,128)S(1)}, u32[]{:S(2)}, u32[]{:S(2)}) %collective-permute-start.17) | collective-permute-done | bytes 196640 | tf_op jit(solution)/shard_map/ppermute | solution.py:42
  75.8 6.4 %collective-permute-start.20 = (f32[48,512]{1,0:T(8,128)S(1)}, f32[48,512]{1,0:T(8,128)S(1)}, u32[]{:S(2)}, u32[]{:S(2)}) collective-permute-start(f32[48,512]{1,0:T(8,128)S(1)} %get-tuple-element.110), channel_id=1, source_target_pairs={{0,16},{2,18},{4,20},{6,22},{8,24},{10,26},{12,28},{14,30},{16,0},... | collective-permute-start | bytes 294920 | tf_op jit(solution)/shard_map/ppermute | solution.py:42
  93.3 2.0 %collective-permute-done.24 = f32[136,128]{1,0:T(8,128)S(1)} collective-permute-done((f32[136,128]{1,0:T(8,128)S(1)}, f32[136,128]{1,0:T(8,128)S(1)}, u32[]{:S(2)}, u32[]{:S(2)}) %collective-permute-start.24) | collective-permute-done | bytes 69664 | tf_op jit(solution)/shard_map/ppermute | solution.py:42
  96.2 2.2 %collective-permute-start.27 = (f32[136,128]{1,0:T(8,128)S(1)}, f32[136,128]{1,0:T(8,128)S(1)}, u32[]{:S(2)}, u32[]{:S(2)}) collective-permute-start(f32[136,128]{1,0:T(8,128)S(1)} %add_add_fusion.1), channel_id=1, source_target_pairs={{0,24},{2,26},{4,28},{6,30},{8,16},{10,18},{12,20},{14,22},{16,8},... | collective-permute-start | bytes 208904 | tf_op jit(solution)/shard_map/ppermute | solution.py:42
  98.5 2.1 %collective-permute-start.25 = (f32[136,128]{1,0:T(8,128)S(1)}, f32[136,128]{1,0:T(8,128)S(1)}, u32[]{:S(2)}, u32[]{:S(2)}) collective-permute-start(f32[136,128]{1,0:T(8,128)S(1)} %add_add_fusion.1), channel_id=1, source_target_pairs={{0,8},{2,10},{4,12},{6,14},{8,0},{10,2},{12,4},{14,6},{16,24},{18,... | collective-permute-start | bytes 208904 | tf_op jit(solution)/shard_map/ppermute | solution.py:42
  100.6 2.5 %collective-permute-done.27 = f32[136,128]{1,0:T(8,128)S(1)} collective-permute-done((f32[136,128]{1,0:T(8,128)S(1)}, f32[136,128]{1,0:T(8,128)S(1)}, u32[]{:S(2)}, u32[]{:S(2)}) %collective-permute-start.27) | collective-permute-done | bytes 69664 | tf_op jit(solution)/shard_map/ppermute | solution.py:42
  103.1 2.0 %collective-permute-done.26 = f32[136,128]{1,0:T(8,128)S(1)} collective-permute-done((f32[136,128]{1,0:T(8,128)S(1)}, f32[136,128]{1,0:T(8,128)S(1)}, u32[]{:S(2)}, u32[]{:S(2)}) %collective-permute-start.26) | collective-permute-done | bytes 69664 | tf_op jit(solution)/shard_map/ppermute | solution.py:42
  109.7 1.8 %collective-permute-done.29 = f32[136,128]{1,0:T(8,128)S(1)} collective-permute-done((f32[136,128]{1,0:T(8,128)S(1)}, f32[136,128]{1,0:T(8,128)S(1)}, u32[]{:S(2)}, u32[]{:S(2)}) %collective-permute-start.29) | collective-permute-done | bytes 69664 | tf_op jit(solution)/shard_map/ppermute | solution.py:42
  114.6 3.1 %shard_map.118 = (f32[512,512]{1,0:T(8,128)S(1)}, f32[512,128]{1,0:T(8,128)S(1)}, f32[128,128]{1,0:T(8,128)S(1)}, f32[256,128]{1,0:T(8,128)S(1)}) custom-call(f32[1088,128]{1,0:T(8,128)S(1)} %constant_dynamic-update-slice_fusion.packed_ref, f32[512,128]{1,0:T(8,128)S(1)} %copy-done.1, f32[48,512]{1,0:T(8,128)S(1)} %shard_map.109.refs_0_, ...), custom_call_target="tpu_custom_call" | custom-call | tf_op jit(solution)/shard_map/pallas_call | solution.py:473
  118.5 6.7 %shard_map.119 = (f32[128,128]{1,0:T(8,128)S(1)}, f32[512,128]{1,0:T(8,128)S(1)}, f32[128,128]{1,0:T(8,128)S(1)}) custom-call(f32[512,512]{1,0:T(8,128)S(1)} %get-tuple-element.111.whole_ref, f32[512,128]{1,0:T(8,128)S(1)} %get-tuple-element.112.right_ref, f32[128,128]{1,0:T(8,128)S(1)} %get-tuple-element.113.gram_ref), custom_call_target="tpu_custom_call" | custom-call | tf_op jit(solution)/shard_map/pallas_call | solution.py:506
  129.1 3.9 %collective-permute-done.34.refs_4_ = f32[128,128]{1,0:T(8,128)S(1)} collective-permute-done((f32[128,128]{1,0:T(8,128)S(1)}, f32[128,128]{1,0:T(8,128)S(1)}, u32[]{:S(2)}, u32[]{:S(2)}) %collective-permute-start.34) | collective-permute-done | bytes 65568 | tf_op jit(solution)/shard_map/ppermute | solution.py:42
  137.0 5.2 %shard_map.120 = (bf16[128,512]{1,0:T(8,128)(2,1)S(1)}, bf16[128,512]{1,0:T(8,128)(2,1)S(1)}) custom-call(f32[128,128]{1,0:T(8,128)S(1)} %get-tuple-element.114.first_ref, f32[512,128]{1,0:T(8,128)S(1)} %get-tuple-element.115.plain_ref, f32[128,128]{1,0:T(8,128)S(1)} %get-tuple-element.116.gram_ref.refs_2_.refs_6_), custom_call_target="tpu_custom_call" | custom-call | tf_op jit(solution)/shard_map/pallas_call | solution.py:513
  145.7 5.6 %shard_map.124 = (f32[4096,512]{1,0:T(8,128)}, f32[2048,512]{1,0:T(8,128)S(1)}) custom-call(s32[5]{0:T(128)S(1)} %copy-done.7, bf16[128,512]{1,0:T(8,128)(2,1)S(1)} %get-tuple-element.117.refs_6_.high_ref, bf16[128,512]{1,0:T(8,128)(2,1)S(1)} %get-tuple-element.118.low_ref, f32[2048,512]{1,0:T(8,128)} %get-tuple-element.119.own_ref, ...), custom_call_target="tpu_custom_call" | custom-call | flops 805306368 | bytes 8388608 | tf_op jit(solution)/shard_map/pallas_call | solution.py:627
  151.9 3.9 %shard_map.125 = (f32[4096,512]{1,0:T(8,128)}, f32[256,512]{1,0:T(8,128)}, f32[256,512]{1,0:T(8,128)}) custom-call(s32[11]{0:T(128)S(1)} %stack.76.starts_ref, bf16[128,512]{1,0:T(8,128)(2,1)S(1)} %get-tuple-element.117.refs_6_.high_ref, bf16[128,512]{1,0:T(8,128)(2,1)S(1)} %get-tuple-element.118.low_ref, ...), custom_call_target="tpu_custom_call", output_to_operand_aliasing={{0}: (12, {})} | custom-call | flops 805306368 | bytes 8388608 | tf_op jit(solution)/shard_map/pallas_call | solution.py:652
  (126 shorter events, 61.5 us)
Async XLA Ops:
  8.7 26.7 %collective-permute-start.4 = (f32[512,512]{1,0:T(8,128)}, f32[512,512]{1,0:T(8,128)S(1)}, u32[]{:S(2)}, u32[]{:S(2)}) collective-permute-start(f32[512,512]{1,0:T(8,128)} %get-tuple-element.80.refs_1_), channel_id=1, source_target_pairs={{0,8},{2,10},{4,12},{6,14},{8,0},{10,2},{12,4},{14,6},{16,24},{18,... | collective-permute-start | bytes 3145736 | tf_op jit(solution)/shard_map/ppermute | solution.py:42
  11.7 20.6 %collective-permute-start.1 = (f32[384,512]{1,0:T(8,128)}, f32[384,512]{1,0:T(8,128)S(1)}, u32[]{:S(2)}, u32[]{:S(2)}) collective-permute-start(f32[384,512]{1,0:T(8,128)} %get-tuple-element.72.refs_0_), channel_id=1, source_target_pairs={{0,2},{2,0},{4,6},{6,4},{8,10},{10,8},{12,14},{14,12},{16,18},{18,... | collective-permute-start | bytes 2359304 | tf_op jit(solution)/shard_map/ppermute | solution.py:42
  13.2 20.8 %collective-permute-start.5 = (f32[384,512]{1,0:T(8,128)}, f32[384,512]{1,0:T(8,128)}, u32[]{:S(2)}, u32[]{:S(2)}) collective-permute-start(f32[384,512]{1,0:T(8,128)} %get-tuple-element.81.refs_4_), channel_id=1, source_target_pairs={{0,4},{2,6},{4,0},{6,2},{8,12},{10,14},{12,8},{14,10},{16,20},{18,... | collective-permute-start | bytes 2359304 | tf_op jit(solution)/shard_map/ppermute | solution.py:42
  14.7 34.5 %collective-permute-start.6 = (f32[384,512]{1,0:T(8,128)}, f32[384,512]{1,0:T(8,128)S(1)}, u32[]{:S(2)}, u32[]{:S(2)}) collective-permute-start(f32[384,512]{1,0:T(8,128)} %get-tuple-element.84.refs_2_), channel_id=1, source_target_pairs={{0,2},{2,0},{4,6},{6,4},{8,10},{10,8},{12,14},{14,12},{16,18},{18,... | collective-permute-start | bytes 2359304 | tf_op jit(solution)/shard_map/ppermute | solution.py:42
  15.3 35.6 %collective-permute-start.3 = (f32[384,512]{1,0:T(8,128)}, f32[384,512]{1,0:T(8,128)S(1)}, u32[]{:S(2)}, u32[]{:S(2)}) collective-permute-start(f32[384,512]{1,0:T(8,128)} %get-tuple-element.79.refs_3_), channel_id=1, source_target_pairs={{0,4},{2,6},{4,0},{6,2},{8,12},{10,14},{12,8},{14,10},{16,20},{18,... | collective-permute-start | bytes 2359304 | tf_op jit(solution)/shard_map/ppermute | solution.py:42
  35.5 24.9 %collective-permute-start.10 = (f32[256,512]{1,0:T(8,128)S(1)}, f32[256,512]{1,0:T(8,128)S(1)}, u32[]{:S(2)}, u32[]{:S(2)}) collective-permute-start(f32[256,512]{1,0:T(8,128)S(1)} %get-tuple-element.91), channel_id=1, source_target_pairs={{0,2},{2,0},{4,6},{6,4},{8,10},{10,8},{12,14},{14,12},{16,18},{18,... | collective-permute-start | bytes 1572872 | tf_op jit(solution)/shard_map/ppermute | solution.py:42
  37.2 20.5 %collective-permute-start.2 = (f32[192,512]{1,0:T(8,128)S(1)}, f32[192,512]{1,0:T(8,128)S(1)}, u32[]{:S(2)}, u32[]{:S(2)}) collective-permute-start(f32[192,512]{1,0:T(8,128)S(1)} %get-tuple-element.78), channel_id=1, source_target_pairs={{0,8},{2,10},{4,12},{6,14},{8,0},{10,2},{12,4},{14,6},{16,24},{18,... | collective-permute-start | bytes 1179656 | tf_op jit(solution)/shard_map/ppermute | solution.py:42
  38.8 19.0 %collective-permute-start.8 = (f32[192,512]{1,0:T(8,128)S(1)}, f32[192,512]{1,0:T(8,128)S(1)}, u32[]{:S(2)}, u32[]{:S(2)}) collective-permute-start(f32[192,512]{1,0:T(8,128)S(1)} %get-tuple-element.89), channel_id=1, source_target_pairs={{0,16},{2,18},{4,20},{6,22},{8,24},{10,26},{12,28},{14,30},{16,0},... | collective-permute-start | bytes 1179656 | tf_op jit(solution)/shard_map/ppermute | solution.py:42
  49.3 12.8 %collective-permute-start.11 = (f32[192,512]{1,0:T(8,128)S(1)}, f32[192,512]{1,0:T(8,128)S(1)}, u32[]{:S(2)}, u32[]{:S(2)}) collective-permute-start(f32[192,512]{1,0:T(8,128)S(1)} %get-tuple-element.94), channel_id=1, source_target_pairs={{0,4},{2,6},{4,0},{6,2},{8,12},{10,14},{12,8},{14,10},{16,20},{18,... | collective-permute-start | bytes 1179656 | tf_op jit(solution)/shard_map/ppermute | solution.py:42
  51.0 15.0 %collective-permute-start.13 = (f32[192,512]{1,0:T(8,128)S(1)}, f32[192,512]{1,0:T(8,128)S(1)}, u32[]{:S(2)}, u32[]{:S(2)}) collective-permute-start(f32[192,512]{1,0:T(8,128)S(1)} %get-tuple-element.99), channel_id=1, source_target_pairs={{0,8},{2,10},{4,12},{6,14},{8,0},{10,2},{12,4},{14,6},{16,24},{18,... | collective-permute-start | bytes 1179656 | tf_op jit(solution)/shard_map/ppermute | solution.py:42
  57.8 7.0 %collective-permute-start.9 = (f32[96,512]{1,0:T(8,128)S(1)}, f32[96,512]{1,0:T(8,128)S(1)}, u32[]{:S(2)}, u32[]{:S(2)}) collective-permute-start(f32[96,512]{1,0:T(8,128)S(1)} %get-tuple-element.90), channel_id=1, source_target_pairs={{0,2},{2,0},{4,6},{6,4},{8,10},{10,8},{12,14},{14,12},{16,18},{18,... | collective-permute-start | bytes 589832 | tf_op jit(solution)/shard_map/ppermute | solution.py:42
  58.2 7.7 %collective-permute-start.7 = (f32[96,512]{1,0:T(8,128)S(1)}, f32[96,512]{1,0:T(8,128)S(1)}, u32[]{:S(2)}, u32[]{:S(2)}) collective-permute-start(f32[96,512]{1,0:T(8,128)S(1)} %get-tuple-element.88), channel_id=1, source_target_pairs={{0,4},{2,6},{4,0},{6,2},{8,12},{10,14},{12,8},{14,10},{16,20},{18,... | collective-permute-start | bytes 589832 | tf_op jit(solution)/shard_map/ppermute | solution.py:42
  60.5 8.3 %collective-permute-start.15 = (f32[128,512]{1,0:T(8,128)S(1)}, f32[128,512]{1,0:T(8,128)S(1)}, u32[]{:S(2)}, u32[]{:S(2)}) collective-permute-start(f32[128,512]{1,0:T(8,128)S(1)} %get-tuple-element.101), channel_id=1, source_target_pairs={{0,4},{2,6},{4,0},{6,2},{8,12},{10,14},{12,8},{14,10},{16,20},{18,... | collective-permute-start | bytes 786440 | tf_op jit(solution)/shard_map/ppermute | solution.py:42
  62.1 13.1 %collective-permute-start.17 = (f32[96,512]{1,0:T(8,128)S(1)}, f32[96,512]{1,0:T(8,128)S(1)}, u32[]{:S(2)}, u32[]{:S(2)}) collective-permute-start(f32[96,512]{1,0:T(8,128)S(1)} %get-tuple-element.105), channel_id=1, source_target_pairs={{0,16},{2,18},{4,20},{6,22},{8,24},{10,26},{12,28},{14,30},{16,0},... | collective-permute-start | bytes 589832 | tf_op jit(solution)/shard_map/ppermute | solution.py:42
  66.0 9.7 %collective-permute-start.14 = (f32[96,512]{1,0:T(8,128)S(1)}, f32[96,512]{1,0:T(8,128)S(1)}, u32[]{:S(2)}, u32[]{:S(2)}) collective-permute-start(f32[96,512]{1,0:T(8,128)S(1)} %get-tuple-element.100), channel_id=1, source_target_pairs={{0,2},{2,0},{4,6},{6,4},{8,10},{10,8},{12,14},{14,12},{16,18},{18,... | collective-permute-start | bytes 589832 | tf_op jit(solution)/shard_map/ppermute | solution.py:42
  68.8 15.7 %collective-permute-start.16 = (f32[64,512]{1,0:T(8,128)S(1)}, f32[64,512]{1,0:T(8,128)S(1)}, u32[]{:S(2)}, u32[]{:S(2)}) collective-permute-start(f32[64,512]{1,0:T(8,128)S(1)} %get-tuple-element.104), channel_id=1, source_target_pairs={{0,16},{2,18},{4,20},{6,22},{8,24},{10,26},{12,28},{14,30},{16,0},... | collective-permute-start | bytes 393224 | tf_op jit(solution)/shard_map/ppermute | solution.py:42
  71.5 12.3 %collective-permute-start.12 = (f32[48,512]{1,0:T(8,128)S(1)}, f32[48,512]{1,0:T(8,128)S(1)}, u32[]{:S(2)}, u32[]{:S(2)}) collective-permute-start(f32[48,512]{1,0:T(8,128)S(1)} %get-tuple-element.98), channel_id=1, source_target_pairs={{0,16},{2,18},{4,20},{6,22},{8,24},{10,26},{12,28},{14,30},{16,0},... | collective-permute-start | bytes 294920 | tf_op jit(solution)/shard_map/ppermute | solution.py:42
  75.3 9.2 %collective-permute-start.18 = (f32[48,512]{1,0:T(8,128)S(1)}, f32[48,512]{1,0:T(8,128)S(1)}, u32[]{:S(2)}, u32[]{:S(2)}) collective-permute-start(f32[48,512]{1,0:T(8,128)S(1)} %get-tuple-element.106), channel_id=1, source_target_pairs={{0,8},{2,10},{4,12},{6,14},{8,0},{10,2},{12,4},{14,6},{16,24},{18,... | collective-permute-start | bytes 294920 | tf_op jit(solution)/shard_map/ppermute | solution.py:42
  75.8 10.1 %collective-permute-start.20 = (f32[48,512]{1,0:T(8,128)S(1)}, f32[48,512]{1,0:T(8,128)S(1)}, u32[]{:S(2)}, u32[]{:S(2)}) collective-permute-start(f32[48,512]{1,0:T(8,128)S(1)} %get-tuple-element.110), channel_id=1, source_target_pairs={{0,16},{2,18},{4,20},{6,22},{8,24},{10,26},{12,28},{14,30},{16,0},... | collective-permute-start | bytes 294920 | tf_op jit(solution)/shard_map/ppermute | solution.py:42
  117.7 9.2 %collective-permute-start.32 = (f32[256,128]{1,0:T(8,128)S(1)}, f32[256,128]{1,0:T(8,128)S(1)}, u32[]{:S(2)}, u32[]{:S(2)}) collective-permute-start(f32[256,128]{1,0:T(8,128)S(1)} %get-tuple-element.120.refs_0_), channel_id=1, source_target_pairs={{0,16},{2,18},{4,20},{6,22},{8,24},{10,26},{12,28},{14,30},{16,0},... | collective-permute-start | bytes 393224 | tf_op jit(solution)/shard_map/ppermute | solution.py:42
  133.5 8.7 %collective-permute-start.37 = (f32[384,128]{1,0:T(8,128)S(1)}, f32[384,128]{1,0:T(8,128)S(1)}, u32[]{:S(2)}, u32[]{:S(2)}) collective-permute-start(f32[384,128]{1,0:T(8,128)S(1)} %get-tuple-element.125.refs_1_), channel_id=1, source_target_pairs={{0,4},{2,6},{4,0},{6,2},{8,12},{10,14},{12,8},{14,10},{16,20},{18,... | collective-permute-start | bytes 589832 | tf_op jit(solution)/shard_map/ppermute | solution.py:42
  134.0 8.2 %collective-permute-start.38 = (f32[384,128]{1,0:T(8,128)S(1)}, f32[384,128]{1,0:T(8,128)S(1)}, u32[]{:S(2)}, u32[]{:S(2)}) collective-permute-start(f32[384,128]{1,0:T(8,128)S(1)} %get-tuple-element.126.refs_2_), channel_id=1, source_target_pairs={{0,8},{2,10},{4,12},{6,14},{8,0},{10,2},{12,4},{14,6},{16,24},{18,... | collective-permute-start | bytes 589832 | tf_op jit(solution)/shard_map/ppermute | solution.py:42
  142.9 8.9 %collective-permute-start.39 = (f32[768,128]{1,0:T(8,128)S(1)}, f32[768,128]{1,0:T(8,128)S(1)}, u32[]{:S(2)}, u32[]{:S(2)}) collective-permute-start(f32[768,128]{1,0:T(8,128)S(1)} %get-tuple-element.127.refs_5_.refs_3_), channel_id=1, source_target_pairs={{0,2},{2,0},{4,6},{6,4},{8,10},{10,8},{12,14},{14,12},{16,18},{18,... | collective-permute-start | bytes 1179656 | tf_op jit(solution)/shard_map/ppermute | solution.py:42
  143.4 8.5 %collective-permute-start.40 = (f32[768,128]{1,0:T(8,128)S(1)}, f32[768,128]{1,0:T(8,128)S(1)}, u32[]{:S(2)}, u32[]{:S(2)}) collective-permute-start(f32[768,128]{1,0:T(8,128)S(1)} %get-tuple-element.128.refs_6_.refs_4_), channel_id=1, source_target_pairs={{0,4},{2,6},{4,0},{6,2},{8,12},{10,14},{12,8},{14,10},{16,20},{18,... | collective-permute-start | bytes 1179656 | tf_op jit(solution)/shard_map/ppermute | solution.py:42
  (26 other events, 322.4 us)

commit v7 on v6

--- a/solution.py
+++ b/solution.py
@@ -186,7 +186,7 @@
         outs, whole_ref = refs[-n - 1 : -1], refs[-1]
     pieces, base = [], 0
     for s, count in enumerate(counts):
-        for place, size in pieces_of(count, 4 * BLOCK):
+        for place, size in pieces_of(count, 2 * BLOCK):
             there = pl.ds(pl.multiple_of(starts_ref[s] + place, BLOCK), size)
             here, spot = pl.ds(place, size), pl.ds(base + place, size)
             number = len(pieces)
@@ -219,7 +219,7 @@
 
 def merge(leaves, starts, counts, depth, tokens, square_sums, gain, grad, error, after=()):
     rows, width = sum(counts), grad.shape[1]
-    pieces = sum(len(pieces_of(count, 4 * BLOCK)) for count in counts)
+    pieces = sum(len(pieces_of(count, 2 * BLOCK)) for count in counts)
     if leaves:
         shapes = [pltpu.HBM((count, width), jnp.float32) for count in counts]
         places = [pltpu.HBM] * len(counts)

time: 156 us -> 157 us (level)
  transfers between devices with their start and end apart: 42 -> 42, of which waited for: 28 -> 28; matrix products, arithmetic and copies ran while one was open for 1% -> 1% of each run, Pallas kernels for 15% -> 16%
where the time goes in v7:
time: 157 us
  starting transfers between devices  54.3 us (35%)
  waiting for transfers between devices  53.6 us (34%)
  Pallas kernels  41.8 us (27%)
  local copies, waits for them, and re-layouts  3.19 us (2%)
  blocking collectives  2.37 us (2%)
    ppermute x42, starting transfers between devices, flip(): return lax.ppermute(value, axis, [(i, i ^ mask) for i in range(size)])  54.3 us
    ppermute x42, waiting for transfers between devices, flip(): return lax.ppermute(value, axis, [(i, i ^ mask) for i in range(size)])  53.6 us
    pallas_call x2, Pallas kernels, merge(): kernel_call(functools.partial(merge_kernel, counts, leaves, depth), out_s...  10.9 us
    pallas_call x1, Pallas kernels, second_pass(): kernel_call(product_kernel, out_shape=(square, near_shape((width, rank)),...  6.65 us
    pallas_call x1, Pallas kernels, error_rows(): kernel_call(functools.partial(error_kernel, plan, replicas), out_shape=(j...  5.62 us
    pallas_call x1, Pallas kernels, second_pass(): kernel_call(weight_kernel, out_shape=(half, half), in_specs=specs(*[pltpu...  5.16 us
    pallas_call x1, Pallas kernels, last_rows(): kernel_call(functools.partial(last_error_kernel, plan, replicas), out_sha...  3.92 us
  transfers between devices with their start and end apart: 42, of which 28 were waited for; matrix products, arithmetic and copies ran while one was open for 1% of the time, Pallas kernels for 16%

profile of v7, /device:TPU:0, one launch (start us, length us, event | category | flops | bytes accessed | tf_op | source)
XLA Modules:
  0.0 156.7 jit_solution(12795125816321844347)
XLA Ops:
  3.9 5.4 %shard_map.96 = (f32[384,512]{1,0:T(8,128)}, f32[512,512]{1,0:T(8,128)}, f32[384,512]{1,0:T(8,128)}, f32[384,512]{1,0:T(8,128)}, f32[384,512]{1,0:T(8,128)}) custom-call(s32[5]{0:T(128)S(1)} %stack.78.starts_ref, bf16[256,4096]{1,0:T(8,128)(2,1)} %tokens_ref.5, f32[256,128]{1,0:T(8,128)S(1)} %add.79.squares_ref, ...), custom_call_target="tpu_custom_call" | custom-call | flops 536870912 | bytes 9437184 | tf_op jit(solution)/shard_map/pallas_call | solution.py:232
  9.4 3.0 %collective-permute-start.4 = (f32[512,512]{1,0:T(8,128)}, f32[512,512]{1,0:T(8,128)S(1)}, u32[]{:S(2)}, u32[]{:S(2)}) collective-permute-start(f32[512,512]{1,0:T(8,128)} %get-tuple-element.80.refs_1_), channel_id=1, source_target_pairs={{0,8},{2,10},{4,12},{6,14},{8,0},{10,2},{12,4},{14,6},{16,24},{18,... | collective-permute-start | bytes 3145736 | tf_op jit(solution)/shard_map/ppermute | solution.py:42
  17.1 2.4 %all_gather.3.refs_0_.basis_ref = f32[512,128]{1,0:T(8,128)S(1)} all-gather(f32[256,128]{1,0:T(8,128)} %param.11), channel_id=1, replica_groups=mesh['rep'=16,'mp'=2] {'mp'}, dimensions={0}, use_global_device_ids=true | all-gather | bytes 393216 | tf_op jit(solution)/shard_map/all_gather | solution.py:697
  21.0 5.4 %shard_map.95 = (f32[384,512]{1,0:T(8,128)S(1)}, f32[512,512]{1,0:T(8,128)S(1)}, f32[384,512]{1,0:T(8,128)S(1)}, f32[384,512]{1,0:T(8,128)S(1)}, f32[384,512]{1,0:T(8,128)S(1)}, /*index=5*/f32[2048,512]{1,0:T(8,128)}) custom-call(s32[5]{0:T(128)S(1)} %copy-done.6, bf16[256,4096]{1,0:T(8,128)(2,1)} %tokens_ref.5, f32[256,128]{1,0:T(8,128)S(1)} %add.79.squares_ref, ...), custom_call_target="tpu_custom_call" | custom-call | flops 536870912 | bytes 9437184 | tf_op jit(solution)/shard_map/pallas_call | solution.py:232
  26.4 6.6 %collective-permute-done.1.got_ref.refs_0_ = f32[384,512]{1,0:T(8,128)S(1)} collective-permute-done((f32[384,512]{1,0:T(8,128)}, f32[384,512]{1,0:T(8,128)S(1)}, u32[]{:S(2)}, u32[]{:S(2)}) %collective-permute-start.1) | collective-permute-done | bytes 786464 | tf_op jit(solution)/shard_map/ppermute | solution.py:42
  39.5 2.6 %collective-permute-start.8 = (f32[192,512]{1,0:T(8,128)S(1)}, f32[192,512]{1,0:T(8,128)S(1)}, u32[]{:S(2)}, u32[]{:S(2)}) collective-permute-start(f32[192,512]{1,0:T(8,128)S(1)} %get-tuple-element.89), channel_id=1, source_target_pairs={{0,16},{2,18},{4,20},{6,22},{8,24},{10,26},{12,28},{14,30},{16,0},... | collective-permute-start | bytes 1179656 | tf_op jit(solution)/shard_map/ppermute | solution.py:42
  42.1 7.8 %collective-permute-done.6.got_ref.refs_0_ = f32[384,512]{1,0:T(8,128)S(1)} collective-permute-done((f32[384,512]{1,0:T(8,128)}, f32[384,512]{1,0:T(8,128)S(1)}, u32[]{:S(2)}, u32[]{:S(2)}) %collective-permute-start.6) | collective-permute-done | bytes 786464 | tf_op jit(solution)/shard_map/ppermute | solution.py:42
  52.2 6.2 %collective-permute-done.2.got_ref.refs_0_ = f32[192,512]{1,0:T(8,128)S(1)} collective-permute-done((f32[192,512]{1,0:T(8,128)S(1)}, f32[192,512]{1,0:T(8,128)S(1)}, u32[]{:S(2)}, u32[]{:S(2)}) %collective-permute-start.2) | collective-permute-done | bytes 393248 | tf_op jit(solution)/shard_map/ppermute | solution.py:42
  62.8 2.6 %collective-permute-start.17 = (f32[96,512]{1,0:T(8,128)S(1)}, f32[96,512]{1,0:T(8,128)S(1)}, u32[]{:S(2)}, u32[]{:S(2)}) collective-permute-start(f32[96,512]{1,0:T(8,128)S(1)} %get-tuple-element.105), channel_id=1, source_target_pairs={{0,16},{2,18},{4,20},{6,22},{8,24},{10,26},{12,28},{14,30},{16,0},... | collective-permute-start | bytes 589832 | tf_op jit(solution)/shard_map/ppermute | solution.py:42
  69.5 2.6 %collective-permute-start.16 = (f32[64,512]{1,0:T(8,128)S(1)}, f32[64,512]{1,0:T(8,128)S(1)}, u32[]{:S(2)}, u32[]{:S(2)}) collective-permute-start(f32[64,512]{1,0:T(8,128)S(1)} %get-tuple-element.104), channel_id=1, source_target_pairs={{0,16},{2,18},{4,20},{6,22},{8,24},{10,26},{12,28},{14,30},{16,0},... | collective-permute-start | bytes 393224 | tf_op jit(solution)/shard_map/ppermute | solution.py:42
  74.1 1.9 %collective-permute-done.17.got_ref.refs_0_ = f32[96,512]{1,0:T(8,128)S(1)} collective-permute-done((f32[96,512]{1,0:T(8,128)S(1)}, f32[96,512]{1,0:T(8,128)S(1)}, u32[]{:S(2)}, u32[]{:S(2)}) %collective-permute-start.17) | collective-permute-done | bytes 196640 | tf_op jit(solution)/shard_map/ppermute | solution.py:42
  76.5 6.4 %collective-permute-start.20 = (f32[48,512]{1,0:T(8,128)S(1)}, f32[48,512]{1,0:T(8,128)S(1)}, u32[]{:S(2)}, u32[]{:S(2)}) collective-permute-start(f32[48,512]{1,0:T(8,128)S(1)} %get-tuple-element.110), channel_id=1, source_target_pairs={{0,16},{2,18},{4,20},{6,22},{8,24},{10,26},{12,28},{14,30},{16,0},... | collective-permute-start | bytes 294920 | tf_op jit(solution)/shard_map/ppermute | solution.py:42
  94.0 2.0 %collective-permute-done.24 = f32[136,128]{1,0:T(8,128)S(1)} collective-permute-done((f32[136,128]{1,0:T(8,128)S(1)}, f32[136,128]{1,0:T(8,128)S(1)}, u32[]{:S(2)}, u32[]{:S(2)}) %collective-permute-start.24) | collective-permute-done | bytes 69664 | tf_op jit(solution)/shard_map/ppermute | solution.py:42
  96.9 2.2 %collective-permute-start.27 = (f32[136,128]{1,0:T(8,128)S(1)}, f32[136,128]{1,0:T(8,128)S(1)}, u32[]{:S(2)}, u32[]{:S(2)}) collective-permute-start(f32[136,128]{1,0:T(8,128)S(1)} %add_add_fusion.1), channel_id=1, source_target_pairs={{0,24},{2,26},{4,28},{6,30},{8,16},{10,18},{12,20},{14,22},{16,8},... | collective-permute-start | bytes 208904 | tf_op jit(solution)/shard_map/ppermute | solution.py:42
  99.2 2.1 %collective-permute-start.25 = (f32[136,128]{1,0:T(8,128)S(1)}, f32[136,128]{1,0:T(8,128)S(1)}, u32[]{:S(2)}, u32[]{:S(2)}) collective-permute-start(f32[136,128]{1,0:T(8,128)S(1)} %add_add_fusion.1), channel_id=1, source_target_pairs={{0,8},{2,10},{4,12},{6,14},{8,0},{10,2},{12,4},{14,6},{16,24},{18,... | collective-permute-start | bytes 208904 | tf_op jit(solution)/shard_map/ppermute | solution.py:42
  101.3 2.5 %collective-permute-done.27 = f32[136,128]{1,0:T(8,128)S(1)} collective-permute-done((f32[136,128]{1,0:T(8,128)S(1)}, f32[136,128]{1,0:T(8,128)S(1)}, u32[]{:S(2)}, u32[]{:S(2)}) %collective-permute-start.27) | collective-permute-done | bytes 69664 | tf_op jit(solution)/shard_map/ppermute | solution.py:42
  103.8 2.0 %collective-permute-done.26 = f32[136,128]{1,0:T(8,128)S(1)} collective-permute-done((f32[136,128]{1,0:T(8,128)S(1)}, f32[136,128]{1,0:T(8,128)S(1)}, u32[]{:S(2)}, u32[]{:S(2)}) %collective-permute-start.26) | collective-permute-done | bytes 69664 | tf_op jit(solution)/shard_map/ppermute | solution.py:42
  110.4 1.8 %collective-permute-done.29 = f32[136,128]{1,0:T(8,128)S(1)} collective-permute-done((f32[136,128]{1,0:T(8,128)S(1)}, f32[136,128]{1,0:T(8,128)S(1)}, u32[]{:S(2)}, u32[]{:S(2)}) %collective-permute-start.29) | collective-permute-done | bytes 69664 | tf_op jit(solution)/shard_map/ppermute | solution.py:42
  115.2 3.1 %shard_map.118 = (f32[512,512]{1,0:T(8,128)S(1)}, f32[512,128]{1,0:T(8,128)S(1)}, f32[128,128]{1,0:T(8,128)S(1)}, f32[256,128]{1,0:T(8,128)S(1)}) custom-call(f32[1088,128]{1,0:T(8,128)S(1)} %constant_dynamic-update-slice_fusion.packed_ref, f32[512,128]{1,0:T(8,128)S(1)} %copy-done.1, f32[48,512]{1,0:T(8,128)S(1)} %shard_map.109.refs_0_, ...), custom_call_target="tpu_custom_call" | custom-call | tf_op jit(solution)/shard_map/pallas_call | solution.py:473
  119.2 6.6 %shard_map.119 = (f32[128,128]{1,0:T(8,128)S(1)}, f32[512,128]{1,0:T(8,128)S(1)}, f32[128,128]{1,0:T(8,128)S(1)}) custom-call(f32[512,512]{1,0:T(8,128)S(1)} %get-tuple-element.111.whole_ref, f32[512,128]{1,0:T(8,128)S(1)} %get-tuple-element.112.right_ref, f32[128,128]{1,0:T(8,128)S(1)} %get-tuple-element.113.gram_ref), custom_call_target="tpu_custom_call" | custom-call | tf_op jit(solution)/shard_map/pallas_call | solution.py:506
  129.7 3.9 %collective-permute-done.34.refs_4_ = f32[128,128]{1,0:T(8,128)S(1)} collective-permute-done((f32[128,128]{1,0:T(8,128)S(1)}, f32[128,128]{1,0:T(8,128)S(1)}, u32[]{:S(2)}, u32[]{:S(2)}) %collective-permute-start.34) | collective-permute-done | bytes 65568 | tf_op jit(solution)/shard_map/ppermute | solution.py:42
  137.7 5.2 %shard_map.120 = (bf16[128,512]{1,0:T(8,128)(2,1)S(1)}, bf16[128,512]{1,0:T(8,128)(2,1)S(1)}) custom-call(f32[128,128]{1,0:T(8,128)S(1)} %get-tuple-element.114.first_ref, f32[512,128]{1,0:T(8,128)S(1)} %get-tuple-element.115.plain_ref, f32[128,128]{1,0:T(8,128)S(1)} %get-tuple-element.116.gram_ref.refs_2_.refs_6_), custom_call_target="tpu_custom_call" | custom-call | tf_op jit(solution)/shard_map/pallas_call | solution.py:513
  146.3 5.6 %shard_map.124 = (f32[4096,512]{1,0:T(8,128)}, f32[2048,512]{1,0:T(8,128)S(1)}) custom-call(s32[5]{0:T(128)S(1)} %copy-done.7, bf16[128,512]{1,0:T(8,128)(2,1)S(1)} %get-tuple-element.117.refs_6_.high_ref, bf16[128,512]{1,0:T(8,128)(2,1)S(1)} %get-tuple-element.118.low_ref, f32[2048,512]{1,0:T(8,128)} %get-tuple-element.119.own_ref, ...), custom_call_target="tpu_custom_call" | custom-call | flops 805306368 | bytes 8388608 | tf_op jit(solution)/shard_map/pallas_call | solution.py:627
  152.6 3.9 %shard_map.125 = (f32[4096,512]{1,0:T(8,128)}, f32[256,512]{1,0:T(8,128)}, f32[256,512]{1,0:T(8,128)}) custom-call(s32[11]{0:T(128)S(1)} %stack.76.starts_ref, bf16[128,512]{1,0:T(8,128)(2,1)S(1)} %get-tuple-element.117.refs_6_.high_ref, bf16[128,512]{1,0:T(8,128)(2,1)S(1)} %get-tuple-element.118.low_ref, ...), custom_call_target="tpu_custom_call", output_to_operand_aliasing={{0}: (12, {})} | custom-call | flops 805306368 | bytes 8388608 | tf_op jit(solution)/shard_map/pallas_call | solution.py:652
  (126 shorter events, 61.5 us)
Async XLA Ops:
  9.4 26.7 %collective-permute-start.4 = (f32[512,512]{1,0:T(8,128)}, f32[512,512]{1,0:T(8,128)S(1)}, u32[]{:S(2)}, u32[]{:S(2)}) collective-permute-start(f32[512,512]{1,0:T(8,128)} %get-tuple-element.80.refs_1_), channel_id=1, source_target_pairs={{0,8},{2,10},{4,12},{6,14},{8,0},{10,2},{12,4},{14,6},{16,24},{18,... | collective-permute-start | bytes 3145736 | tf_op jit(solution)/shard_map/ppermute | solution.py:42
  12.4 20.6 %collective-permute-start.1 = (f32[384,512]{1,0:T(8,128)}, f32[384,512]{1,0:T(8,128)S(1)}, u32[]{:S(2)}, u32[]{:S(2)}) collective-permute-start(f32[384,512]{1,0:T(8,128)} %get-tuple-element.72.refs_0_), channel_id=1, source_target_pairs={{0,2},{2,0},{4,6},{6,4},{8,10},{10,8},{12,14},{14,12},{16,18},{18,... | collective-permute-start | bytes 2359304 | tf_op jit(solution)/shard_map/ppermute | solution.py:42
  13.9 20.8 %collective-permute-start.5 = (f32[384,512]{1,0:T(8,128)}, f32[384,512]{1,0:T(8,128)}, u32[]{:S(2)}, u32[]{:S(2)}) collective-permute-start(f32[384,512]{1,0:T(8,128)} %get-tuple-element.81.refs_4_), channel_id=1, source_target_pairs={{0,4},{2,6},{4,0},{6,2},{8,12},{10,14},{12,8},{14,10},{16,20},{18,... | collective-permute-start | bytes 2359304 | tf_op jit(solution)/shard_map/ppermute | solution.py:42
  15.4 34.5 %collective-permute-start.6 = (f32[384,512]{1,0:T(8,128)}, f32[384,512]{1,0:T(8,128)S(1)}, u32[]{:S(2)}, u32[]{:S(2)}) collective-permute-start(f32[384,512]{1,0:T(8,128)} %get-tuple-element.84.refs_2_), channel_id=1, source_target_pairs={{0,2},{2,0},{4,6},{6,4},{8,10},{10,8},{12,14},{14,12},{16,18},{18,... | collective-permute-start | bytes 2359304 | tf_op jit(solution)/shard_map/ppermute | solution.py:42
  15.9 35.6 %collective-permute-start.3 = (f32[384,512]{1,0:T(8,128)}, f32[384,512]{1,0:T(8,128)S(1)}, u32[]{:S(2)}, u32[]{:S(2)}) collective-permute-start(f32[384,512]{1,0:T(8,128)} %get-tuple-element.79.refs_3_), channel_id=1, source_target_pairs={{0,4},{2,6},{4,0},{6,2},{8,12},{10,14},{12,8},{14,10},{16,20},{18,... | collective-permute-start | bytes 2359304 | tf_op jit(solution)/shard_map/ppermute | solution.py:42
  36.2 24.9 %collective-permute-start.10 = (f32[256,512]{1,0:T(8,128)S(1)}, f32[256,512]{1,0:T(8,128)S(1)}, u32[]{:S(2)}, u32[]{:S(2)}) collective-permute-start(f32[256,512]{1,0:T(8,128)S(1)} %get-tuple-element.91), channel_id=1, source_target_pairs={{0,2},{2,0},{4,6},{6,4},{8,10},{10,8},{12,14},{14,12},{16,18},{18,... | collective-permute-start | bytes 1572872 | tf_op jit(solution)/shard_map/ppermute | solution.py:42
  37.9 20.5 %collective-permute-start.2 = (f32[192,512]{1,0:T(8,128)S(1)}, f32[192,512]{1,0:T(8,128)S(1)}, u32[]{:S(2)}, u32[]{:S(2)}) collective-permute-start(f32[192,512]{1,0:T(8,128)S(1)} %get-tuple-element.78), channel_id=1, source_target_pairs={{0,8},{2,10},{4,12},{6,14},{8,0},{10,2},{12,4},{14,6},{16,24},{18,... | collective-permute-start | bytes 1179656 | tf_op jit(solution)/shard_map/ppermute | solution.py:42
  39.5 18.9 %collective-permute-start.8 = (f32[192,512]{1,0:T(8,128)S(1)}, f32[192,512]{1,0:T(8,128)S(1)}, u32[]{:S(2)}, u32[]{:S(2)}) collective-permute-start(f32[192,512]{1,0:T(8,128)S(1)} %get-tuple-element.89), channel_id=1, source_target_pairs={{0,16},{2,18},{4,20},{6,22},{8,24},{10,26},{12,28},{14,30},{16,0},... | collective-permute-start | bytes 1179656 | tf_op jit(solution)/shard_map/ppermute | solution.py:42
  50.0 12.8 %collective-permute-start.11 = (f32[192,512]{1,0:T(8,128)S(1)}, f32[192,512]{1,0:T(8,128)S(1)}, u32[]{:S(2)}, u32[]{:S(2)}) collective-permute-start(f32[192,512]{1,0:T(8,128)S(1)} %get-tuple-element.94), channel_id=1, source_target_pairs={{0,4},{2,6},{4,0},{6,2},{8,12},{10,14},{12,8},{14,10},{16,20},{18,... | collective-permute-start | bytes 1179656 | tf_op jit(solution)/shard_map/ppermute | solution.py:42
  51.6 15.0 %collective-permute-start.13 = (f32[192,512]{1,0:T(8,128)S(1)}, f32[192,512]{1,0:T(8,128)S(1)}, u32[]{:S(2)}, u32[]{:S(2)}) collective-permute-start(f32[192,512]{1,0:T(8,128)S(1)} %get-tuple-element.99), channel_id=1, source_target_pairs={{0,8},{2,10},{4,12},{6,14},{8,0},{10,2},{12,4},{14,6},{16,24},{18,... | collective-permute-start | bytes 1179656 | tf_op jit(solution)/shard_map/ppermute | solution.py:42
  58.5 7.0 %collective-permute-start.9 = (f32[96,512]{1,0:T(8,128)S(1)}, f32[96,512]{1,0:T(8,128)S(1)}, u32[]{:S(2)}, u32[]{:S(2)}) collective-permute-start(f32[96,512]{1,0:T(8,128)S(1)} %get-tuple-element.90), channel_id=1, source_target_pairs={{0,2},{2,0},{4,6},{6,4},{8,10},{10,8},{12,14},{14,12},{16,18},{18,... | collective-permute-start | bytes 589832 | tf_op jit(solution)/shard_map/ppermute | solution.py:42
  58.9 7.7 %collective-permute-start.7 = (f32[96,512]{1,0:T(8,128)S(1)}, f32[96,512]{1,0:T(8,128)S(1)}, u32[]{:S(2)}, u32[]{:S(2)}) collective-permute-start(f32[96,512]{1,0:T(8,128)S(1)} %get-tuple-element.88), channel_id=1, source_target_pairs={{0,4},{2,6},{4,0},{6,2},{8,12},{10,14},{12,8},{14,10},{16,20},{18,... | collective-permute-start | bytes 589832 | tf_op jit(solution)/shard_map/ppermute | solution.py:42
  61.2 8.3 %collective-permute-start.15 = (f32[128,512]{1,0:T(8,128)S(1)}, f32[128,512]{1,0:T(8,128)S(1)}, u32[]{:S(2)}, u32[]{:S(2)}) collective-permute-start(f32[128,512]{1,0:T(8,128)S(1)} %get-tuple-element.101), channel_id=1, source_target_pairs={{0,4},{2,6},{4,0},{6,2},{8,12},{10,14},{12,8},{14,10},{16,20},{18,... | collective-permute-start | bytes 786440 | tf_op jit(solution)/shard_map/ppermute | solution.py:42
  62.8 13.1 %collective-permute-start.17 = (f32[96,512]{1,0:T(8,128)S(1)}, f32[96,512]{1,0:T(8,128)S(1)}, u32[]{:S(2)}, u32[]{:S(2)}) collective-permute-start(f32[96,512]{1,0:T(8,128)S(1)} %get-tuple-element.105), channel_id=1, source_target_pairs={{0,16},{2,18},{4,20},{6,22},{8,24},{10,26},{12,28},{14,30},{16,0},... | collective-permute-start | bytes 589832 | tf_op jit(solution)/shard_map/ppermute | solution.py:42
  66.7 9.7 %collective-permute-start.14 = (f32[96,512]{1,0:T(8,128)S(1)}, f32[96,512]{1,0:T(8,128)S(1)}, u32[]{:S(2)}, u32[]{:S(2)}) collective-permute-start(f32[96,512]{1,0:T(8,128)S(1)} %get-tuple-element.100), channel_id=1, source_target_pairs={{0,2},{2,0},{4,6},{6,4},{8,10},{10,8},{12,14},{14,12},{16,18},{18,... | collective-permute-start | bytes 589832 | tf_op jit(solution)/shard_map/ppermute | solution.py:42
  69.5 15.7 %collective-permute-start.16 = (f32[64,512]{1,0:T(8,128)S(1)}, f32[64,512]{1,0:T(8,128)S(1)}, u32[]{:S(2)}, u32[]{:S(2)}) collective-permute-start(f32[64,512]{1,0:T(8,128)S(1)} %get-tuple-element.104), channel_id=1, source_target_pairs={{0,16},{2,18},{4,20},{6,22},{8,24},{10,26},{12,28},{14,30},{16,0},... | collective-permute-start | bytes 393224 | tf_op jit(solution)/shard_map/ppermute | solution.py:42
  72.1 12.3 %collective-permute-start.12 = (f32[48,512]{1,0:T(8,128)S(1)}, f32[48,512]{1,0:T(8,128)S(1)}, u32[]{:S(2)}, u32[]{:S(2)}) collective-permute-start(f32[48,512]{1,0:T(8,128)S(1)} %get-tuple-element.98), channel_id=1, source_target_pairs={{0,16},{2,18},{4,20},{6,22},{8,24},{10,26},{12,28},{14,30},{16,0},... | collective-permute-start | bytes 294920 | tf_op jit(solution)/shard_map/ppermute | solution.py:42
  76.0 9.2 %collective-permute-start.18 = (f32[48,512]{1,0:T(8,128)S(1)}, f32[48,512]{1,0:T(8,128)S(1)}, u32[]{:S(2)}, u32[]{:S(2)}) collective-permute-start(f32[48,512]{1,0:T(8,128)S(1)} %get-tuple-element.106), channel_id=1, source_target_pairs={{0,8},{2,10},{4,12},{6,14},{8,0},{10,2},{12,4},{14,6},{16,24},{18,... | collective-permute-start | bytes 294920 | tf_op jit(solution)/shard_map/ppermute | solution.py:42
  76.5 10.0 %collective-permute-start.20 = (f32[48,512]{1,0:T(8,128)S(1)}, f32[48,512]{1,0:T(8,128)S(1)}, u32[]{:S(2)}, u32[]{:S(2)}) collective-permute-start(f32[48,512]{1,0:T(8,128)S(1)} %get-tuple-element.110), channel_id=1, source_target_pairs={{0,16},{2,18},{4,20},{6,22},{8,24},{10,26},{12,28},{14,30},{16,0},... | collective-permute-start | bytes 294920 | tf_op jit(solution)/shard_map/ppermute | solution.py:42
  118.3 9.2 %collective-permute-start.32 = (f32[256,128]{1,0:T(8,128)S(1)}, f32[256,128]{1,0:T(8,128)S(1)}, u32[]{:S(2)}, u32[]{:S(2)}) collective-permute-start(f32[256,128]{1,0:T(8,128)S(1)} %get-tuple-element.120.refs_0_), channel_id=1, source_target_pairs={{0,16},{2,18},{4,20},{6,22},{8,24},{10,26},{12,28},{14,30},{16,0},... | collective-permute-start | bytes 393224 | tf_op jit(solution)/shard_map/ppermute | solution.py:42
  134.2 8.7 %collective-permute-start.37 = (f32[384,128]{1,0:T(8,128)S(1)}, f32[384,128]{1,0:T(8,128)S(1)}, u32[]{:S(2)}, u32[]{:S(2)}) collective-permute-start(f32[384,128]{1,0:T(8,128)S(1)} %get-tuple-element.125.refs_1_), channel_id=1, source_target_pairs={{0,4},{2,6},{4,0},{6,2},{8,12},{10,14},{12,8},{14,10},{16,20},{18,... | collective-permute-start | bytes 589832 | tf_op jit(solution)/shard_map/ppermute | solution.py:42
  134.7 8.3 %collective-permute-start.38 = (f32[384,128]{1,0:T(8,128)S(1)}, f32[384,128]{1,0:T(8,128)S(1)}, u32[]{:S(2)}, u32[]{:S(2)}) collective-permute-start(f32[384,128]{1,0:T(8,128)S(1)} %get-tuple-element.126.refs_2_), channel_id=1, source_target_pairs={{0,8},{2,10},{4,12},{6,14},{8,0},{10,2},{12,4},{14,6},{16,24},{18,... | collective-permute-start | bytes 589832 | tf_op jit(solution)/shard_map/ppermute | solution.py:42
  143.6 8.9 %collective-permute-start.39 = (f32[768,128]{1,0:T(8,128)S(1)}, f32[768,128]{1,0:T(8,128)S(1)}, u32[]{:S(2)}, u32[]{:S(2)}) collective-permute-start(f32[768,128]{1,0:T(8,128)S(1)} %get-tuple-element.127.refs_5_.refs_3_), channel_id=1, source_target_pairs={{0,2},{2,0},{4,6},{6,4},{8,10},{10,8},{12,14},{14,12},{16,18},{18,... | collective-permute-start | bytes 1179656 | tf_op jit(solution)/shard_map/ppermute | solution.py:42
  144.1 8.5 %collective-permute-start.40 = (f32[768,128]{1,0:T(8,128)S(1)}, f32[768,128]{1,0:T(8,128)S(1)}, u32[]{:S(2)}, u32[]{:S(2)}) collective-permute-start(f32[768,128]{1,0:T(8,128)S(1)} %get-tuple-element.128.refs_6_.refs_4_), channel_id=1, source_target_pairs={{0,4},{2,6},{4,0},{6,2},{8,12},{10,14},{12,8},{14,10},{16,20},{18,... | collective-permute-start | bytes 1179656 | tf_op jit(solution)/shard_map/ppermute | solution.py:42
  (26 other events, 323.0 us)
